TPU v7x, 128 devices: a whole 4x4x4 slice. The times are simulated.
128 devices in a mesh: blk: 16 (over z, x), grid: 8 (over y, core).
Axes of the slice: x: 4, y: 4, z: 4, core: 2. Of those that a mesh axis runs over, the one named last changes fastest.
Arguments:
- state: bfloat16 [256, 2048, 128], P('grid', 'blk'), may hold values from -6 to 6
- courant: float32 [256, 2048], P('grid', 'blk'), may hold values from 0.2 to 0.5
- diffusion: float32 [128], replicated, may hold values from 0.02 to 0.12
- table_value: bfloat16 [4096, 128], P('blk'), may hold values from -6 to 6
- table_base: bfloat16 [4096, 128], P('blk'), may hold values from -6 to 6
- table_sens: bfloat16 [4096, 128, 128], P('blk'), may hold values from -0.5 to 0.5
- slot_cell: int32 [8, 768, 128], P('grid', 'blk'), may hold values from -1 to 4095, as said below
- hit_step: int32 [8, 768, 128], P('grid', 'blk'), may hold values from 0 to 15, as said below
- entry_ids: int32 [16, 8, 768], P('blk', 'grid'), may hold values from 0 to 255
Outputs:
- advanced: float32 [256, 2048, 128], P('grid', 'blk')
Inputs may be any that keep to these rules, and one draw needn't show every extreme that they name: `slot_cell`: on each device, its 48 blocks of 128 slots hold each of its 4096 local cells in exactly one slot; all other slots hold -1. `hit_step`: on each device, at most 512 occupied slots name any one partition, and in every draw some partition is named by exactly 512 of them on each device.
All inputs are finite; a program needn't handle non-finite values.
Results may differ from a plain program's by a relative error of at most 0.0038.
Values may be sent and summed in bfloat16 or wider, within the bound.
No kernel may reach another device: no remote copies, remote signals or barrier semaphores. Data moves between devices by JAX's collectives and lax.ppermute only.
A program may use at most 192 MiB of HBM per device.

v0:
```python
import jax
import jax.numpy as jnp
from jax import lax
from jax.sharding import PartitionSpec as P


def from_behind(value, axis, steps):
    count = lax.axis_size(axis)
    pairs = [(source, (source + steps) % count) for source in range(count)]
    return lax.ppermute(value, axis, pairs)


def extended(block, sides, width):
    for axis, dim in sides:
        count = lax.axis_size(axis)
        forward = [(i, i + 1) for i in range(count - 1)]
        backward = [(target, source) for source, target in forward]
        low = lax.ppermute(
            lax.slice_in_dim(block, block.shape[dim] - width, None, axis=dim), axis, forward
        )
        high = lax.ppermute(lax.slice_in_dim(block, 0, width, axis=dim), axis, backward)
        block = jnp.concatenate([low, block, high], axis=dim)
    return block


def evaluate(blocks, chosen, table_value, table_base, table_sens):
    base = table_base[chosen].astype(jnp.float32)
    delta = (blocks.astype(jnp.float32) - base[:, None, :]).astype(jnp.bfloat16)
    mapped = jnp.einsum(
        "kqi,kij->kqj", delta, table_sens[chosen], preferred_element_type=jnp.float32
    )
    mapped = mapped + table_value[chosen].astype(jnp.float32)[:, None, :]
    return mapped.astype(jnp.bfloat16)


def local(
    state, courant, diffusion, table_value, table_base, table_sens, slot_cell, hit_step, entry_ids
):
    rows_here, cols_here, width = state.shape
    nblocks = slot_cell.shape[1]
    nparts = lax.axis_size("blk")
    myself = lax.axis_index("blk")
    flat = state.reshape(rows_here * cols_here, width)
    slots = slot_cell[0]
    live = slots >= 0
    picked = flat[jnp.maximum(slots, 0)]
    queries = jnp.where(live[..., None], picked, jnp.zeros_like(picked))
    entries = entry_ids[0, 0]
    marks = hit_step[0]

    def turn(step, carry):
        blocks, steps_held = carry
        anchor = (myself - step) % nparts
        chosen = lax.dynamic_slice_in_dim(entries, anchor * nblocks, nblocks)
        mapped = evaluate(blocks, chosen, table_value, table_base, table_sens)
        taken = steps_held.astype(jnp.float32) == step.astype(jnp.float32)
        blocks = jnp.where(taken[..., None], mapped, blocks)
        return from_behind((blocks, steps_held), "blk", 1)

    results, unused = lax.fori_loop(0, nparts, turn, (queries, marks.astype(jnp.bfloat16)))
    target = jnp.where(live, slots, rows_here * cols_here).reshape(-1)
    reacted = (
        flat.at[target]
        .set(results.reshape(-1, width), mode="drop")
        .reshape(rows_here, cols_here, width)
    )
    padded = extended(reacted, (("blk", 1), ("grid", 0)), 1).astype(jnp.float32)
    field = reacted.astype(jnp.float32)
    upper = padded[:-2, 1:-1]
    lower = padded[2:, 1:-1]
    left_side = padded[1:-1, :-2]
    right_side = padded[1:-1, 2:]
    return (
        field
        - courant[..., None] * (field - upper)
        + diffusion * (upper + lower + left_side + right_side - 4.0 * field)
    )


def solution(mesh):
    return jax.shard_map(
        local,
        mesh=mesh,
        in_specs=(
            P("grid", "blk", None),
            P("grid", "blk"),
            P(),
            P("blk", None),
            P("blk", None),
            P("blk", None, None),
            P("grid", "blk", None),
            P("grid", "blk", None),
            P("blk", "grid", None),
        ),
        out_specs=P("grid", "blk", None),
        check_vma=False,
    )
```

profile of v0, /device:TPU:30, one launch (start us, length us, event | category | flops | bytes accessed | tf_op | source)
XLA Modules:
  0.0 749.8 jit_solution(781379613446054790)
XLA Ops:
  1.4 18.1 %gather_fusion.3 = bf16[6144,128]{1,0:T(8,128)(2,1)S(1)} fusion(bf16[4096,128]{1,0:T(8,128)(2,1)S(1)} %bitcast.15, s32[6144]{0:T(1024)S(1)} %bitcast_clamp_fusion), kind=kCustom, calls=%fused_computation.3 | custom fusion | bytes 3170304 | tf_op jit(solution)/shard_map/gather | solution.py:46
  21.9 691.3 %while.17 = (s32[]{:T(128)}, bf16[48,128,128]{2,1,0:T(8,128)(2,1)}, bf16[48,128]{1,0:T(8,128)(2,1)S(1)}, s32[]{:T(128)}, s32[768]{0:T(1024)S(1)}, /*index=5*/bf1...) while((s32[]{:T(128)}, bf16[48,128,128]{2,1,0:T(8,128)(2,1)}, ...), condition=%wide.region_1.2_spmd, body=%wide.region_0.1_spmd.sunk | while | flops 206070944 | bytes 20723240 | solution.py:60
  22.0 4.2 gather_fusion
  34.6 33.3 %collective-permute-done.1 = bf16[48,128]{1,0:T(8,128)(2,1)S(1)} collective-permute-done((bf16[48,128]{1,0:T(8,128)(2,1)S(1)}, bf16[48,128]{1,0:T(8,128)(2,1)S(1)}, u32[]{:S(2)}, u32[]{:S(2)}) %collective-permute-start.1) | collective-permute-done | bytes 12320 | tf_op jit(solution)/shard_map/while/body/eval_jaxpr/ppermute | solution.py:10
  69.1 4.2 gather_fusion
  82.5 33.2 %collective-permute-done.1 = bf16[48,128]{1,0:T(8,128)(2,1)S(1)} collective-permute-done((bf16[48,128]{1,0:T(8,128)(2,1)S(1)}, bf16[48,128]{1,0:T(8,128)(2,1)S(1)}, u32[]{:S(2)}, u32[]{:S(2)}) %collective-permute-start.1) | collective-permute-done | bytes 12320 | tf_op jit(solution)/shard_map/while/body/eval_jaxpr/ppermute | solution.py:10
  116.9 4.2 gather_fusion
  126.3 4.6 collective-permute-start
  130.9 32.3 %collective-permute-done.1 = bf16[48,128]{1,0:T(8,128)(2,1)S(1)} collective-permute-done((bf16[48,128]{1,0:T(8,128)(2,1)S(1)}, bf16[48,128]{1,0:T(8,128)(2,1)S(1)}, u32[]{:S(2)}, u32[]{:S(2)}) %collective-permute-start.1) | collective-permute-done | bytes 12320 | tf_op jit(solution)/shard_map/while/body/eval_jaxpr/ppermute | solution.py:10
  164.4 4.2 gather_fusion
  173.7 4.6 collective-permute-start
  178.4 31.4 %collective-permute-done.1 = bf16[48,128]{1,0:T(8,128)(2,1)S(1)} collective-permute-done((bf16[48,128]{1,0:T(8,128)(2,1)S(1)}, bf16[48,128]{1,0:T(8,128)(2,1)S(1)}, u32[]{:S(2)}, u32[]{:S(2)}) %collective-permute-start.1) | collective-permute-done | bytes 12320 | tf_op jit(solution)/shard_map/while/body/eval_jaxpr/ppermute | solution.py:10
  211.0 4.2 gather_fusion
  220.3 4.6 collective-permute-start
  224.9 30.4 %collective-permute-done.1 = bf16[48,128]{1,0:T(8,128)(2,1)S(1)} collective-permute-done((bf16[48,128]{1,0:T(8,128)(2,1)S(1)}, bf16[48,128]{1,0:T(8,128)(2,1)S(1)}, u32[]{:S(2)}, u32[]{:S(2)}) %collective-permute-start.1) | collective-permute-done | bytes 12320 | tf_op jit(solution)/shard_map/while/body/eval_jaxpr/ppermute | solution.py:10
  256.6 4.2 gather_fusion
  266.0 4.6 collective-permute-start
  270.6 29.9 %collective-permute-done.1 = bf16[48,128]{1,0:T(8,128)(2,1)S(1)} collective-permute-done((bf16[48,128]{1,0:T(8,128)(2,1)S(1)}, bf16[48,128]{1,0:T(8,128)(2,1)S(1)}, u32[]{:S(2)}, u32[]{:S(2)}) %collective-permute-start.1) | collective-permute-done | bytes 12320 | tf_op jit(solution)/shard_map/while/body/eval_jaxpr/ppermute | solution.py:10
  311.0 4.2 collective-permute-start
  315.3 30.5 %collective-permute-done.1 = bf16[48,128]{1,0:T(8,128)(2,1)S(1)} collective-permute-done((bf16[48,128]{1,0:T(8,128)(2,1)S(1)}, bf16[48,128]{1,0:T(8,128)(2,1)S(1)}, u32[]{:S(2)}, u32[]{:S(2)}) %collective-permute-start.1) | collective-permute-done | bytes 12320 | tf_op jit(solution)/shard_map/while/body/eval_jaxpr/ppermute | solution.py:10
  347.0 4.2 gather_fusion
  359.1 31.1 %collective-permute-done.1 = bf16[48,128]{1,0:T(8,128)(2,1)S(1)} collective-permute-done((bf16[48,128]{1,0:T(8,128)(2,1)S(1)}, bf16[48,128]{1,0:T(8,128)(2,1)S(1)}, u32[]{:S(2)}, u32[]{:S(2)}) %collective-permute-start.1) | collective-permute-done | bytes 12320 | tf_op jit(solution)/shard_map/while/body/eval_jaxpr/ppermute | solution.py:10
  402.0 31.7 %collective-permute-done.1 = bf16[48,128]{1,0:T(8,128)(2,1)S(1)} collective-permute-done((bf16[48,128]{1,0:T(8,128)(2,1)S(1)}, bf16[48,128]{1,0:T(8,128)(2,1)S(1)}, u32[]{:S(2)}, u32[]{:S(2)}) %collective-permute-start.1) | collective-permute-done | bytes 12320 | tf_op jit(solution)/shard_map/while/body/eval_jaxpr/ppermute | solution.py:10
  444.2 32.0 %collective-permute-done.1 = bf16[48,128]{1,0:T(8,128)(2,1)S(1)} collective-permute-done((bf16[48,128]{1,0:T(8,128)(2,1)S(1)}, bf16[48,128]{1,0:T(8,128)(2,1)S(1)}, u32[]{:S(2)}, u32[]{:S(2)}) %collective-permute-start.1) | collective-permute-done | bytes 12320 | tf_op jit(solution)/shard_map/while/body/eval_jaxpr/ppermute | solution.py:10
  486.8 31.0 %collective-permute-done.1 = bf16[48,128]{1,0:T(8,128)(2,1)S(1)} collective-permute-done((bf16[48,128]{1,0:T(8,128)(2,1)S(1)}, bf16[48,128]{1,0:T(8,128)(2,1)S(1)}, u32[]{:S(2)}, u32[]{:S(2)}) %collective-permute-start.1) | collective-permute-done | bytes 12320 | tf_op jit(solution)/shard_map/while/body/eval_jaxpr/ppermute | solution.py:10
  528.4 30.1 %collective-permute-done.1 = bf16[48,128]{1,0:T(8,128)(2,1)S(1)} collective-permute-done((bf16[48,128]{1,0:T(8,128)(2,1)S(1)}, bf16[48,128]{1,0:T(8,128)(2,1)S(1)}, u32[]{:S(2)}, u32[]{:S(2)}) %collective-permute-start.1) | collective-permute-done | bytes 12320 | tf_op jit(solution)/shard_map/while/body/eval_jaxpr/ppermute | solution.py:10
  569.1 29.2 %collective-permute-done.1 = bf16[48,128]{1,0:T(8,128)(2,1)S(1)} collective-permute-done((bf16[48,128]{1,0:T(8,128)(2,1)S(1)}, bf16[48,128]{1,0:T(8,128)(2,1)S(1)}, u32[]{:S(2)}, u32[]{:S(2)}) %collective-permute-start.1) | collective-permute-done | bytes 12320 | tf_op jit(solution)/shard_map/while/body/eval_jaxpr/ppermute | solution.py:10
  608.9 28.3 %collective-permute-done.1 = bf16[48,128]{1,0:T(8,128)(2,1)S(1)} collective-permute-done((bf16[48,128]{1,0:T(8,128)(2,1)S(1)}, bf16[48,128]{1,0:T(8,128)(2,1)S(1)}, u32[]{:S(2)}, u32[]{:S(2)}) %collective-permute-start.1) | collective-permute-done | bytes 12320 | tf_op jit(solution)/shard_map/while/body/eval_jaxpr/ppermute | solution.py:10
  647.7 27.3 %collective-permute-done.1 = bf16[48,128]{1,0:T(8,128)(2,1)S(1)} collective-permute-done((bf16[48,128]{1,0:T(8,128)(2,1)S(1)}, bf16[48,128]{1,0:T(8,128)(2,1)S(1)}, u32[]{:S(2)}, u32[]{:S(2)}) %collective-permute-start.1) | collective-permute-done | bytes 12320 | tf_op jit(solution)/shard_map/while/body/eval_jaxpr/ppermute | solution.py:10
  685.7 26.4 %collective-permute-done.1 = bf16[48,128]{1,0:T(8,128)(2,1)S(1)} collective-permute-done((bf16[48,128]{1,0:T(8,128)(2,1)S(1)}, bf16[48,128]{1,0:T(8,128)(2,1)S(1)}, u32[]{:S(2)}, u32[]{:S(2)}) %collective-permute-start.1) | collective-permute-done | bytes 12320 | tf_op jit(solution)/shard_map/while/body/eval_jaxpr/ppermute | solution.py:10
  713.2 16.7 %scatter_fusion = bf16[4096,128]{1,0:T(8,128)(2,1)S(1)} fusion(bf16[4096,128]{1,0:T(8,128)(2,1)S(1)} %bitcast.16, s32[6144]{0:T(1024)S(1)} %bitcast.24, bf16[6144,128]{1,0:T(8,128)(2,1)} %bitcast.22), kind=kCustom, calls=%fused_computation.4 | custom fusion | bytes 4743168 | tf_op jit(solution)/shard_map/scatter | solution.py:64
  731.9 6.4 collective-permute-start.3
  (260 shorter events, 167.6 us)
Async XLA Ops:
  31.3 36.6 %collective-permute-start = (bf16[48,128,128]{2,1,0:T(8,128)(2,1)}, bf16[48,128,128]{2,1,0:T(8,128)(2,1)S(1)}, u32[]{:S(2)}, u32[]{:S(2)}) collective-permute-start(bf16[48,128,128]{2,1,0:T(8,128)(2,1)} %fusion.11), channel_id=1, source_target_pairs={{0,8},{8,16},{16,24},{24,32},{32,40},{40,48},{48,56},{56,64},{64,7... | collective-permute-start | bytes 4718600 | tf_op jit(solution)/shard_map/while/body/eval_jaxpr/ppermute | solution.py:10
  33.1 34.8 %collective-permute-start.1 = (bf16[48,128]{1,0:T(8,128)(2,1)S(1)}, bf16[48,128]{1,0:T(8,128)(2,1)S(1)}, u32[]{:S(2)}, u32[]{:S(2)}) collective-permute-start(bf16[48,128]{1,0:T(8,128)(2,1)S(1)} %copy.15), channel_id=1, source_target_pairs={{0,8},{8,16},{16,24},{24,32},{32,40},{40,48},{48,56},{56,64},{64,7... | collective-permute-start | bytes 36872 | tf_op jit(solution)/shard_map/while/body/eval_jaxpr/ppermute | solution.py:10
  78.5 37.2 %collective-permute-start = (bf16[48,128,128]{2,1,0:T(8,128)(2,1)}, bf16[48,128,128]{2,1,0:T(8,128)(2,1)S(1)}, u32[]{:S(2)}, u32[]{:S(2)}) collective-permute-start(bf16[48,128,128]{2,1,0:T(8,128)(2,1)} %fusion.11), channel_id=1, source_target_pairs={{0,8},{8,16},{16,24},{24,32},{32,40},{40,48},{48,56},{56,64},{64,7... | collective-permute-start | bytes 4718600 | tf_op jit(solution)/shard_map/while/body/eval_jaxpr/ppermute | solution.py:10
  82.4 33.3 %collective-permute-start.1 = (bf16[48,128]{1,0:T(8,128)(2,1)S(1)}, bf16[48,128]{1,0:T(8,128)(2,1)S(1)}, u32[]{:S(2)}, u32[]{:S(2)}) collective-permute-start(bf16[48,128]{1,0:T(8,128)(2,1)S(1)} %copy.15), channel_id=1, source_target_pairs={{0,8},{8,16},{16,24},{24,32},{32,40},{40,48},{48,56},{56,64},{64,7... | collective-permute-start | bytes 36872 | tf_op jit(solution)/shard_map/while/body/eval_jaxpr/ppermute | solution.py:10
  126.3 36.9 %collective-permute-start = (bf16[48,128,128]{2,1,0:T(8,128)(2,1)}, bf16[48,128,128]{2,1,0:T(8,128)(2,1)S(1)}, u32[]{:S(2)}, u32[]{:S(2)}) collective-permute-start(bf16[48,128,128]{2,1,0:T(8,128)(2,1)} %fusion.11), channel_id=1, source_target_pairs={{0,8},{8,16},{16,24},{24,32},{32,40},{40,48},{48,56},{56,64},{64,7... | collective-permute-start | bytes 4718600 | tf_op jit(solution)/shard_map/while/body/eval_jaxpr/ppermute | solution.py:10
  130.8 32.3 %collective-permute-start.1 = (bf16[48,128]{1,0:T(8,128)(2,1)S(1)}, bf16[48,128]{1,0:T(8,128)(2,1)S(1)}, u32[]{:S(2)}, u32[]{:S(2)}) collective-permute-start(bf16[48,128]{1,0:T(8,128)(2,1)S(1)} %copy.15), channel_id=1, source_target_pairs={{0,8},{8,16},{16,24},{24,32},{32,40},{40,48},{48,56},{56,64},{64,7... | collective-permute-start | bytes 36872 | tf_op jit(solution)/shard_map/while/body/eval_jaxpr/ppermute | solution.py:10
  173.7 36.0 %collective-permute-start = (bf16[48,128,128]{2,1,0:T(8,128)(2,1)}, bf16[48,128,128]{2,1,0:T(8,128)(2,1)S(1)}, u32[]{:S(2)}, u32[]{:S(2)}) collective-permute-start(bf16[48,128,128]{2,1,0:T(8,128)(2,1)} %fusion.11), channel_id=1, source_target_pairs={{0,8},{8,16},{16,24},{24,32},{32,40},{40,48},{48,56},{56,64},{64,7... | collective-permute-start | bytes 4718600 | tf_op jit(solution)/shard_map/while/body/eval_jaxpr/ppermute | solution.py:10
  178.3 31.4 %collective-permute-start.1 = (bf16[48,128]{1,0:T(8,128)(2,1)S(1)}, bf16[48,128]{1,0:T(8,128)(2,1)S(1)}, u32[]{:S(2)}, u32[]{:S(2)}) collective-permute-start(bf16[48,128]{1,0:T(8,128)(2,1)S(1)} %copy.15), channel_id=1, source_target_pairs={{0,8},{8,16},{16,24},{24,32},{32,40},{40,48},{48,56},{56,64},{64,7... | collective-permute-start | bytes 36872 | tf_op jit(solution)/shard_map/while/body/eval_jaxpr/ppermute | solution.py:10
  220.3 35.1 %collective-permute-start = (bf16[48,128,128]{2,1,0:T(8,128)(2,1)}, bf16[48,128,128]{2,1,0:T(8,128)(2,1)S(1)}, u32[]{:S(2)}, u32[]{:S(2)}) collective-permute-start(bf16[48,128,128]{2,1,0:T(8,128)(2,1)} %fusion.11), channel_id=1, source_target_pairs={{0,8},{8,16},{16,24},{24,32},{32,40},{40,48},{48,56},{56,64},{64,7... | collective-permute-start | bytes 4718600 | tf_op jit(solution)/shard_map/while/body/eval_jaxpr/ppermute | solution.py:10
  224.9 30.5 %collective-permute-start.1 = (bf16[48,128]{1,0:T(8,128)(2,1)S(1)}, bf16[48,128]{1,0:T(8,128)(2,1)S(1)}, u32[]{:S(2)}, u32[]{:S(2)}) collective-permute-start(bf16[48,128]{1,0:T(8,128)(2,1)S(1)} %copy.15), channel_id=1, source_target_pairs={{0,8},{8,16},{16,24},{24,32},{32,40},{40,48},{48,56},{56,64},{64,7... | collective-permute-start | bytes 36872 | tf_op jit(solution)/shard_map/while/body/eval_jaxpr/ppermute | solution.py:10
  266.0 34.5 %collective-permute-start = (bf16[48,128,128]{2,1,0:T(8,128)(2,1)}, bf16[48,128,128]{2,1,0:T(8,128)(2,1)S(1)}, u32[]{:S(2)}, u32[]{:S(2)}) collective-permute-start(bf16[48,128,128]{2,1,0:T(8,128)(2,1)} %fusion.11), channel_id=1, source_target_pairs={{0,8},{8,16},{16,24},{24,32},{32,40},{40,48},{48,56},{56,64},{64,7... | collective-permute-start | bytes 4718600 | tf_op jit(solution)/shard_map/while/body/eval_jaxpr/ppermute | solution.py:10
  270.6 29.9 %collective-permute-start.1 = (bf16[48,128]{1,0:T(8,128)(2,1)S(1)}, bf16[48,128]{1,0:T(8,128)(2,1)S(1)}, u32[]{:S(2)}, u32[]{:S(2)}) collective-permute-start(bf16[48,128]{1,0:T(8,128)(2,1)S(1)} %copy.15), channel_id=1, source_target_pairs={{0,8},{8,16},{16,24},{24,32},{32,40},{40,48},{48,56},{56,64},{64,7... | collective-permute-start | bytes 36872 | tf_op jit(solution)/shard_map/while/body/eval_jaxpr/ppermute | solution.py:10
  311.0 34.8 %collective-permute-start = (bf16[48,128,128]{2,1,0:T(8,128)(2,1)}, bf16[48,128,128]{2,1,0:T(8,128)(2,1)S(1)}, u32[]{:S(2)}, u32[]{:S(2)}) collective-permute-start(bf16[48,128,128]{2,1,0:T(8,128)(2,1)} %fusion.11), channel_id=1, source_target_pairs={{0,8},{8,16},{16,24},{24,32},{32,40},{40,48},{48,56},{56,64},{64,7... | collective-permute-start | bytes 4718600 | tf_op jit(solution)/shard_map/while/body/eval_jaxpr/ppermute | solution.py:10
  315.3 30.5 %collective-permute-start.1 = (bf16[48,128]{1,0:T(8,128)(2,1)S(1)}, bf16[48,128]{1,0:T(8,128)(2,1)S(1)}, u32[]{:S(2)}, u32[]{:S(2)}) collective-permute-start(bf16[48,128]{1,0:T(8,128)(2,1)S(1)} %copy.15), channel_id=1, source_target_pairs={{0,8},{8,16},{16,24},{24,32},{32,40},{40,48},{48,56},{56,64},{64,7... | collective-permute-start | bytes 36872 | tf_op jit(solution)/shard_map/while/body/eval_jaxpr/ppermute | solution.py:10
  356.3 33.8 %collective-permute-start = (bf16[48,128,128]{2,1,0:T(8,128)(2,1)}, bf16[48,128,128]{2,1,0:T(8,128)(2,1)S(1)}, u32[]{:S(2)}, u32[]{:S(2)}) collective-permute-start(bf16[48,128,128]{2,1,0:T(8,128)(2,1)} %fusion.11), channel_id=1, source_target_pairs={{0,8},{8,16},{16,24},{24,32},{32,40},{40,48},{48,56},{56,64},{64,7... | collective-permute-start | bytes 4718600 | tf_op jit(solution)/shard_map/while/body/eval_jaxpr/ppermute | solution.py:10
  359.1 31.1 %collective-permute-start.1 = (bf16[48,128]{1,0:T(8,128)(2,1)S(1)}, bf16[48,128]{1,0:T(8,128)(2,1)S(1)}, u32[]{:S(2)}, u32[]{:S(2)}) collective-permute-start(bf16[48,128]{1,0:T(8,128)(2,1)S(1)} %copy.15), channel_id=1, source_target_pairs={{0,8},{8,16},{16,24},{24,32},{32,40},{40,48},{48,56},{56,64},{64,7... | collective-permute-start | bytes 36872 | tf_op jit(solution)/shard_map/while/body/eval_jaxpr/ppermute | solution.py:10
  400.7 32.9 %collective-permute-start = (bf16[48,128,128]{2,1,0:T(8,128)(2,1)}, bf16[48,128,128]{2,1,0:T(8,128)(2,1)S(1)}, u32[]{:S(2)}, u32[]{:S(2)}) collective-permute-start(bf16[48,128,128]{2,1,0:T(8,128)(2,1)} %fusion.11), channel_id=1, source_target_pairs={{0,8},{8,16},{16,24},{24,32},{32,40},{40,48},{48,56},{56,64},{64,7... | collective-permute-start | bytes 4718600 | tf_op jit(solution)/shard_map/while/body/eval_jaxpr/ppermute | solution.py:10
  401.9 31.7 %collective-permute-start.1 = (bf16[48,128]{1,0:T(8,128)(2,1)S(1)}, bf16[48,128]{1,0:T(8,128)(2,1)S(1)}, u32[]{:S(2)}, u32[]{:S(2)}) collective-permute-start(bf16[48,128]{1,0:T(8,128)(2,1)S(1)} %copy.15), channel_id=1, source_target_pairs={{0,8},{8,16},{16,24},{24,32},{32,40},{40,48},{48,56},{56,64},{64,7... | collective-permute-start | bytes 36872 | tf_op jit(solution)/shard_map/while/body/eval_jaxpr/ppermute | solution.py:10
  444.2 32.0 %collective-permute-start = (bf16[48,128,128]{2,1,0:T(8,128)(2,1)}, bf16[48,128,128]{2,1,0:T(8,128)(2,1)S(1)}, u32[]{:S(2)}, u32[]{:S(2)}) collective-permute-start(bf16[48,128,128]{2,1,0:T(8,128)(2,1)} %fusion.11), channel_id=1, source_target_pairs={{0,8},{8,16},{16,24},{24,32},{32,40},{40,48},{48,56},{56,64},{64,7... | collective-permute-start | bytes 4718600 | tf_op jit(solution)/shard_map/while/body/eval_jaxpr/ppermute | solution.py:10
  444.2 32.0 %collective-permute-start.1 = (bf16[48,128]{1,0:T(8,128)(2,1)S(1)}, bf16[48,128]{1,0:T(8,128)(2,1)S(1)}, u32[]{:S(2)}, u32[]{:S(2)}) collective-permute-start(bf16[48,128]{1,0:T(8,128)(2,1)S(1)} %copy.15), channel_id=1, source_target_pairs={{0,8},{8,16},{16,24},{24,32},{32,40},{40,48},{48,56},{56,64},{64,7... | collective-permute-start | bytes 36872 | tf_op jit(solution)/shard_map/while/body/eval_jaxpr/ppermute | solution.py:10
  486.8 31.1 %collective-permute-start = (bf16[48,128,128]{2,1,0:T(8,128)(2,1)}, bf16[48,128,128]{2,1,0:T(8,128)(2,1)S(1)}, u32[]{:S(2)}, u32[]{:S(2)}) collective-permute-start(bf16[48,128,128]{2,1,0:T(8,128)(2,1)} %fusion.11), channel_id=1, source_target_pairs={{0,8},{8,16},{16,24},{24,32},{32,40},{40,48},{48,56},{56,64},{64,7... | collective-permute-start | bytes 4718600 | tf_op jit(solution)/shard_map/while/body/eval_jaxpr/ppermute | solution.py:10
  486.8 31.1 %collective-permute-start.1 = (bf16[48,128]{1,0:T(8,128)(2,1)S(1)}, bf16[48,128]{1,0:T(8,128)(2,1)S(1)}, u32[]{:S(2)}, u32[]{:S(2)}) collective-permute-start(bf16[48,128]{1,0:T(8,128)(2,1)S(1)} %copy.15), channel_id=1, source_target_pairs={{0,8},{8,16},{16,24},{24,32},{32,40},{40,48},{48,56},{56,64},{64,7... | collective-permute-start | bytes 36872 | tf_op jit(solution)/shard_map/while/body/eval_jaxpr/ppermute | solution.py:10
  528.4 30.1 %collective-permute-start = (bf16[48,128,128]{2,1,0:T(8,128)(2,1)}, bf16[48,128,128]{2,1,0:T(8,128)(2,1)S(1)}, u32[]{:S(2)}, u32[]{:S(2)}) collective-permute-start(bf16[48,128,128]{2,1,0:T(8,128)(2,1)} %fusion.11), channel_id=1, source_target_pairs={{0,8},{8,16},{16,24},{24,32},{32,40},{40,48},{48,56},{56,64},{64,7... | collective-permute-start | bytes 4718600 | tf_op jit(solution)/shard_map/while/body/eval_jaxpr/ppermute | solution.py:10
  528.4 30.1 %collective-permute-start.1 = (bf16[48,128]{1,0:T(8,128)(2,1)S(1)}, bf16[48,128]{1,0:T(8,128)(2,1)S(1)}, u32[]{:S(2)}, u32[]{:S(2)}) collective-permute-start(bf16[48,128]{1,0:T(8,128)(2,1)S(1)} %copy.15), channel_id=1, source_target_pairs={{0,8},{8,16},{16,24},{24,32},{32,40},{40,48},{48,56},{56,64},{64,7... | collective-permute-start | bytes 36872 | tf_op jit(solution)/shard_map/while/body/eval_jaxpr/ppermute | solution.py:10
  569.1 29.2 %collective-permute-start = (bf16[48,128,128]{2,1,0:T(8,128)(2,1)}, bf16[48,128,128]{2,1,0:T(8,128)(2,1)S(1)}, u32[]{:S(2)}, u32[]{:S(2)}) collective-permute-start(bf16[48,128,128]{2,1,0:T(8,128)(2,1)} %fusion.11), channel_id=1, source_target_pairs={{0,8},{8,16},{16,24},{24,32},{32,40},{40,48},{48,56},{56,64},{64,7... | collective-permute-start | bytes 4718600 | tf_op jit(solution)/shard_map/while/body/eval_jaxpr/ppermute | solution.py:10
  569.1 29.2 %collective-permute-start.1 = (bf16[48,128]{1,0:T(8,128)(2,1)S(1)}, bf16[48,128]{1,0:T(8,128)(2,1)S(1)}, u32[]{:S(2)}, u32[]{:S(2)}) collective-permute-start(bf16[48,128]{1,0:T(8,128)(2,1)S(1)} %copy.15), channel_id=1, source_target_pairs={{0,8},{8,16},{16,24},{24,32},{32,40},{40,48},{48,56},{56,64},{64,7... | collective-permute-start | bytes 36872 | tf_op jit(solution)/shard_map/while/body/eval_jaxpr/ppermute | solution.py:10
  608.9 28.3 %collective-permute-start = (bf16[48,128,128]{2,1,0:T(8,128)(2,1)}, bf16[48,128,128]{2,1,0:T(8,128)(2,1)S(1)}, u32[]{:S(2)}, u32[]{:S(2)}) collective-permute-start(bf16[48,128,128]{2,1,0:T(8,128)(2,1)} %fusion.11), channel_id=1, source_target_pairs={{0,8},{8,16},{16,24},{24,32},{32,40},{40,48},{48,56},{56,64},{64,7... | collective-permute-start | bytes 4718600 | tf_op jit(solution)/shard_map/while/body/eval_jaxpr/ppermute | solution.py:10
  608.9 28.3 %collective-permute-start.1 = (bf16[48,128]{1,0:T(8,128)(2,1)S(1)}, bf16[48,128]{1,0:T(8,128)(2,1)S(1)}, u32[]{:S(2)}, u32[]{:S(2)}) collective-permute-start(bf16[48,128]{1,0:T(8,128)(2,1)S(1)} %copy.15), channel_id=1, source_target_pairs={{0,8},{8,16},{16,24},{24,32},{32,40},{40,48},{48,56},{56,64},{64,7... | collective-permute-start | bytes 36872 | tf_op jit(solution)/shard_map/while/body/eval_jaxpr/ppermute | solution.py:10
  647.7 27.3 %collective-permute-start = (bf16[48,128,128]{2,1,0:T(8,128)(2,1)}, bf16[48,128,128]{2,1,0:T(8,128)(2,1)S(1)}, u32[]{:S(2)}, u32[]{:S(2)}) collective-permute-start(bf16[48,128,128]{2,1,0:T(8,128)(2,1)} %fusion.11), channel_id=1, source_target_pairs={{0,8},{8,16},{16,24},{24,32},{32,40},{40,48},{48,56},{56,64},{64,7... | collective-permute-start | bytes 4718600 | tf_op jit(solution)/shard_map/while/body/eval_jaxpr/ppermute | solution.py:10
  647.7 27.3 %collective-permute-start.1 = (bf16[48,128]{1,0:T(8,128)(2,1)S(1)}, bf16[48,128]{1,0:T(8,128)(2,1)S(1)}, u32[]{:S(2)}, u32[]{:S(2)}) collective-permute-start(bf16[48,128]{1,0:T(8,128)(2,1)S(1)} %copy.15), channel_id=1, source_target_pairs={{0,8},{8,16},{16,24},{24,32},{32,40},{40,48},{48,56},{56,64},{64,7... | collective-permute-start | bytes 36872 | tf_op jit(solution)/shard_map/while/body/eval_jaxpr/ppermute | solution.py:10
  685.6 26.4 %collective-permute-start = (bf16[48,128,128]{2,1,0:T(8,128)(2,1)}, bf16[48,128,128]{2,1,0:T(8,128)(2,1)S(1)}, u32[]{:S(2)}, u32[]{:S(2)}) collective-permute-start(bf16[48,128,128]{2,1,0:T(8,128)(2,1)} %fusion.11), channel_id=1, source_target_pairs={{0,8},{8,16},{16,24},{24,32},{32,40},{40,48},{48,56},{56,64},{64,7... | collective-permute-start | bytes 4718600 | tf_op jit(solution)/shard_map/while/body/eval_jaxpr/ppermute | solution.py:10
  685.6 26.4 %collective-permute-start.1 = (bf16[48,128]{1,0:T(8,128)(2,1)S(1)}, bf16[48,128]{1,0:T(8,128)(2,1)S(1)}, u32[]{:S(2)}, u32[]{:S(2)}) collective-permute-start(bf16[48,128]{1,0:T(8,128)(2,1)S(1)} %copy.15), channel_id=1, source_target_pairs={{0,8},{8,16},{16,24},{24,32},{32,40},{40,48},{48,56},{56,64},{64,7... | collective-permute-start | bytes 36872 | tf_op jit(solution)/shard_map/while/body/eval_jaxpr/ppermute | solution.py:10
  (27 other events, 85.0 us)
where the time goes:
time: 763 us; the launch traced here: 750 us
  waiting for transfers between devices  491 us (64%)
  local copies, waits for them, and re-layouts  142 us (19%)
  matrix products  61.2 us (8%)
  starting transfers between devices  48 us (6%)
    ppermute x32, waiting for transfers between devices, from_behind(): return lax.ppermute(value, axis, pairs)  488 us
    gather x16, local copies, waits for them, and re-layouts, evaluate(): table_sens[chosen]  67.7 us
    dot_general x16, matrix products, evaluate(): jnp.einsum('kqi,kij->kqj', delta, table_sens[chosen], preferred_element_t...  61.2 us
    ppermute x32, starting transfers between devices, from_behind(): return lax.ppermute(value, axis, pairs)  34.1 us
    while x32, local copies, waits for them, and re-layouts  18.3 us
    gather x1, local copies, waits for them, and re-layouts, local(): picked = flat[jnp.maximum(slots, 0)]  18.1 us
    scatter x1, local copies, waits for them, and re-layouts, local(): reacted = flat.at[target].set(results.reshape(-1, width), mode='drop').re...  16.7 us
  transfers between devices with their start and end apart: 36, of which 18 were waited for; matrix products, arithmetic and copies ran while one was open for 0% of the time, Pallas kernels for 0%

commit v1 on v0

v1 whole, which is shorter than its diff:
```python
import jax
import jax.numpy as jnp
from jax import lax
from jax.experimental import pallas as pl
from jax.experimental.pallas import tpu as pltpu
from jax.sharding import PartitionSpec as P

F32 = jnp.float32
BF16 = jnp.bfloat16
CAP = 512
META = 16
SEG = CAP + META
WIN = 16


def iota(shape, dim):
    return lax.broadcasted_iota(jnp.int32, shape, dim)


def zero_one(mask):
    return jnp.where(mask, 1.0, 0.0).astype(BF16)


def dot(a, b):
    return lax.dot_general(a, b, (((1,), (0,)), ((), ())), preferred_element_type=F32)


def dot_nt(a, b):
    return lax.dot_general(a, b, (((1,), (1,)), ((), ())), preferred_element_type=F32)


def pack_kernel(
    nparts, me_ref, slots_ref, hits_ref, state_ref, send_ref, back_ref,
    field, packed, code_vmem, code_smem, sem,
):
    nblocks, width = slots_ref.shape
    cells = state_ref.shape[0]
    slots = slots_ref[...]
    live = slots >= 0
    cell = jnp.maximum(slots, 0)
    owner = jnp.where(live, (hits_ref[...] + me_ref[0]) & (nparts - 1), nparts)
    before = zero_one(iota((width, width), 0) < iota((width, width), 1))
    both = jnp.concatenate([before, jnp.ones((width, width), BF16)], axis=1)
    earlier = zero_one(iota((nblocks, nblocks), 1) < iota((nblocks, nblocks), 0))
    starts = zero_one(iota((nblocks, width), 0) < iota((nblocks, width), 1))
    ones = jnp.ones((META, width), BF16)
    top = iota((META, width), 0) == 0
    place = jnp.zeros((nblocks, width), F32)
    for part in range(nparts):
        mine = owner == part
        mask = zero_one(mine)
        ranks = dot(mask, both)
        offsets = dot(earlier, ranks[:, width:].astype(BF16))
        place = place + jnp.where(mine, ranks[:, :width] + offsets, 0.0)
        in_lanes = dot_nt(ones, mask).astype(BF16)
        begin = dot(in_lanes, starts)
        high = jnp.floor(begin * (1.0 / 16.0))
        send_ref[pl.ds(part * SEG + CAP, META), :] = jnp.where(
            top, high, begin - 16.0 * high
        ).astype(BF16)
    place = place.astype(jnp.int32)
    forth = jnp.where(live, owner * SEG + place, nparts * SEG)
    code_vmem[...] = forth * cells + cell
    back_ref[...] = jnp.where(live, (owner * CAP + place) * (2 * cells) + cell, cells)
    copy = pltpu.make_async_copy(code_vmem, code_smem, sem)
    copy.start()
    field[...] = state_ref[...].astype(F32)
    copy.wait()

    def block(k, _):
        for q in range(width):
            code = code_smem[k, q]
            packed[pl.ds(code // cells, 1), :] = field[pl.ds(code & (cells - 1), 1), :]
        return 0

    lax.fori_loop(0, nblocks, block, 0)

    def convert(part, _):
        at = pl.multiple_of(part * SEG, 16)
        send_ref[pl.ds(at, CAP), :] = packed[pl.ds(at, CAP), :].astype(BF16)
        return 0

    lax.fori_loop(0, nparts, convert, 0)


def pack(me, slots, hits, flat, nparts):
    nblocks, width = slots.shape
    cells = flat.shape[0]
    return pl.pallas_call(
        lambda *refs: pack_kernel(nparts, *refs),
        out_shape=(
            jax.ShapeDtypeStruct((nparts * SEG, width), BF16),
            jax.ShapeDtypeStruct((nblocks, width), jnp.int32),
        ),
        in_specs=[pl.BlockSpec(memory_space=pltpu.SMEM)]
        + [pl.BlockSpec(memory_space=pltpu.VMEM)] * 3,
        out_specs=[pl.BlockSpec(memory_space=pltpu.VMEM)] * 2,
        scratch_shapes=[
            pltpu.VMEM((cells, width), F32),
            pltpu.VMEM((nparts * SEG + 8, width), F32),
            pltpu.VMEM((nblocks, width), jnp.int32),
            pltpu.SMEM((nblocks, width), jnp.int32),
            pltpu.SemaphoreType.DMA,
        ],
        compiler_params=pltpu.CompilerParams(vmem_limit_bytes=32 << 20),
    )(me, slots, hits, flat)


def react_kernel(
    nparts, nblocks, entries_ref, recv_ref, value_ref, base_ref, sens_ref, out_ref,
    rows, mapped, begin_vmem, begin_smem, sem,
):
    width = recv_ref.shape[1]
    for part in range(nparts):
        meta = recv_ref[pl.ds(part * SEG + CAP, META), :].astype(F32)
        begin_vmem[pl.ds(part, 1), :] = (meta[0:1] * 16.0 + meta[1:2]).astype(jnp.int32)
    copy = pltpu.make_async_copy(begin_vmem, begin_smem, sem)
    copy.start()

    def widen(part, _):
        at = pl.multiple_of(part * SEG, 16)
        rows[pl.ds(at, SEG), :] = recv_ref[pl.ds(at, SEG), :].astype(F32)
        return 0

    lax.fori_loop(0, nparts, widen, 0)
    copy.wait()
    zero = jnp.zeros((WIN, width), BF16)
    four = 4

    def delta(at, entry):
        base = base_ref[pl.ds(entry, 1), :]
        return (rows[pl.ds(at, WIN), :] - base).astype(BF16)

    def fours(step, _):
        part = step // (nblocks // four)
        first = (step % (nblocks // four)) * four
        begins = [begin_smem[part, first + i] for i in range(four + 1)]
        entry = [entries_ref[part * nblocks + first + i] for i in range(four)]
        at = [part * SEG + begins[i] for i in range(four)]
        dx = [delta(at[i], entry[i]) for i in range(four)]
        lhs = jnp.concatenate(
            [
                jnp.concatenate([dx[0], zero], axis=1),
                jnp.concatenate([dx[1], zero], axis=1),
                jnp.concatenate([zero, dx[2]], axis=1),
                jnp.concatenate([zero, dx[3]], axis=1),
            ],
            axis=0,
        )
        rhs = jnp.concatenate(
            [
                jnp.concatenate([sens_ref[entry[0]], sens_ref[entry[1]]], axis=1),
                jnp.concatenate([sens_ref[entry[2]], sens_ref[entry[3]]], axis=1),
            ],
            axis=0,
        )
        product = dot(lhs, rhs)
        for i in range(four):
            half = (i % 2) * width
            mapped[pl.ds(at[i], WIN), :] = (
                product[i * WIN : (i + 1) * WIN, half : half + width]
                + value_ref[pl.ds(entry[i], 1), :]
            )
        counts = [begins[i + 1] - begins[i] for i in range(four)]
        most = jnp.maximum(
            jnp.maximum(counts[0], counts[1]), jnp.maximum(counts[2], counts[3])
        )

        @pl.when(most > WIN)
        def _():
            for i in range(four):

                def more(w, _, i=i):
                    here = at[i] + w * WIN
                    left = counts[i] - w * WIN
                    result = dot(delta(here, entry[i]), sens_ref[entry[i]])
                    result = result + value_ref[pl.ds(entry[i], 1), :]
                    keep = iota((WIN, width), 0) < left
                    mapped[pl.ds(here, WIN), :] = jnp.where(
                        keep, result, mapped[pl.ds(here, WIN), :]
                    )
                    return 0

                lax.fori_loop(1, (counts[i] + WIN - 1) // WIN, more, 0)

        return 0

    lax.fori_loop(0, nparts * nblocks // four, fours, 0)

    def narrow(part, _):
        out_ref[pl.ds(pl.multiple_of(part * CAP, 16), CAP), :] = mapped[
            pl.ds(pl.multiple_of(part * SEG, 16), CAP), :
        ].astype(BF16)
        return 0

    lax.fori_loop(0, nparts, narrow, 0)


def react(entries, recv, value, base, sens, nparts):
    width = recv.shape[1]
    nblocks = entries.shape[0] // nparts
    return pl.pallas_call(
        lambda *refs: react_kernel(nparts, nblocks, *refs),
        out_shape=jax.ShapeDtypeStruct((nparts * CAP, width), BF16),
        in_specs=[pl.BlockSpec(memory_space=pltpu.SMEM)]
        + [pl.BlockSpec(memory_space=pltpu.VMEM)] * 4,
        out_specs=pl.BlockSpec(memory_space=pltpu.VMEM),
        scratch_shapes=[
            pltpu.VMEM((nparts * SEG, width), F32),
            pltpu.VMEM((nparts * SEG, width), F32),
            pltpu.VMEM((nparts, width), jnp.int32),
            pltpu.SMEM((nparts, width), jnp.int32),
            pltpu.SemaphoreType.DMA,
        ],
        compiler_params=pltpu.CompilerParams(vmem_limit_bytes=48 << 20),
    )(entries, recv, value.astype(F32), base.astype(F32), sens)


def unpack_kernel(code_ref, ret_ref, out_ref, rows, field):
    nblocks, width = code_ref.shape
    cells = out_ref.shape[0]
    rows[...] = ret_ref[...].astype(F32)

    def block(k, _):
        for q in range(width):
            code = code_ref[k, q]
            field[pl.ds(code & (2 * cells - 1), 1), :] = rows[
                pl.ds(code // (2 * cells), 1), :
            ]
        return 0

    lax.fori_loop(0, nblocks, block, 0)
    out_ref[...] = field[pl.ds(0, cells), :].astype(BF16)


def unpack(code, ret, cells):
    width = ret.shape[1]
    return pl.pallas_call(
        unpack_kernel,
        out_shape=jax.ShapeDtypeStruct((cells, width), BF16),
        in_specs=[
            pl.BlockSpec(memory_space=pltpu.SMEM),
            pl.BlockSpec(memory_space=pltpu.VMEM),
        ],
        out_specs=pl.BlockSpec(memory_space=pltpu.VMEM),
        scratch_shapes=[
            pltpu.VMEM(ret.shape, F32),
            pltpu.VMEM((cells + 8, width), F32),
        ],
        compiler_params=pltpu.CompilerParams(vmem_limit_bytes=32 << 20),
    )(code, ret)


def transport_kernel(
    mid_ref, up_ref, down_ref, left_ref, right_ref, courant_ref, diffusion_ref, out_ref
):
    rows_here, cols, width = mid_ref.shape
    diffusion = diffusion_ref[...]
    first = iota((cols, width), 0) == 0
    last = iota((cols, width), 0) == cols - 1

    def row(i):
        if i < 0:
            return up_ref[...].astype(F32)
        if i >= rows_here:
            return down_ref[...].astype(F32)
        return mid_ref[i].astype(F32)

    above, here = row(-1), row(0)
    for i in range(rows_here):
        below = row(i + 1)
        left = jnp.where(first, left_ref[i : i + 1, :].astype(F32), pltpu.roll(here, 1, 0))
        right = jnp.where(
            last, right_ref[i : i + 1, :].astype(F32), pltpu.roll(here, cols - 1, 0)
        )
        courant = courant_ref[:, i : i + 1]
        out_ref[i] = (
            here
            - courant * (here - above)
            + diffusion * (above + below + left + right - 4.0 * here)
        )
        above, here = here, below


def transport(reacted, up, down, left, right, courant, diffusion):
    shape = reacted.shape
    return pl.pallas_call(
        transport_kernel,
        out_shape=jax.ShapeDtypeStruct(shape, F32),
        in_specs=[pl.BlockSpec(memory_space=pltpu.VMEM)] * 7,
        out_specs=pl.BlockSpec(memory_space=pltpu.VMEM),
        compiler_params=pltpu.CompilerParams(vmem_limit_bytes=32 << 20),
    )(reacted, up, down, left, right, courant, diffusion)


def shifted(block, axis, ahead):
    count = lax.axis_size(axis)
    forward = [(i, i + 1) for i in range(count - 1)]
    return lax.ppermute(block, axis, forward if ahead else [(j, i) for i, j in forward])


def local(
    state, courant, diffusion, table_value, table_base, table_sens, slot_cell, hit_step, entry_ids
):
    rows_here, cols_here, width = state.shape
    cells = rows_here * cols_here
    nparts = lax.axis_size("blk")
    me = lax.axis_index("blk").astype(jnp.int32).reshape(1)
    flat = state.reshape(cells, width)
    send, code = pack(me, slot_cell[0], hit_step[0], flat, nparts)
    recv = lax.all_to_all(send.reshape(nparts, SEG, width), "blk", 0, 0, tiled=True)
    done = react(
        entry_ids[0, 0], recv.reshape(nparts * SEG, width),
        table_value, table_base, table_sens, nparts,
    )
    back = lax.all_to_all(done.reshape(nparts, CAP, width), "blk", 0, 0, tiled=True)
    reacted = unpack(code, back.reshape(nparts * CAP, width), cells)
    reacted = reacted.reshape(rows_here, cols_here, width)
    left = shifted(reacted[:, -1], "blk", True)
    right = shifted(reacted[:, 0], "blk", False)
    up = shifted(reacted[-1], "grid", True)
    down = shifted(reacted[0], "grid", False)
    return transport(
        reacted, up, down, left, right, courant.T, diffusion.reshape(1, width)
    )


def solution(mesh):
    return jax.shard_map(
        local,
        mesh=mesh,
        in_specs=(
            P("grid", "blk", None),
            P("grid", "blk"),
            P(),
            P("blk", None),
            P("blk", None),
            P("blk", None, None),
            P("grid", "blk", None),
            P("grid", "blk", None),
            P("blk", "grid", None),
        ),
        out_specs=P("grid", "blk", None),
        check_vma=False,
    )
```

time: 763 us -> 202 us (0.26); the launches traced: 750 us -> 202 us
  waiting for transfers between devices: 491 us -> 34.4 us
  local copies, waits for them, and re-layouts: 142 us -> 4.21 us
  Pallas kernels: 0 us -> 110 us
  matrix products: 61.2 us -> 0 us
  blocking collectives: 0 us -> 32.9 us
  starting transfers between devices: 48 us -> 19.8 us
    ppermute x36 -> x4, waiting for transfers between devices: 491 us -> 5.1 us  [shifted(): lax.ppermute(block, axis, forward if ahead else [(j, i) for i, j in forwa...]
    pallas_call x0 -> x4, Pallas kernels: none -> 110 us  [the longest x1 37.9 us: pack(): pl.pallas_call(lambda *refs: pack_kernel(nparts, *refs), out_shape=(jax.S...]
    gather x49 -> x0, local copies, waits for them, and re-layouts: 105 us -> none  [the longest x16 67.7 us: evaluate(): table_sens[chosen]]
    dot_general x16 -> x0, matrix products: 61.2 us -> none  [evaluate(): jnp.einsum('kqi,kij->kqj', delta, table_sens[chosen], preferred_element_t...]
    ppermute x36 -> x4, starting transfers between devices: 48 us -> 11.4 us  [shifted(): lax.ppermute(block, axis, forward if ahead else [(j, i) for i, j in forwa...]
    all_to_all x0 -> x1, blocking collectives: none -> 32.9 us  [local(): lax.all_to_all(done.reshape(nparts, CAP, width), 'blk', 0, 0, tiled=True)]
    all_to_all x0 -> x1, waiting for transfers between devices: none -> 29.3 us  [local(): lax.all_to_all(send.reshape(nparts, SEG, width), 'blk', 0, 0, tiled=True)]
    while x32 -> x0, local copies, waits for them, and re-layouts: 18.3 us -> none
  transfers between devices with their start and end apart: 36 -> 5, of which waited for: 18 -> 2; matrix products, arithmetic and copies ran while one was open for 0% -> 0% of each run, Pallas kernels for 0% -> 0%
where the time goes in v1:
time: 202 us
  Pallas kernels  110 us (54%)
  waiting for transfers between devices  34.4 us (17%)
  blocking collectives  32.9 us (16%)
  starting transfers between devices  19.8 us (10%)
  local copies, waits for them, and re-layouts  4.21 us (2%)
    pallas_call x1, Pallas kernels, pack(): pl.pallas_call(lambda *refs: pack_kernel(nparts, *refs), out_shape=(jax.S...  37.9 us
    pallas_call x1, Pallas kernels, unpack(): pl.pallas_call(unpack_kernel, out_shape=jax.ShapeDtypeStruct((cells, widt...  35.4 us
    pallas_call x1, Pallas kernels, react(): pl.pallas_call(lambda *refs: react_kernel(nparts, nblocks, *refs), out_sh...  34.6 us
    all_to_all x1, blocking collectives, local(): lax.all_to_all(done.reshape(nparts, CAP, width), 'blk', 0, 0, tiled=True)  32.9 us
    all_to_all x1, waiting for transfers between devices, local(): lax.all_to_all(send.reshape(nparts, SEG, width), 'blk', 0, 0, tiled=True)  29.3 us
    ppermute x4, starting transfers between devices, shifted(): lax.ppermute(block, axis, forward if ahead else [(j, i) for i, j in forwa...  11.4 us
    all_to_all x1, starting transfers between devices, local(): lax.all_to_all(send.reshape(nparts, SEG, width), 'blk', 0, 0, tiled=True)  8.4 us
    ppermute x4, waiting for transfers between devices, shifted(): lax.ppermute(block, axis, forward if ahead else [(j, i) for i, j in forwa...  5.1 us
  transfers between devices with their start and end apart: 5, of which 2 were waited for; matrix products, arithmetic and copies ran while one was open for 0% of the time, Pallas kernels for 0%

profile of v1, /device:TPU:30, one launch (start us, length us, event | category | flops | bytes accessed | tf_op | source)
XLA Modules:
  0.0 201.8 jit_solution(13818815564957520081)
XLA Ops:
  0.0 0.0 copy-start.1
  0.0 1.2 copy-done.1
  1.2 0.0 copy-start.2
  1.2 0.7 copy-done.2
  2.0 0.0 copy-start.3
  2.0 0.7 copy-done.3
  2.7 37.9 %shard_map.91 = (bf16[8448,128]{1,0:T(8,128)(2,1)S(1)}, s32[48,128]{1,0:T(8,128)S(1)}) custom-call(s32[1]{0:T(128)} %bitcast.refs_0_, s32[48,128]{1,0:T(8,128)S(1)} %bitcast.25, s32[48,128]{1,0:T(8,128)S(1)} %bitcast.26, bf16[4096,128]{1,0:T(8,128)(2,1)S(1)} %bitcast.23), custom_call_target="tpu_custom_call" | custom-call | tf_op jit(solution)/shard_map/pallas_call | solution.py:89
  40.6 0.0 copy-start
  40.6 1.4 copy-done
  42.0 0.0 copy-start.5
  42.0 0.0 copy-start.6
  42.0 0.0 copy-start.8
  42.0 8.4 %all-to-all-start = ((bf16[16,528,128]{2,1,0:T(8,128)(2,1)}), bf16[16,528,128]{2,1,0:T(8,128)(2,1)S(1)}, u32[]{:S(2)}, u32[]{:S(2)}) async-start(bf16[16,528,128]{2,1,0:T(8,128)(2,1)} %bitcast.22), calls=%async_computation | async-start | bytes 4325376 | tf_op jit(solution)/shard_map/all_to_all | solution.py:311
  50.4 0.0 copy-done.5
  50.4 0.0 copy-done.6
  50.4 0.0 copy-done.8
  50.4 29.3 %all-to-all-done = bf16[16,528,128]{2,1,0:T(8,128)(2,1)S(1)} async-done(((bf16[16,528,128]{2,1,0:T(8,128)(2,1)}), bf16[16,528,128]{2,1,0:T(8,128)(2,1)S(1)}, u32[]{:S(2)}, u32[]{:S(2)}) %all-to-all-start) | async-done | bytes 2162720 | tf_op jit(solution)/shard_map/all_to_all | solution.py:311
  79.7 34.6 %shard_map.92 = bf16[8192,128]{1,0:T(8,128)(2,1)S(1)} custom-call(s32[768]{0:T(1024)S(1)} %reduce.refs_0_, bf16[8448,128]{1,0:T(8,128)(2,1)S(1)} %bitcast.17, f32[256,128]{1,0:T(8,128)S(1)} %convert_element_type.6.refs_2_, f32[256,128]{1,0:T(8,128)S(1)} %convert_element_type.7.refs_3_, bf16[256,128,128]{2,1,0:T(8,128)(2,1)} %refs_4_.1), custom_call_target="tpu_custom_call" | custom-call | tf_op jit(solution)/shard_map/pallas_call | solution.py:202
  114.3 32.9 %all_to_all.10 = bf16[16,512,128]{2,1,0:T(8,128)(2,1)S(1)} all-to-all(bf16[16,512,128]{2,1,0:T(8,128)(2,1)S(1)} %bitcast.19), channel_id=1, replica_groups=mesh['blk'=16,'grid'=8] {'blk'}, dimensions={0} | all-to-all | bytes 4194304 | tf_op jit(solution)/shard_map/all_to_all | solution.py:316
  147.1 35.4 %shard_map.93 = bf16[4096,128]{1,0:T(8,128)(2,1)S(1)} custom-call(s32[48,128]{1,0:T(8,128)S(1)} %get-tuple-element.7.code_ref, bf16[8192,128]{1,0:T(8,128)(2,1)S(1)} %bitcast.18), custom_call_target="tpu_custom_call" | custom-call | tf_op jit(solution)/shard_map/pallas_call | solution.py:238
  182.6 1.9 collective-permute-start
  184.5 3.6 %collective-permute-start.1 = (bf16[128,128]{1,0:T(8,128)(2,1)S(1)}, bf16[128,128]{1,0:T(8,128)(2,1)S(1)}, u32[]{:S(2)}, u32[]{:S(2)}) collective-permute-start(bf16[128,128]{1,0:T(8,128)(2,1)S(1)} %get-tuple-element.11), channel_id=1, source_target_pairs={{1,0},{2,1},{3,2},{4,3},{5,4},{6,5},{7,6},{9,8},{10,9},{11,10},{12... | collective-permute-start | bytes 98312 | tf_op jit(solution)/shard_map/ppermute | solution.py:299
  188.2 3.4 %collective-permute-start.2 = (bf16[32,128]{1,0:T(8,128)(2,1)S(1)}, bf16[32,128]{1,0:T(8,128)(2,1)S(1)}, u32[]{:S(2)}, u32[]{:S(2)}) collective-permute-start(bf16[32,128]{1,0:T(8,128)(2,1)S(1)} %bitcast.28), channel_id=1, source_target_pairs={{0,8},{8,16},{16,24},{24,32},{32,40},{40,48},{48,56},{56,64},{64,7... | collective-permute-start | bytes 24584 | tf_op jit(solution)/shard_map/ppermute | solution.py:299
  191.7 2.4 %collective-permute-start.3 = (bf16[32,128]{1,0:T(8,128)(2,1)S(1)}, bf16[32,128]{1,0:T(8,128)(2,1)S(1)}, u32[]{:S(2)}, u32[]{:S(2)}) collective-permute-start(bf16[32,128]{1,0:T(8,128)(2,1)S(1)} %bitcast.29), channel_id=1, source_target_pairs={{8,0},{16,8},{24,16},{32,24},{40,32},{48,40},{56,48},{64,56},{72,6... | collective-permute-start | bytes 24584 | tf_op jit(solution)/shard_map/ppermute | solution.py:299
  194.1 0.0 copy-done.7
  194.1 0.1 copy.14
  194.2 0.0 collective-permute-done.2.left_ref
  194.2 5.1 %collective-permute-done.3.right_ref = bf16[32,128]{1,0:T(8,128)(2,1)S(1)} collective-permute-done((bf16[32,128]{1,0:T(8,128)(2,1)S(1)}, bf16[32,128]{1,0:T(8,128)(2,1)S(1)}, u32[]{:S(2)}, u32[]{:S(2)}) %collective-permute-start.3) | collective-permute-done | bytes 8224 | tf_op jit(solution)/shard_map/ppermute | solution.py:299
  199.3 0.0 collective-permute-done.up_ref
  199.3 0.0 collective-permute-done.1.down_ref
  199.3 0.0 copy-done.4
  199.3 2.5 %shard_map.94 = f32[32,128,128]{2,1,0:T(8,128)} custom-call(bf16[32,128,128]{2,1,0:T(8,128)(2,1)S(1)} %bitcast.21, bf16[128,128]{1,0:T(8,128)(2,1)S(1)} %collective-permute-done.up_ref, bf16[128,128]{1,0:T(8,128)(2,1)S(1)} %collective-permute-done.1.down_ref, bf16[32,128]{1,0:T(8,128)(2,1)S(1)} %collective-permute-done.2.left_ref, ...), custom_call_target="tpu_custom_call" | custom-call | tf_op jit(solution)/shard_map/pallas_call | solution.py:287
  (9 shorter events, 0.1 us)
Async XLA Ops:
  0.0 1.2 copy-start.1
  1.2 0.7 copy-start.2
  2.0 0.7 copy-start.3
  40.6 1.4 copy-start
  42.0 8.4 %copy-start.5 = (bf16[256,128]{1,0:T(8,128)(2,1)S(1)}, bf16[256,128]{1,0:T(8,128)(2,1)}, u32[]{:S(2)}) copy-start(bf16[256,128]{1,0:T(8,128)(2,1)} %param.12) | copy-start | bytes 196612
  42.0 8.4 %copy-start.6 = (bf16[256,128]{1,0:T(8,128)(2,1)S(1)}, bf16[256,128]{1,0:T(8,128)(2,1)}, u32[]{:S(2)}) copy-start(bf16[256,128]{1,0:T(8,128)(2,1)} %param.13) | copy-start | bytes 196612
  42.0 8.5 %copy-start.8 = (s32[1,1,768]{2,1,0:T(1,128)S(1)}, s32[1,1,768]{2,1,0:T(1,128)}, u32[]{:S(2)}) copy-start(s32[1,1,768]{2,1,0:T(1,128)} %param.17) | copy-start | bytes 9220
  42.0 37.7 %all-to-all-start = ((bf16[16,528,128]{2,1,0:T(8,128)(2,1)}), bf16[16,528,128]{2,1,0:T(8,128)(2,1)S(1)}, u32[]{:S(2)}, u32[]{:S(2)}) async-start(bf16[16,528,128]{2,1,0:T(8,128)(2,1)} %bitcast.22), calls=%async_computation | async-start | bytes 4325376 | tf_op jit(solution)/shard_map/all_to_all | solution.py:311
  147.1 47.0 %copy-start.7 = (f32[32,128]{1,0:T(8,128)S(1)}, f32[32,128]{1,0:T(8,128)}, u32[]{:S(2)}) copy-start(f32[32,128]{1,0:T(8,128)} %param.10) | copy-start | bytes 49156
  147.1 52.2 %copy-start.4 = (f32[128]{0:T(128)S(1)}, f32[128]{0:T(128)}, u32[]{:S(2)}) copy-start(f32[128]{0:T(128)} %param.11) | copy-start | bytes 1540
  182.6 16.7 %collective-permute-start = (bf16[128,128]{1,0:T(8,128)(2,1)S(1)}, bf16[128,128]{1,0:T(8,128)(2,1)S(1)}, u32[]{:S(2)}, u32[]{:S(2)}) collective-permute-start(bf16[128,128]{1,0:T(8,128)(2,1)S(1)} %get-tuple-element.12), channel_id=1, source_target_pairs={{0,1},{1,2},{2,3},{3,4},{4,5},{5,6},{6,7},{8,9},{9,10},{10,11},{11... | collective-permute-start | bytes 98312 | tf_op jit(solution)/shard_map/ppermute | solution.py:299
  184.5 14.8 %collective-permute-start.1 = (bf16[128,128]{1,0:T(8,128)(2,1)S(1)}, bf16[128,128]{1,0:T(8,128)(2,1)S(1)}, u32[]{:S(2)}, u32[]{:S(2)}) collective-permute-start(bf16[128,128]{1,0:T(8,128)(2,1)S(1)} %get-tuple-element.11), channel_id=1, source_target_pairs={{1,0},{2,1},{3,2},{4,3},{5,4},{6,5},{7,6},{9,8},{10,9},{11,10},{12... | collective-permute-start | bytes 98312 | tf_op jit(solution)/shard_map/ppermute | solution.py:299
  188.2 6.0 %collective-permute-start.2 = (bf16[32,128]{1,0:T(8,128)(2,1)S(1)}, bf16[32,128]{1,0:T(8,128)(2,1)S(1)}, u32[]{:S(2)}, u32[]{:S(2)}) collective-permute-start(bf16[32,128]{1,0:T(8,128)(2,1)S(1)} %bitcast.28), channel_id=1, source_target_pairs={{0,8},{8,16},{16,24},{24,32},{32,40},{40,48},{48,56},{56,64},{64,7... | collective-permute-start | bytes 24584 | tf_op jit(solution)/shard_map/ppermute | solution.py:299
  191.7 7.7 %collective-permute-start.3 = (bf16[32,128]{1,0:T(8,128)(2,1)S(1)}, bf16[32,128]{1,0:T(8,128)(2,1)S(1)}, u32[]{:S(2)}, u32[]{:S(2)}) collective-permute-start(bf16[32,128]{1,0:T(8,128)(2,1)S(1)} %bitcast.29), channel_id=1, source_target_pairs={{8,0},{16,8},{24,16},{32,24},{40,32},{48,40},{56,48},{64,56},{72,6... | collective-permute-start | bytes 24584 | tf_op jit(solution)/shard_map/ppermute | solution.py:299

commit v2 on v1

v2 whole, which is shorter than its diff:
```python
import jax
import jax.numpy as jnp
from jax import lax
from jax.experimental import pallas as pl
from jax.experimental.pallas import tpu as pltpu
from jax.sharding import PartitionSpec as P

F32 = jnp.float32
BF16 = jnp.bfloat16
CAP = 512
META = 16
SEG = CAP + META
WIN = 16
GROUPS = 48
GROUP = 16


def iota(shape, dim):
    return lax.broadcasted_iota(jnp.int32, shape, dim)


def zero_one(mask):
    return jnp.where(mask, 1.0, 0.0).astype(BF16)


def dot(a, b):
    return lax.dot_general(a, b, (((1,), (0,)), ((), ())), preferred_element_type=F32)


def dot_nt(a, b):
    return lax.dot_general(a, b, (((1,), (1,)), ((), ())), preferred_element_type=F32)


def pack_kernel(
    nparts, me_ref, slots_hbm, hits_hbm, state_hbm, send_hbm, back_ref,
    slots_ref, hits_ref, state_ref, field, packed, send_ref, code_vmem, code_smem, sems, out_sems,
):
    nblocks, width = slots_ref.shape
    cells = state_ref.shape[0]
    rows_here = cells // width
    loads = [
        pltpu.make_async_copy(slots_hbm, slots_ref, sems.at[0]),
        pltpu.make_async_copy(hits_hbm, hits_ref, sems.at[1]),
        pltpu.make_async_copy(state_hbm, state_ref, sems.at[2]),
    ]
    for load in loads:
        load.start()
    before = zero_one(iota((width, width), 0) < iota((width, width), 1))
    both = jnp.concatenate([before, jnp.ones((width, width), BF16)], axis=1)
    earlier = zero_one(iota((nblocks, nblocks), 1) < iota((nblocks, nblocks), 0))
    starts = zero_one(iota((nblocks, width), 0) < iota((nblocks, width), 1))
    ones = jnp.ones((META, width), BF16)
    top = iota((META, width), 0) == 0
    loads[0].wait()
    loads[1].wait()
    slots = slots_ref[...]
    live = slots >= 0
    owner = jnp.where(live, (hits_ref[...] + me_ref[0]) & (nparts - 1), nparts)
    place = jnp.zeros((nblocks, width), F32)
    for part in range(nparts):
        mine = owner == part
        mask = zero_one(mine)
        ranks = dot(mask, both)
        offsets = dot(earlier, ranks[:, width:].astype(BF16))
        place = place + jnp.where(mine, ranks[:, :width] + offsets, 0.0)
        in_lanes = dot_nt(ones, mask).astype(BF16)
        begin = dot(in_lanes, starts)
        high = jnp.floor(begin * (1.0 / 16.0))
        send_ref[pl.ds(part * SEG + CAP, META), :] = jnp.where(
            top, high, begin - 16.0 * high
        ).astype(BF16)
    spot = owner * CAP + place.astype(jnp.int32)
    spot_high = (spot >> 7).astype(F32)
    spot_low = (spot & 127).astype(F32)
    cell_row = slots >> 7
    cell_col = slots & 127
    total = jnp.zeros((2 * rows_here, width), F32)
    row_ids = iota((rows_here, width), 0)
    col_ids = iota((width, width), 0)
    for pair in range(0, nblocks, 2):
        lhs, rhs = [], []
        for k in (pair, pair + 1):
            at_row = row_ids == cell_row[k : k + 1, :]
            lhs.append(
                jnp.concatenate(
                    [
                        jnp.where(at_row, spot_high[k : k + 1, :], 0.0),
                        jnp.where(at_row, spot_low[k : k + 1, :], 0.0),
                    ],
                    axis=0,
                ).astype(BF16)
            )
            rhs.append(zero_one(col_ids == cell_col[k : k + 1, :]))
        total = total + dot_nt(jnp.concatenate(lhs, axis=1), jnp.concatenate(rhs, axis=1))
    back = (total[:rows_here] * 128.0 + total[rows_here:]).astype(jnp.int32)
    back_ref[...] = back
    code_vmem[...] = back + (back >> 9) * META
    copy = pltpu.make_async_copy(code_vmem, code_smem, sems.at[3])
    copy.start()
    loads[2].wait()
    field[...] = state_ref[...].astype(F32)
    copy.wait()

    def line(i, _):
        for q in range(0, width, GROUP):
            values = [field[pl.ds(i * width + q + j, 1), :] for j in range(GROUP)]
            spots = [code_smem[i, q + j] for j in range(GROUP)]
            for value, at in zip(values, spots):
                packed[pl.ds(at, 1), :] = value
        return 0

    lax.fori_loop(0, rows_here, line, 0)
    stores = []
    for part in range(nparts):
        send_ref[pl.ds(part * SEG, CAP), :] = packed[pl.ds(part * SEG, CAP), :].astype(BF16)
        stores.append(
            pltpu.make_async_copy(
                send_ref.at[pl.ds(part * SEG, SEG), :],
                send_hbm.at[pl.ds(part * SEG, SEG), :],
                out_sems.at[part],
            )
        )
        stores[-1].start()
    for store in stores:
        store.wait()


def pack(me, slots, hits, flat, nparts):
    nblocks, width = slots.shape
    cells = flat.shape[0]
    return pl.pallas_call(
        lambda *refs: pack_kernel(nparts, *refs),
        out_shape=(
            jax.ShapeDtypeStruct((nparts * SEG, width), BF16),
            jax.ShapeDtypeStruct((cells // width, width), jnp.int32),
        ),
        in_specs=[pl.BlockSpec(memory_space=pltpu.SMEM)]
        + [pl.BlockSpec(memory_space=pltpu.HBM)] * 3,
        out_specs=[pl.BlockSpec(memory_space=pltpu.HBM), pl.BlockSpec(memory_space=pltpu.VMEM)],
        scratch_shapes=[
            pltpu.VMEM((nblocks, width), jnp.int32),
            pltpu.VMEM((nblocks, width), jnp.int32),
            pltpu.VMEM((cells, width), BF16),
            pltpu.VMEM((cells, width), F32),
            pltpu.VMEM((nparts * SEG, width), F32),
            pltpu.VMEM((nparts * SEG, width), BF16),
            pltpu.VMEM((cells // width, width), jnp.int32),
            pltpu.SMEM((cells // width, width), jnp.int32),
            pltpu.SemaphoreType.DMA((4,)),
            pltpu.SemaphoreType.DMA((nparts,)),
        ],
        compiler_params=pltpu.CompilerParams(vmem_limit_bytes=62 << 20),
    )(me, slots, hits, flat)


def react_kernel(
    nparts, nblocks, entries_ref, recv_ref, value_ref, base_ref, sens_ref, out_ref,
    rows, mapped, values, bases, begin_vmem, begin_smem, sem,
):
    width = recv_ref.shape[1]
    values[...] = value_ref[...].astype(F32)
    bases[...] = base_ref[...].astype(F32)
    for part in range(nparts):
        meta = recv_ref[pl.ds(part * SEG + CAP, META), :].astype(F32)
        begin_vmem[pl.ds(part, 1), :] = (meta[0:1] * 16.0 + meta[1:2]).astype(jnp.int32)
    copy = pltpu.make_async_copy(begin_vmem, begin_smem, sem)
    copy.start()

    def widen(part, _):
        at = pl.multiple_of(part * SEG, 16)
        rows[pl.ds(at, SEG), :] = recv_ref[pl.ds(at, SEG), :].astype(F32)
        return 0

    lax.fori_loop(0, nparts, widen, 0)
    copy.wait()
    zero = jnp.zeros((WIN, width), BF16)
    four = 4

    def delta(at, entry):
        base = bases[pl.ds(entry, 1), :]
        return (rows[pl.ds(at, WIN), :] - base).astype(BF16)

    def batch(part, first):
        begins = [begin_smem[part, first + i] for i in range(GROUPS + 1)]
        entry = [entries_ref[0, 0, part * nblocks + first + i] for i in range(GROUPS)]
        at = [part * SEG + begins[i] for i in range(GROUPS)]
        dx = [delta(at[i], entry[i]) for i in range(GROUPS)]
        results = []
        for i in range(0, GROUPS, four):
            lhs = jnp.concatenate(
                [
                    jnp.concatenate([dx[i], zero], axis=1),
                    jnp.concatenate([dx[i + 1], zero], axis=1),
                    jnp.concatenate([zero, dx[i + 2]], axis=1),
                    jnp.concatenate([zero, dx[i + 3]], axis=1),
                ],
                axis=0,
            )
            rhs = jnp.concatenate(
                [
                    jnp.concatenate([sens_ref[entry[i]], sens_ref[entry[i + 1]]], axis=1),
                    jnp.concatenate([sens_ref[entry[i + 2]], sens_ref[entry[i + 3]]], axis=1),
                ],
                axis=0,
            )
            product = dot(lhs, rhs)
            for j in range(four):
                half = (j % 2) * width
                results.append(
                    product[j * WIN : (j + 1) * WIN, half : half + width]
                    + values[pl.ds(entry[i + j], 1), :]
                )
        for i in range(GROUPS):
            mapped[pl.ds(at[i], WIN), :] = results[i]
        counts = [begins[i + 1] - begins[i] for i in range(GROUPS)]
        most = counts[0]
        for count in counts[1:]:
            most = jnp.maximum(most, count)

        @pl.when(most > WIN)
        def _():
            for i in range(GROUPS):

                def more(w, _, i=i):
                    here = at[i] + w * WIN
                    left = counts[i] - w * WIN
                    result = dot(delta(here, entry[i]), sens_ref[entry[i]])
                    result = result + values[pl.ds(entry[i], 1), :]
                    keep = iota((WIN, width), 0) < left
                    mapped[pl.ds(here, WIN), :] = jnp.where(
                        keep, result, mapped[pl.ds(here, WIN), :]
                    )
                    return 0

                lax.fori_loop(1, (counts[i] + (WIN - 1)) >> 4, more, 0)

    def source(part, _):
        def batches(step, _):
            batch(part, step * GROUPS)
            return 0

        return lax.fori_loop(0, nblocks // GROUPS, batches, 0)

    lax.fori_loop(0, nparts, source, 0)

    def narrow(part, _):
        out_ref[pl.ds(pl.multiple_of(part * CAP, 16), CAP), :] = mapped[
            pl.ds(pl.multiple_of(part * SEG, 16), CAP), :
        ].astype(BF16)
        return 0

    lax.fori_loop(0, nparts, narrow, 0)


def react(entries, recv, value, base, sens, nparts):
    width = recv.shape[1]
    nblocks = entries.shape[-1] // nparts
    return pl.pallas_call(
        lambda *refs: react_kernel(nparts, nblocks, *refs),
        out_shape=jax.ShapeDtypeStruct((nparts * CAP, width), BF16),
        in_specs=[pl.BlockSpec(memory_space=pltpu.SMEM)]
        + [pl.BlockSpec(memory_space=pltpu.VMEM)] * 4,
        out_specs=pl.BlockSpec(memory_space=pltpu.VMEM),
        scratch_shapes=[
            pltpu.VMEM((nparts * SEG, width), F32),
            pltpu.VMEM((nparts * SEG, width), F32),
            pltpu.VMEM(value.shape, F32),
            pltpu.VMEM(base.shape, F32),
            pltpu.VMEM((nparts, width), jnp.int32),
            pltpu.SMEM((nparts, width), jnp.int32),
            pltpu.SemaphoreType.DMA,
        ],
        compiler_params=pltpu.CompilerParams(vmem_limit_bytes=24 << 20),
    )(entries, recv, value, base, sens)


def unpack_kernel(code_ref, ret_ref, out_ref, rows):
    rows_here, width = code_ref.shape
    rows[...] = ret_ref[...].astype(F32)

    def line(i, _):
        for q in range(0, width, GROUP):
            spots = [code_ref[i, q + j] for j in range(GROUP)]
            values = [rows[pl.ds(at, 1), :] for at in spots]
            out_ref[pl.ds(pl.multiple_of(i * width + q, GROUP), GROUP), :] = jnp.concatenate(
                values, axis=0
            ).astype(BF16)
        return 0

    lax.fori_loop(0, rows_here, line, 0)


def unpack(code, ret, cells):
    width = ret.shape[1]
    return pl.pallas_call(
        unpack_kernel,
        out_shape=jax.ShapeDtypeStruct((cells, width), BF16),
        in_specs=[
            pl.BlockSpec(memory_space=pltpu.SMEM),
            pl.BlockSpec(memory_space=pltpu.VMEM),
        ],
        out_specs=pl.BlockSpec(memory_space=pltpu.VMEM),
        scratch_shapes=[pltpu.VMEM(ret.shape, F32)],
        compiler_params=pltpu.CompilerParams(vmem_limit_bytes=20 << 20),
    )(code, ret)


def transport_kernel(
    mid_ref, up_ref, down_ref, left_ref, right_ref, courant_ref, diffusion_ref, out_ref
):
    rows_here, cols, width = mid_ref.shape
    diffusion = diffusion_ref[...]
    first = iota((cols, width), 0) == 0
    last = iota((cols, width), 0) == cols - 1

    def row(i):
        if i < 0:
            return up_ref[...].astype(F32)
        if i >= rows_here:
            return down_ref[...].astype(F32)
        return mid_ref[i].astype(F32)

    above, here = row(-1), row(0)
    for i in range(rows_here):
        below = row(i + 1)
        left = jnp.where(first, left_ref[i : i + 1, :].astype(F32), pltpu.roll(here, 1, 0))
        right = jnp.where(
            last, right_ref[i : i + 1, :].astype(F32), pltpu.roll(here, cols - 1, 0)
        )
        courant = courant_ref[:, i : i + 1]
        out_ref[i] = (
            here
            - courant * (here - above)
            + diffusion * (above + below + left + right - 4.0 * here)
        )
        above, here = here, below


def transport(reacted, up, down, left, right, courant, diffusion):
    shape = reacted.shape
    return pl.pallas_call(
        transport_kernel,
        out_shape=jax.ShapeDtypeStruct(shape, F32),
        in_specs=[pl.BlockSpec(memory_space=pltpu.VMEM)] * 7,
        out_specs=pl.BlockSpec(memory_space=pltpu.VMEM),
        compiler_params=pltpu.CompilerParams(vmem_limit_bytes=20 << 20),
    )(reacted, up, down, left, right, courant, diffusion)


def shifted(block, axis, ahead):
    count = lax.axis_size(axis)
    forward = [(i, i + 1) for i in range(count - 1)]
    return lax.ppermute(block, axis, forward if ahead else [(j, i) for i, j in forward])


def local(
    state, courant, diffusion, table_value, table_base, table_sens, slot_cell, hit_step, entry_ids
):
    rows_here, cols_here, width = state.shape
    cells = rows_here * cols_here
    nparts = lax.axis_size("blk")
    me = lax.axis_index("blk").astype(jnp.int32).reshape(1)
    flat = state.reshape(cells, width)
    send, code = pack(me, slot_cell[0], hit_step[0], flat, nparts)
    recv = lax.all_to_all(send.reshape(nparts, SEG, width), "blk", 0, 0, tiled=True)
    done = react(
        entry_ids, recv.reshape(nparts * SEG, width),
        table_value, table_base, table_sens, nparts,
    )
    back = lax.all_to_all(done.reshape(nparts, CAP, width), "blk", 0, 0, tiled=True)
    reacted = unpack(code, back.reshape(nparts * CAP, width), cells)
    reacted = reacted.reshape(rows_here, cols_here, width)
    left = shifted(reacted[:, -1], "blk", True)
    right = shifted(reacted[:, 0], "blk", False)
    up = shifted(reacted[-1], "grid", True)
    down = shifted(reacted[0], "grid", False)
    return transport(
        reacted, up, down, left, right, courant.T, diffusion.reshape(1, width)
    )


def solution(mesh):
    return jax.shard_map(
        local,
        mesh=mesh,
        in_specs=(
            P("grid", "blk", None),
            P("grid", "blk"),
            P(),
            P("blk", None),
            P("blk", None),
            P("blk", None, None),
            P("grid", "blk", None),
            P("grid", "blk", None),
            P("blk", "grid", None),
        ),
        out_specs=P("grid", "blk", None),
        check_vma=False,
    )
```

time: 202 us -> 113 us (0.56)
  Pallas kernels: 110 us -> 25.6 us
  blocking collectives: 32.9 us -> 65.3 us
  waiting for transfers between devices: 34.4 us -> 5.59 us
  starting transfers between devices: 19.8 us -> 11.4 us
    all_to_all x0 -> x1, blocking collectives: none -> 35.6 us  [local(): lax.all_to_all(send.reshape(nparts, SEG, width), 'blk', 0, 0, tiled=True)]
    pallas_call x1, Pallas kernels: 35.4 us -> 4.74 us  [unpack(): pl.pallas_call(unpack_kernel, out_shape=jax.ShapeDtypeStruct((cells, widt...]
    all_to_all x1 -> x0, waiting for transfers between devices: 29.3 us -> none  [local(): lax.all_to_all(send.reshape(nparts, SEG, width), 'blk', 0, 0, tiled=True)]
    pallas_call x1, Pallas kernels: 37.9 us -> 10.3 us  [pack(): pl.pallas_call(lambda *refs: pack_kernel(nparts, *refs), out_shape=(jax.S...]
    pallas_call x1, Pallas kernels: 34.6 us -> 8.09 us  [react(): pl.pallas_call(lambda *refs: react_kernel(nparts, nblocks, *refs), out_sh...]
    all_to_all x1 -> x0, starting transfers between devices: 8.4 us -> none  [local(): lax.all_to_all(send.reshape(nparts, SEG, width), 'blk', 0, 0, tiled=True)]
    all_to_all x1, blocking collectives: 32.9 us -> 29.8 us  [local(): lax.all_to_all(done.reshape(nparts, CAP, width), 'blk', 0, 0, tiled=True)]
    unnamed x21 -> x17, local copies, waits for them, and re-layouts: 4.18 us -> 3.51 us
  transfers between devices with their start and end apart: 5 -> 4, of which waited for: 2 -> 1; matrix products, arithmetic and copies ran while one was open for 0% -> 0% of each run, Pallas kernels for 0% -> 0%
where the time goes in v2:
time: 113 us; the launch traced here: 112 us
  blocking collectives  65.3 us (58%)
  Pallas kernels  25.6 us (23%)
  starting transfers between devices  11.4 us (10%)
  waiting for transfers between devices  5.59 us (5%)
  local copies, waits for them, and re-layouts  3.55 us (3%)
    all_to_all x1, blocking collectives, local(): lax.all_to_all(send.reshape(nparts, SEG, width), 'blk', 0, 0, tiled=True)  35.6 us
    all_to_all x1, blocking collectives, local(): lax.all_to_all(done.reshape(nparts, CAP, width), 'blk', 0, 0, tiled=True)  29.8 us
    ppermute x4, starting transfers between devices, shifted(): lax.ppermute(block, axis, forward if ahead else [(j, i) for i, j in forwa...  11.4 us
    pallas_call x1, Pallas kernels, pack(): pl.pallas_call(lambda *refs: pack_kernel(nparts, *refs), out_shape=(jax.S...  10.3 us
    pallas_call x1, Pallas kernels, react(): pl.pallas_call(lambda *refs: react_kernel(nparts, nblocks, *refs), out_sh...  8.09 us
    ppermute x4, waiting for transfers between devices, shifted(): lax.ppermute(block, axis, forward if ahead else [(j, i) for i, j in forwa...  5.59 us
    pallas_call x1, Pallas kernels, unpack(): pl.pallas_call(unpack_kernel, out_shape=jax.ShapeDtypeStruct((cells, widt...  4.74 us
    unnamed x17, local copies, waits for them, and re-layouts  3.51 us
  transfers between devices with their start and end apart: 4, of which 1 were waited for; matrix products, arithmetic and copies ran while one was open for 0% of the time, Pallas kernels for 0%

profile of v2, /device:TPU:30, one launch (start us, length us, event | category | flops | bytes accessed | tf_op | source)
XLA Modules:
  0.0 111.6 jit_solution(6512779560467274485)
XLA Ops:
  0.0 10.3 %shard_map.91 = (bf16[8448,128]{1,0:T(8,128)(2,1)}, s32[32,128]{1,0:T(8,128)}) custom-call(s32[1]{0:T(128)} %bitcast.refs_0_, s32[48,128]{1,0:T(8,128)} %bitcast.26, s32[48,128]{1,0:T(8,128)} %bitcast.27, bf16[4096,128]{1,0:T(8,128)(2,1)} %bitcast.25), custom_call_target="tpu_custom_call" | custom-call | tf_op jit(solution)/shard_map/pallas_call | solution.py:131
  10.3 0.0 copy-start.1
  10.3 0.0 copy-start.2
  10.3 0.0 copy-start.4
  10.3 35.6 %all_to_all.10 = bf16[16,528,128]{2,1,0:T(8,128)(2,1)S(1)} all-to-all(bf16[16,528,128]{2,1,0:T(8,128)(2,1)} %bitcast.24), channel_id=1, replica_groups=mesh['blk'=16,'grid'=8] {'blk'}, dimensions={0} | all-to-all | bytes 4325376 | tf_op jit(solution)/shard_map/all_to_all | solution.py:365
  45.9 0.0 copy-done.1
  45.9 0.0 copy-done.2
  45.9 0.0 copy-done.4
  45.9 0.0 copy-start
  45.9 3.4 %copy-done = bf16[256,128,128]{2,1,0:T(8,128)(2,1)S(1)} copy-done((bf16[256,128,128]{2,1,0:T(8,128)(2,1)S(1)}, bf16[256,128,128]{2,1,0:T(8,128)(2,1)}, u32[]{:S(2)}) %copy-start) | copy-done | bytes 8388632
  49.3 8.1 %shard_map.92 = bf16[8192,128]{1,0:T(8,128)(2,1)S(1)} custom-call(s32[1,1,768]{2,1,0:T(1,128)S(1)} %copy-done.4, bf16[8448,128]{1,0:T(8,128)(2,1)S(1)} %bitcast.17, bf16[256,128]{1,0:T(8,128)(2,1)S(1)} %copy-done.1, bf16[256,128]{1,0:T(8,128)(2,1)S(1)} %copy-done.2, bf16[256,128,128]{2,1,0:T(8,128)(2,1)S(1)} %copy-done), custom_call_target="tpu_custom_call" | custom-call | tf_op jit(solution)/shard_map/pallas_call | solution.py:258
  57.4 0.0 copy-start.3
  57.4 29.8 %all_to_all.11 = bf16[16,512,128]{2,1,0:T(8,128)(2,1)S(1)} all-to-all(bf16[16,512,128]{2,1,0:T(8,128)(2,1)S(1)} %bitcast.19), channel_id=1, replica_groups=mesh['blk'=16,'grid'=8] {'blk'}, dimensions={0} | all-to-all | bytes 4194304 | tf_op jit(solution)/shard_map/all_to_all | solution.py:370
  87.1 0.0 copy-start.6
  87.1 0.0 copy-start.5
  87.1 0.0 copy-done.3
  87.1 4.7 %shard_map.93 = bf16[4096,128]{1,0:T(8,128)(2,1)S(1)} custom-call(s32[32,128]{1,0:T(8,128)S(1)} %copy-done.3, bf16[8192,128]{1,0:T(8,128)(2,1)S(1)} %bitcast.18), custom_call_target="tpu_custom_call" | custom-call | tf_op jit(solution)/shard_map/pallas_call | solution.py:295
  91.9 1.9 %collective-permute-start = (bf16[128,128]{1,0:T(8,128)(2,1)S(1)}, bf16[128,128]{1,0:T(8,128)(2,1)S(1)}, u32[]{:S(2)}, u32[]{:S(2)}) collective-permute-start(bf16[128,128]{1,0:T(8,128)(2,1)S(1)} %get-tuple-element.12), channel_id=1, source_target_pairs={{0,1},{1,2},{2,3},{3,4},{4,5},{5,6},{6,7},{8,9},{9,10},{10,11},{11... | collective-permute-start | bytes 98312 | tf_op jit(solution)/shard_map/ppermute | solution.py:353
  93.8 3.6 %collective-permute-start.1 = (bf16[128,128]{1,0:T(8,128)(2,1)S(1)}, bf16[128,128]{1,0:T(8,128)(2,1)S(1)}, u32[]{:S(2)}, u32[]{:S(2)}) collective-permute-start(bf16[128,128]{1,0:T(8,128)(2,1)S(1)} %get-tuple-element.11), channel_id=1, source_target_pairs={{1,0},{2,1},{3,2},{4,3},{5,4},{6,5},{7,6},{9,8},{10,9},{11,10},{12... | collective-permute-start | bytes 98312 | tf_op jit(solution)/shard_map/ppermute | solution.py:353
  97.5 3.9 %collective-permute-start.2 = (bf16[32,128]{1,0:T(8,128)(2,1)S(1)}, bf16[32,128]{1,0:T(8,128)(2,1)S(1)}, u32[]{:S(2)}, u32[]{:S(2)}) collective-permute-start(bf16[32,128]{1,0:T(8,128)(2,1)S(1)} %bitcast.28), channel_id=1, source_target_pairs={{0,8},{8,16},{16,24},{24,32},{32,40},{40,48},{48,56},{56,64},{64,7... | collective-permute-start | bytes 24584 | tf_op jit(solution)/shard_map/ppermute | solution.py:353
  101.4 1.9 %collective-permute-start.3 = (bf16[32,128]{1,0:T(8,128)(2,1)S(1)}, bf16[32,128]{1,0:T(8,128)(2,1)S(1)}, u32[]{:S(2)}, u32[]{:S(2)}) collective-permute-start(bf16[32,128]{1,0:T(8,128)(2,1)S(1)} %bitcast.29), channel_id=1, source_target_pairs={{8,0},{16,8},{24,16},{32,24},{40,32},{48,40},{56,48},{64,56},{72,6... | collective-permute-start | bytes 24584 | tf_op jit(solution)/shard_map/ppermute | solution.py:353
  103.4 0.0 copy-done.6
  103.4 0.1 copy.14
  103.5 0.0 collective-permute-done.2.left_ref
  103.5 5.6 %collective-permute-done.3.right_ref = bf16[32,128]{1,0:T(8,128)(2,1)S(1)} collective-permute-done((bf16[32,128]{1,0:T(8,128)(2,1)S(1)}, bf16[32,128]{1,0:T(8,128)(2,1)S(1)}, u32[]{:S(2)}, u32[]{:S(2)}) %collective-permute-start.3) | collective-permute-done | bytes 8224 | tf_op jit(solution)/shard_map/ppermute | solution.py:353
  109.1 0.0 collective-permute-done.up_ref
  109.1 0.0 collective-permute-done.1.down_ref
  109.1 0.0 copy-done.5
  109.1 2.5 %shard_map.94 = f32[32,128,128]{2,1,0:T(8,128)} custom-call(bf16[32,128,128]{2,1,0:T(8,128)(2,1)S(1)} %bitcast.21, bf16[128,128]{1,0:T(8,128)(2,1)S(1)} %collective-permute-done.up_ref, bf16[128,128]{1,0:T(8,128)(2,1)S(1)} %collective-permute-done.1.down_ref, bf16[32,128]{1,0:T(8,128)(2,1)S(1)} %collective-permute-done.2.left_ref, ...), custom_call_target="tpu_custom_call" | custom-call | tf_op jit(solution)/shard_map/pallas_call | solution.py:341
  (4 shorter events, 0.0 us)
Async XLA Ops:
  10.3 35.6 %copy-start.1 = (bf16[256,128]{1,0:T(8,128)(2,1)S(1)}, bf16[256,128]{1,0:T(8,128)(2,1)}, u32[]{:S(2)}) copy-start(bf16[256,128]{1,0:T(8,128)(2,1)} %refs_2_.1) | copy-start | bytes 196612
  10.3 35.6 %copy-start.2 = (bf16[256,128]{1,0:T(8,128)(2,1)S(1)}, bf16[256,128]{1,0:T(8,128)(2,1)}, u32[]{:S(2)}) copy-start(bf16[256,128]{1,0:T(8,128)(2,1)} %refs_3_.1) | copy-start | bytes 196612
  10.3 35.6 %copy-start.4 = (s32[1,1,768]{2,1,0:T(1,128)S(1)}, s32[1,1,768]{2,1,0:T(1,128)}, u32[]{:S(2)}) copy-start(s32[1,1,768]{2,1,0:T(1,128)} %refs_0_.1) | copy-start | bytes 9220
  45.9 3.4 %copy-start = (bf16[256,128,128]{2,1,0:T(8,128)(2,1)S(1)}, bf16[256,128,128]{2,1,0:T(8,128)(2,1)}, u32[]{:S(2)}) copy-start(bf16[256,128,128]{2,1,0:T(8,128)(2,1)} %refs_4_.1) | copy-start | bytes 25165828
  57.4 29.8 %copy-start.3 = (s32[32,128]{1,0:T(8,128)S(1)}, s32[32,128]{1,0:T(8,128)}, u32[]{:S(2)}) copy-start(s32[32,128]{1,0:T(8,128)} %get-tuple-element.7.code_ref) | copy-start | bytes 49156
  87.1 16.3 %copy-start.6 = (f32[32,128]{1,0:T(8,128)S(1)}, f32[32,128]{1,0:T(8,128)}, u32[]{:S(2)}) copy-start(f32[32,128]{1,0:T(8,128)} %param.10) | copy-start | bytes 49156
  87.1 22.0 %copy-start.5 = (f32[128]{0:T(128)S(1)}, f32[128]{0:T(128)}, u32[]{:S(2)}) copy-start(f32[128]{0:T(128)} %param.11) | copy-start | bytes 1540
  91.9 17.2 %collective-permute-start = (bf16[128,128]{1,0:T(8,128)(2,1)S(1)}, bf16[128,128]{1,0:T(8,128)(2,1)S(1)}, u32[]{:S(2)}, u32[]{:S(2)}) collective-permute-start(bf16[128,128]{1,0:T(8,128)(2,1)S(1)} %get-tuple-element.12), channel_id=1, source_target_pairs={{0,1},{1,2},{2,3},{3,4},{4,5},{5,6},{6,7},{8,9},{9,10},{10,11},{11... | collective-permute-start | bytes 98312 | tf_op jit(solution)/shard_map/ppermute | solution.py:353
  93.8 15.3 %collective-permute-start.1 = (bf16[128,128]{1,0:T(8,128)(2,1)S(1)}, bf16[128,128]{1,0:T(8,128)(2,1)S(1)}, u32[]{:S(2)}, u32[]{:S(2)}) collective-permute-start(bf16[128,128]{1,0:T(8,128)(2,1)S(1)} %get-tuple-element.11), channel_id=1, source_target_pairs={{1,0},{2,1},{3,2},{4,3},{5,4},{6,5},{7,6},{9,8},{10,9},{11,10},{12... | collective-permute-start | bytes 98312 | tf_op jit(solution)/shard_map/ppermute | solution.py:353
  97.5 6.0 %collective-permute-start.2 = (bf16[32,128]{1,0:T(8,128)(2,1)S(1)}, bf16[32,128]{1,0:T(8,128)(2,1)S(1)}, u32[]{:S(2)}, u32[]{:S(2)}) collective-permute-start(bf16[32,128]{1,0:T(8,128)(2,1)S(1)} %bitcast.28), channel_id=1, source_target_pairs={{0,8},{8,16},{16,24},{24,32},{32,40},{40,48},{48,56},{56,64},{64,7... | collective-permute-start | bytes 24584 | tf_op jit(solution)/shard_map/ppermute | solution.py:353
  101.4 7.7 %collective-permute-start.3 = (bf16[32,128]{1,0:T(8,128)(2,1)S(1)}, bf16[32,128]{1,0:T(8,128)(2,1)S(1)}, u32[]{:S(2)}, u32[]{:S(2)}) collective-permute-start(bf16[32,128]{1,0:T(8,128)(2,1)S(1)} %bitcast.29), channel_id=1, source_target_pairs={{8,0},{16,8},{24,16},{32,24},{40,32},{48,40},{56,48},{64,56},{72,6... | collective-permute-start | bytes 24584 | tf_op jit(solution)/shard_map/ppermute | solution.py:353

commit v3 on v2

--- a/solution.py
+++ b/solution.py
@@ -12,6 +12,7 @@
 SEG = CAP + META
 WIN = 16
 GROUPS = 48
+LINES = 4
 GROUP = 16
 
 
@@ -46,9 +47,8 @@
     for load in loads:
         load.start()
     before = zero_one(iota((width, width), 0) < iota((width, width), 1))
-    both = jnp.concatenate([before, jnp.ones((width, width), BF16)], axis=1)
-    earlier = zero_one(iota((nblocks, nblocks), 1) < iota((nblocks, nblocks), 0))
-    starts = zero_one(iota((nblocks, width), 0) < iota((nblocks, width), 1))
+    weights = jnp.concatenate([jnp.ones((width, width), BF16), before], axis=0)
+    earlier = zero_one(iota((width, nblocks), 1) < iota((width, nblocks), 0))
     ones = jnp.ones((META, width), BF16)
     top = iota((META, width), 0) == 0
     loads[0].wait()
@@ -56,15 +56,20 @@
     slots = slots_ref[...]
     live = slots >= 0
     owner = jnp.where(live, (hits_ref[...] + me_ref[0]) & (nparts - 1), nparts)
+    mine = [owner == part for part in range(nparts)]
+    masks = [zero_one(each) for each in mine]
+    ahead = [dot(earlier, mask).astype(BF16) for mask in masks]
+    ranks = dot(
+        jnp.concatenate(
+            [jnp.concatenate([a[:nblocks], m], axis=1) for a, m in zip(ahead, masks)], axis=0
+        ),
+        weights,
+    )
+    begins = dot_nt(ones, jnp.concatenate(ahead, axis=0))
     place = jnp.zeros((nblocks, width), F32)
     for part in range(nparts):
-        mine = owner == part
-        mask = zero_one(mine)
-        ranks = dot(mask, both)
-        offsets = dot(earlier, ranks[:, width:].astype(BF16))
-        place = place + jnp.where(mine, ranks[:, :width] + offsets, 0.0)
-        in_lanes = dot_nt(ones, mask).astype(BF16)
-        begin = dot(in_lanes, starts)
+        place = place + jnp.where(mine[part], ranks[part * nblocks : (part + 1) * nblocks], 0.0)
+        begin = begins[:, part * width : (part + 1) * width]
         high = jnp.floor(begin * (1.0 / 16.0))
         send_ref[pl.ds(part * SEG + CAP, META), :] = jnp.where(
             top, high, begin - 16.0 * high
@@ -274,6 +279,39 @@
     )(entries, recv, value, base, sens)
 
 
+def edges_kernel(code_ref, ret_ref, up_ref, down_ref, left_ref, right_ref, rows):
+    rows_here, width = code_ref.shape
+    cols_here = width
+    rows[...] = ret_ref[...].astype(F32)
+
+    def gather(out, spots):
+        for first in range(0, len(spots), GROUP):
+            out[pl.ds(first, GROUP), :] = jnp.concatenate(
+                [rows[pl.ds(at, 1), :] for at in spots[first : first + GROUP]], axis=0
+            ).astype(BF16)
+
+    gather(up_ref, [code_ref[rows_here - 1, j] for j in range(cols_here)])
+    gather(down_ref, [code_ref[0, j] for j in range(cols_here)])
+    gather(left_ref, [code_ref[i, cols_here - 1] for i in range(rows_here)])
+    gather(right_ref, [code_ref[i, 0] for i in range(rows_here)])
+
+
+def edges(code, ret):
+    rows_here, width = code.shape
+    ends = [rows_here if side else width for side in (0, 0, 1, 1)]
+    return pl.pallas_call(
+        edges_kernel,
+        out_shape=[jax.ShapeDtypeStruct((end, width), BF16) for end in ends],
+        in_specs=[
+            pl.BlockSpec(memory_space=pltpu.SMEM),
+            pl.BlockSpec(memory_space=pltpu.VMEM),
+        ],
+        out_specs=[pl.BlockSpec(memory_space=pltpu.VMEM)] * 4,
+        scratch_shapes=[pltpu.VMEM(ret.shape, F32)],
+        compiler_params=pltpu.CompilerParams(vmem_limit_bytes=20 << 20),
+    )(code, ret)
+
+
 def unpack_kernel(code_ref, ret_ref, out_ref, rows):
     rows_here, width = code_ref.shape
     rows[...] = ret_ref[...].astype(F32)
@@ -282,19 +320,18 @@
         for q in range(0, width, GROUP):
             spots = [code_ref[i, q + j] for j in range(GROUP)]
             values = [rows[pl.ds(at, 1), :] for at in spots]
-            out_ref[pl.ds(pl.multiple_of(i * width + q, GROUP), GROUP), :] = jnp.concatenate(
-                values, axis=0
-            ).astype(BF16)
+            for j, value in enumerate(values):
+                out_ref[pl.ds(i * width + q + j, 1), :] = value
         return 0
 
     lax.fori_loop(0, rows_here, line, 0)
 
 
-def unpack(code, ret, cells):
-    width = ret.shape[1]
+def unpack(code, ret):
+    cells, width = code.size, ret.shape[1]
     return pl.pallas_call(
         unpack_kernel,
-        out_shape=jax.ShapeDtypeStruct((cells, width), BF16),
+        out_shape=jax.ShapeDtypeStruct((cells, width), F32),
         in_specs=[
             pl.BlockSpec(memory_space=pltpu.SMEM),
             pl.BlockSpec(memory_space=pltpu.VMEM),
@@ -302,11 +339,13 @@
         out_specs=pl.BlockSpec(memory_space=pltpu.VMEM),
         scratch_shapes=[pltpu.VMEM(ret.shape, F32)],
         compiler_params=pltpu.CompilerParams(vmem_limit_bytes=20 << 20),
+        cost_estimate=pl.CostEstimate(flops=0, bytes_accessed=16 << 20, transcendentals=0),
     )(code, ret)
 
 
 def transport_kernel(
-    mid_ref, up_ref, down_ref, left_ref, right_ref, courant_ref, diffusion_ref, out_ref
+    mid_ref, up_ref, down_ref, left_ref, right_ref, courant_ref, diffusion_ref, out_hbm,
+    out_ref, sems,
 ):
     rows_here, cols, width = mid_ref.shape
     diffusion = diffusion_ref[...]
@@ -318,8 +357,9 @@
             return up_ref[...].astype(F32)
         if i >= rows_here:
             return down_ref[...].astype(F32)
-        return mid_ref[i].astype(F32)
-
+        return mid_ref[i]
+
+    stores = []
     above, here = row(-1), row(0)
     for i in range(rows_here):
         below = row(i + 1)
@@ -334,6 +374,14 @@
             + diffusion * (above + below + left + right - 4.0 * here)
         )
         above, here = here, below
+        if i % LINES == LINES - 1:
+            piece = pl.ds(i + 1 - LINES, LINES)
+            stores.append(
+                pltpu.make_async_copy(out_ref.at[piece], out_hbm.at[piece], sems.at[i // LINES])
+            )
+            stores[-1].start()
+    for store in stores:
+        store.wait()
 
 
 def transport(reacted, up, down, left, right, courant, diffusion):
@@ -342,7 +390,11 @@
         transport_kernel,
         out_shape=jax.ShapeDtypeStruct(shape, F32),
         in_specs=[pl.BlockSpec(memory_space=pltpu.VMEM)] * 7,
-        out_specs=pl.BlockSpec(memory_space=pltpu.VMEM),
+        out_specs=pl.BlockSpec(memory_space=pl.ANY),
+        scratch_shapes=[
+            pltpu.VMEM(shape, F32),
+            pltpu.SemaphoreType.DMA((shape[0] // LINES,)),
+        ],
         compiler_params=pltpu.CompilerParams(vmem_limit_bytes=20 << 20),
     )(reacted, up, down, left, right, courant, diffusion)
 
@@ -368,12 +420,13 @@
         table_value, table_base, table_sens, nparts,
     )
     back = lax.all_to_all(done.reshape(nparts, CAP, width), "blk", 0, 0, tiled=True)
-    reacted = unpack(code, back.reshape(nparts * CAP, width), cells)
-    reacted = reacted.reshape(rows_here, cols_here, width)
-    left = shifted(reacted[:, -1], "blk", True)
-    right = shifted(reacted[:, 0], "blk", False)
-    up = shifted(reacted[-1], "grid", True)
-    down = shifted(reacted[0], "grid", False)
+    back = back.reshape(nparts * CAP, width)
+    last_line, first_line, last_column, first_column = edges(code, back)
+    up = shifted(last_line, "grid", True)
+    down = shifted(first_line, "grid", False)
+    left = shifted(last_column, "blk", True)
+    right = shifted(first_column, "blk", False)
+    reacted = unpack(code, back).reshape(rows_here, cols_here, width)
     return transport(
         reacted, up, down, left, right, courant.T, diffusion.reshape(1, width)
     )

time: 113 us -> 108 us (0.956)
  waiting for transfers between devices: 5.59 us -> 1.12 us
  Pallas kernels: 25.6 us -> 23.6 us
    ppermute x4, waiting for transfers between devices: 5.59 us -> 1.12 us  [shifted(): lax.ppermute(block, axis, forward if ahead else [(j, i) for i, j in forwa...]
    pallas_call x1, Pallas kernels: 10.3 us -> 8.4 us  [pack(): pl.pallas_call(lambda *refs: pack_kernel(nparts, *refs), out_shape=(jax.S...]
    pallas_call x0 -> x1, Pallas kernels: none -> 1.31 us  [edges(): pl.pallas_call(edges_kernel, out_shape=[jax.ShapeDtypeStruct((end, width)...]
    all_to_all x1, blocking collectives: 29.8 us -> 30.9 us  [local(): lax.all_to_all(done.reshape(nparts, CAP, width), 'blk', 0, 0, tiled=True)]
    unnamed x17 -> x15, local copies, waits for them, and re-layouts: 3.51 us -> 3.51 us
  transfers between devices with their start and end apart: 4 -> 4, of which waited for: 1 -> 1; matrix products, arithmetic and copies ran while one was open for 0% -> 0% of each run, Pallas kernels for 0% -> 4%
where the time goes in v3:
time: 108 us; the launch traced here: 106 us
  blocking collectives  66.4 us (61%)
  Pallas kernels  23.6 us (22%)
  starting transfers between devices  11.4 us (11%)
  local copies, waits for them, and re-layouts  3.51 us (3%)
  waiting for transfers between devices  1.12 us (1%)
    all_to_all x1, blocking collectives, local(): lax.all_to_all(send.reshape(nparts, SEG, width), 'blk', 0, 0, tiled=True)  35.5 us
    all_to_all x1, blocking collectives, local(): lax.all_to_all(done.reshape(nparts, CAP, width), 'blk', 0, 0, tiled=True)  30.9 us
    ppermute x4, starting transfers between devices, shifted(): lax.ppermute(block, axis, forward if ahead else [(j, i) for i, j in forwa...  11.4 us
    pallas_call x1, Pallas kernels, pack(): pl.pallas_call(lambda *refs: pack_kernel(nparts, *refs), out_shape=(jax.S...  8.4 us
    pallas_call x1, Pallas kernels, react(): pl.pallas_call(lambda *refs: react_kernel(nparts, nblocks, *refs), out_sh...  7.6 us
    pallas_call x1, Pallas kernels, unpack(): pl.pallas_call(unpack_kernel, out_shape=jax.ShapeDtypeStruct((cells, widt...  4.44 us
    unnamed x15, local copies, waits for them, and re-layouts  3.51 us
  transfers between devices with their start and end apart: 4, of which 1 were waited for; matrix products, arithmetic and copies ran while one was open for 0% of the time, Pallas kernels for 4%

profile of v3, /device:TPU:30, one launch (start us, length us, event | category | flops | bytes accessed | tf_op | source)
XLA Modules:
  0.0 106.2 jit_solution(13293115413870815693)
XLA Ops:
  0.0 8.4 %shard_map.91 = (bf16[8448,128]{1,0:T(8,128)(2,1)}, s32[32,128]{1,0:T(8,128)}) custom-call(s32[1]{0:T(128)} %bitcast.refs_0_, s32[48,128]{1,0:T(8,128)} %bitcast.20, s32[48,128]{1,0:T(8,128)} %bitcast.21, bf16[4096,128]{1,0:T(8,128)(2,1)} %bitcast.19), custom_call_target="tpu_custom_call" | custom-call | tf_op jit(solution)/shard_map/pallas_call | solution.py:136
  8.4 0.0 copy-start.1
  8.4 0.0 copy-start.2
  8.4 0.0 copy-start.4
  8.4 35.5 %all_to_all.10 = bf16[16,528,128]{2,1,0:T(8,128)(2,1)S(1)} all-to-all(bf16[16,528,128]{2,1,0:T(8,128)(2,1)} %bitcast.18), channel_id=1, replica_groups=mesh['blk'=16,'grid'=8] {'blk'}, dimensions={0} | all-to-all | bytes 4325376 | tf_op jit(solution)/shard_map/all_to_all | solution.py:417
  44.0 0.0 copy-done.1
  44.0 0.0 copy-done.2
  44.0 0.0 copy-done.4
  44.0 0.0 copy-start
  44.0 3.4 %copy-done = bf16[256,128,128]{2,1,0:T(8,128)(2,1)S(1)} copy-done((bf16[256,128,128]{2,1,0:T(8,128)(2,1)S(1)}, bf16[256,128,128]{2,1,0:T(8,128)(2,1)}, u32[]{:S(2)}) %copy-start) | copy-done | bytes 8388632
  47.4 7.6 %shard_map.92 = bf16[8192,128]{1,0:T(8,128)(2,1)S(1)} custom-call(s32[1,1,768]{2,1,0:T(1,128)S(1)} %copy-done.4, bf16[8448,128]{1,0:T(8,128)(2,1)S(1)} %bitcast.13, bf16[256,128]{1,0:T(8,128)(2,1)S(1)} %copy-done.1, bf16[256,128]{1,0:T(8,128)(2,1)S(1)} %copy-done.2, bf16[256,128,128]{2,1,0:T(8,128)(2,1)S(1)} %copy-done), custom_call_target="tpu_custom_call" | custom-call | tf_op jit(solution)/shard_map/pallas_call | solution.py:263
  55.0 0.0 copy-start.3
  55.0 30.9 %all_to_all.11 = bf16[16,512,128]{2,1,0:T(8,128)(2,1)S(1)} all-to-all(bf16[16,512,128]{2,1,0:T(8,128)(2,1)S(1)} %bitcast.15), channel_id=1, replica_groups=mesh['blk'=16,'grid'=8] {'blk'}, dimensions={0} | all-to-all | bytes 4194304 | tf_op jit(solution)/shard_map/all_to_all | solution.py:422
  85.9 0.0 copy-start.6
  85.9 0.0 copy-done.3
  85.9 1.3 %shard_map.94 = (bf16[128,128]{1,0:T(8,128)(2,1)S(1)}, bf16[128,128]{1,0:T(8,128)(2,1)S(1)}, bf16[32,128]{1,0:T(8,128)(2,1)S(1)}, bf16[32,128]{1,0:T(8,128)(2,1)S(1)}) custom-call(s32[32,128]{1,0:T(8,128)S(1)} %copy-done.3, bf16[8192,128]{1,0:T(8,128)(2,1)S(1)} %bitcast.11), custom_call_target="tpu_custom_call" | custom-call | tf_op jit(solution)/shard_map/pallas_call | solution.py:302
  87.2 1.9 %collective-permute-start = (bf16[128,128]{1,0:T(8,128)(2,1)S(1)}, bf16[128,128]{1,0:T(8,128)(2,1)S(1)}, u32[]{:S(2)}, u32[]{:S(2)}) collective-permute-start(bf16[128,128]{1,0:T(8,128)(2,1)S(1)} %get-tuple-element.13), channel_id=1, source_target_pairs={{0,1},{1,2},{2,3},{3,4},{4,5},{5,6},{6,7},{8,9},{9,10},{10,11},{11... | collective-permute-start | bytes 98312 | tf_op jit(solution)/shard_map/ppermute | solution.py:405
  89.2 3.6 %collective-permute-start.1 = (bf16[128,128]{1,0:T(8,128)(2,1)S(1)}, bf16[128,128]{1,0:T(8,128)(2,1)S(1)}, u32[]{:S(2)}, u32[]{:S(2)}) collective-permute-start(bf16[128,128]{1,0:T(8,128)(2,1)S(1)} %get-tuple-element.14), channel_id=1, source_target_pairs={{1,0},{2,1},{3,2},{4,3},{5,4},{6,5},{7,6},{9,8},{10,9},{11,10},{12... | collective-permute-start | bytes 98312 | tf_op jit(solution)/shard_map/ppermute | solution.py:405
  92.8 3.9 %collective-permute-start.2 = (bf16[32,128]{1,0:T(8,128)(2,1)S(1)}, bf16[32,128]{1,0:T(8,128)(2,1)S(1)}, u32[]{:S(2)}, u32[]{:S(2)}) collective-permute-start(bf16[32,128]{1,0:T(8,128)(2,1)S(1)} %get-tuple-element.15), channel_id=1, source_target_pairs={{0,8},{8,16},{16,24},{24,32},{32,40},{40,48},{48,56},{56,64},{64,7... | collective-permute-start | bytes 24584 | tf_op jit(solution)/shard_map/ppermute | solution.py:405
  96.7 2.0 %collective-permute-start.3 = (bf16[32,128]{1,0:T(8,128)(2,1)S(1)}, bf16[32,128]{1,0:T(8,128)(2,1)S(1)}, u32[]{:S(2)}, u32[]{:S(2)}) collective-permute-start(bf16[32,128]{1,0:T(8,128)(2,1)S(1)} %get-tuple-element.16), channel_id=1, source_target_pairs={{8,0},{16,8},{24,16},{32,24},{40,32},{48,40},{56,48},{64,56},{72,6... | collective-permute-start | bytes 24584 | tf_op jit(solution)/shard_map/ppermute | solution.py:405
  98.7 0.0 copy-done.6
  98.7 0.1 copy.10
  98.8 0.0 copy-start.5
  98.8 4.4 %shard_map.93 = f32[4096,128]{1,0:T(8,128)S(1)} custom-call(s32[32,128]{1,0:T(8,128)S(1)} %copy-done.3, bf16[8192,128]{1,0:T(8,128)(2,1)S(1)} %bitcast.12), custom_call_target="tpu_custom_call" | custom-call | bytes 16777216 | tf_op jit(solution)/shard_map/pallas_call | solution.py:332
  103.2 0.0 collective-permute-done.2.left_ref
  103.2 1.1 %collective-permute-done.3.right_ref = bf16[32,128]{1,0:T(8,128)(2,1)S(1)} collective-permute-done((bf16[32,128]{1,0:T(8,128)(2,1)S(1)}, bf16[32,128]{1,0:T(8,128)(2,1)S(1)}, u32[]{:S(2)}, u32[]{:S(2)}) %collective-permute-start.3) | collective-permute-done | bytes 8224 | tf_op jit(solution)/shard_map/ppermute | solution.py:405
  104.4 0.0 collective-permute-done.up_ref
  104.4 0.0 collective-permute-done.1.down_ref
  104.4 0.0 copy-done.5
  104.4 1.8 %shard_map.95 = f32[32,128,128]{2,1,0:T(8,128)} custom-call(f32[32,128,128]{2,1,0:T(8,128)S(1)} %bitcast.14, bf16[128,128]{1,0:T(8,128)(2,1)S(1)} %collective-permute-done.up_ref, bf16[128,128]{1,0:T(8,128)(2,1)S(1)} %collective-permute-done.1.down_ref, bf16[32,128]{1,0:T(8,128)(2,1)S(1)} %collective-permute-done.2.left_ref, ...), custom_call_target="tpu_custom_call" | custom-call | tf_op jit(solution)/shard_map/pallas_call | solution.py:389
Async XLA Ops:
  8.4 35.6 %copy-start.1 = (bf16[256,128]{1,0:T(8,128)(2,1)S(1)}, bf16[256,128]{1,0:T(8,128)(2,1)}, u32[]{:S(2)}) copy-start(bf16[256,128]{1,0:T(8,128)(2,1)} %refs_2_.1) | copy-start | bytes 196612
  8.4 35.6 %copy-start.2 = (bf16[256,128]{1,0:T(8,128)(2,1)S(1)}, bf16[256,128]{1,0:T(8,128)(2,1)}, u32[]{:S(2)}) copy-start(bf16[256,128]{1,0:T(8,128)(2,1)} %refs_3_.1) | copy-start | bytes 196612
  8.4 35.6 %copy-start.4 = (s32[1,1,768]{2,1,0:T(1,128)S(1)}, s32[1,1,768]{2,1,0:T(1,128)}, u32[]{:S(2)}) copy-start(s32[1,1,768]{2,1,0:T(1,128)} %refs_0_.1) | copy-start | bytes 9220
  44.0 3.4 %copy-start = (bf16[256,128,128]{2,1,0:T(8,128)(2,1)S(1)}, bf16[256,128,128]{2,1,0:T(8,128)(2,1)}, u32[]{:S(2)}) copy-start(bf16[256,128,128]{2,1,0:T(8,128)(2,1)} %refs_4_.1) | copy-start | bytes 25165828
  55.0 30.9 %copy-start.3 = (s32[32,128]{1,0:T(8,128)S(1)}, s32[32,128]{1,0:T(8,128)}, u32[]{:S(2)}) copy-start(s32[32,128]{1,0:T(8,128)} %get-tuple-element.11.code_ref) | copy-start | bytes 49156
  85.9 12.8 %copy-start.6 = (f32[32,128]{1,0:T(8,128)S(1)}, f32[32,128]{1,0:T(8,128)}, u32[]{:S(2)}) copy-start(f32[32,128]{1,0:T(8,128)} %param.10) | copy-start | bytes 49156
  87.2 17.1 %collective-permute-start = (bf16[128,128]{1,0:T(8,128)(2,1)S(1)}, bf16[128,128]{1,0:T(8,128)(2,1)S(1)}, u32[]{:S(2)}, u32[]{:S(2)}) collective-permute-start(bf16[128,128]{1,0:T(8,128)(2,1)S(1)} %get-tuple-element.13), channel_id=1, source_target_pairs={{0,1},{1,2},{2,3},{3,4},{4,5},{5,6},{6,7},{8,9},{9,10},{10,11},{11... | collective-permute-start | bytes 98312 | tf_op jit(solution)/shard_map/ppermute | solution.py:405
  89.2 15.2 %collective-permute-start.1 = (bf16[128,128]{1,0:T(8,128)(2,1)S(1)}, bf16[128,128]{1,0:T(8,128)(2,1)S(1)}, u32[]{:S(2)}, u32[]{:S(2)}) collective-permute-start(bf16[128,128]{1,0:T(8,128)(2,1)S(1)} %get-tuple-element.14), channel_id=1, source_target_pairs={{1,0},{2,1},{3,2},{4,3},{5,4},{6,5},{7,6},{9,8},{10,9},{11,10},{12... | collective-permute-start | bytes 98312 | tf_op jit(solution)/shard_map/ppermute | solution.py:405
  92.8 10.4 %collective-permute-start.2 = (bf16[32,128]{1,0:T(8,128)(2,1)S(1)}, bf16[32,128]{1,0:T(8,128)(2,1)S(1)}, u32[]{:S(2)}, u32[]{:S(2)}) collective-permute-start(bf16[32,128]{1,0:T(8,128)(2,1)S(1)} %get-tuple-element.15), channel_id=1, source_target_pairs={{0,8},{8,16},{16,24},{24,32},{32,40},{40,48},{48,56},{56,64},{64,7... | collective-permute-start | bytes 24584 | tf_op jit(solution)/shard_map/ppermute | solution.py:405
  96.7 7.7 %collective-permute-start.3 = (bf16[32,128]{1,0:T(8,128)(2,1)S(1)}, bf16[32,128]{1,0:T(8,128)(2,1)S(1)}, u32[]{:S(2)}, u32[]{:S(2)}) collective-permute-start(bf16[32,128]{1,0:T(8,128)(2,1)S(1)} %get-tuple-element.16), channel_id=1, source_target_pairs={{8,0},{16,8},{24,16},{32,24},{40,32},{48,40},{56,48},{64,56},{72,6... | collective-permute-start | bytes 24584 | tf_op jit(solution)/shard_map/ppermute | solution.py:405
  98.8 5.6 %copy-start.5 = (f32[128]{0:T(128)S(1)}, f32[128]{0:T(128)}, u32[]{:S(2)}) copy-start(f32[128]{0:T(128)} %param.11) | copy-start | bytes 1540

commit v4 on v3

--- a/solution.py
+++ b/solution.py
@@ -13,6 +13,7 @@
 WIN = 16
 GROUPS = 48
 LINES = 4
+PARTS = 4
 GROUP = 16
 
 
@@ -33,8 +34,8 @@
 
 
 def pack_kernel(
-    nparts, me_ref, slots_hbm, hits_hbm, state_hbm, send_hbm, back_ref,
-    slots_ref, hits_ref, state_ref, field, packed, send_ref, code_vmem, code_smem, sems, out_sems,
+    nparts, me_ref, slots_hbm, hits_hbm, state_hbm, sens_hbm, send_ref, back_ref, sens_ref,
+    slots_ref, hits_ref, state_ref, field, packed, code_vmem, code_smem, sems,
 ):
     nblocks, width = slots_ref.shape
     cells = state_ref.shape[0]
@@ -46,6 +47,8 @@
     ]
     for load in loads:
         load.start()
+    fetch = pltpu.make_async_copy(sens_hbm, sens_ref, sems.at[4])
+    fetch.start()
     before = zero_one(iota((width, width), 0) < iota((width, width), 1))
     weights = jnp.concatenate([jnp.ones((width, width), BF16), before], axis=0)
     earlier = zero_one(iota((width, nblocks), 1) < iota((width, nblocks), 0))
@@ -115,22 +118,12 @@
         return 0
 
     lax.fori_loop(0, rows_here, line, 0)
-    stores = []
     for part in range(nparts):
         send_ref[pl.ds(part * SEG, CAP), :] = packed[pl.ds(part * SEG, CAP), :].astype(BF16)
-        stores.append(
-            pltpu.make_async_copy(
-                send_ref.at[pl.ds(part * SEG, SEG), :],
-                send_hbm.at[pl.ds(part * SEG, SEG), :],
-                out_sems.at[part],
-            )
-        )
-        stores[-1].start()
-    for store in stores:
-        store.wait()
-
-
-def pack(me, slots, hits, flat, nparts):
+    fetch.wait()
+
+
+def pack(me, slots, hits, flat, sens, nparts):
     nblocks, width = slots.shape
     cells = flat.shape[0]
     return pl.pallas_call(
@@ -138,24 +131,23 @@
         out_shape=(
             jax.ShapeDtypeStruct((nparts * SEG, width), BF16),
             jax.ShapeDtypeStruct((cells // width, width), jnp.int32),
+            pltpu.VMEM(sens.shape, BF16),
         ),
         in_specs=[pl.BlockSpec(memory_space=pltpu.SMEM)]
-        + [pl.BlockSpec(memory_space=pltpu.HBM)] * 3,
-        out_specs=[pl.BlockSpec(memory_space=pltpu.HBM), pl.BlockSpec(memory_space=pltpu.VMEM)],
+        + [pl.BlockSpec(memory_space=pltpu.HBM)] * 4,
+        out_specs=[pl.BlockSpec(memory_space=pltpu.VMEM)] * 3,
         scratch_shapes=[
             pltpu.VMEM((nblocks, width), jnp.int32),
             pltpu.VMEM((nblocks, width), jnp.int32),
             pltpu.VMEM((cells, width), BF16),
             pltpu.VMEM((cells, width), F32),
             pltpu.VMEM((nparts * SEG, width), F32),
-            pltpu.VMEM((nparts * SEG, width), BF16),
             pltpu.VMEM((cells // width, width), jnp.int32),
             pltpu.SMEM((cells // width, width), jnp.int32),
-            pltpu.SemaphoreType.DMA((4,)),
-            pltpu.SemaphoreType.DMA((nparts,)),
+            pltpu.SemaphoreType.DMA((5,)),
         ],
-        compiler_params=pltpu.CompilerParams(vmem_limit_bytes=62 << 20),
-    )(me, slots, hits, flat)
+        compiler_params=pltpu.CompilerParams(vmem_limit_bytes=36 << 20),
+    )(me, *[pltpu.with_memory_space_constraint(each, pltpu.HBM) for each in (slots, hits, flat, sens)])
 
 
 def react_kernel(
@@ -222,8 +214,7 @@
         for count in counts[1:]:
             most = jnp.maximum(most, count)
 
-        @pl.when(most > WIN)
-        def _():
+        def rest():
             for i in range(GROUPS):
 
                 def more(w, _, i=i):
@@ -239,14 +230,15 @@
 
                 lax.fori_loop(1, (counts[i] + (WIN - 1)) >> 4, more, 0)
 
-    def source(part, _):
-        def batches(step, _):
-            batch(part, step * GROUPS)
-            return 0
-
-        return lax.fori_loop(0, nblocks // GROUPS, batches, 0)
-
-    lax.fori_loop(0, nparts, source, 0)
+        return most > WIN, rest
+
+    def sources(step, _):
+        rests = [batch(step * PARTS + i, 0) for i in range(PARTS)]
+        for needed, rest in rests:
+            pl.when(needed)(rest)
+        return 0
+
+    lax.fori_loop(0, nparts // PARTS, sources, 0)
 
     def narrow(part, _):
         out_ref[pl.ds(pl.multiple_of(part * CAP, 16), CAP), :] = mapped[
@@ -413,11 +405,11 @@
     nparts = lax.axis_size("blk")
     me = lax.axis_index("blk").astype(jnp.int32).reshape(1)
     flat = state.reshape(cells, width)
-    send, code = pack(me, slot_cell[0], hit_step[0], flat, nparts)
+    send, code, sens = pack(me, slot_cell[0], hit_step[0], flat, table_sens, nparts)
     recv = lax.all_to_all(send.reshape(nparts, SEG, width), "blk", 0, 0, tiled=True)
     done = react(
         entry_ids, recv.reshape(nparts * SEG, width),
-        table_value, table_base, table_sens, nparts,
+        table_value, table_base, sens, nparts,
     )
     back = lax.all_to_all(done.reshape(nparts, CAP, width), "blk", 0, 0, tiled=True)
     back = back.reshape(nparts * CAP, width)

time: 108 us -> 101 us (0.935)
  local copies, waits for them, and re-layouts: 3.51 us -> 0.13 us
  Pallas kernels: 23.6 us -> 21.6 us
  blocking collectives: 66.4 us -> 65.1 us
    unnamed x15 -> x11, local copies, waits for them, and re-layouts: 3.51 us -> 0.13 us
    pallas_call x1, Pallas kernels: 8.4 us -> 6.49 us  [pack(): pl.pallas_call(lambda *refs: pack_kernel(nparts, *refs), out_shape=(jax.S...]
    all_to_all x1, blocking collectives: 30.9 us -> 29.7 us  [local(): lax.all_to_all(done.reshape(nparts, CAP, width), 'blk', 0, 0, tiled=True)]
where the time goes in v4:
time: 101 us; the launch traced here: 99.3 us
  blocking collectives  65.1 us (64%)
  Pallas kernels  21.6 us (21%)
  starting transfers between devices  11.4 us (11%)
  waiting for transfers between devices  1.03 us (1%)
    all_to_all x1, blocking collectives, local(): lax.all_to_all(send.reshape(nparts, SEG, width), 'blk', 0, 0, tiled=True)  35.3 us
    all_to_all x1, blocking collectives, local(): lax.all_to_all(done.reshape(nparts, CAP, width), 'blk', 0, 0, tiled=True)  29.7 us
    ppermute x4, starting transfers between devices, shifted(): lax.ppermute(block, axis, forward if ahead else [(j, i) for i, j in forwa...  11.4 us
    pallas_call x1, Pallas kernels, react(): pl.pallas_call(lambda *refs: react_kernel(nparts, nblocks, *refs), out_sh...  7.49 us
    pallas_call x1, Pallas kernels, pack(): pl.pallas_call(lambda *refs: pack_kernel(nparts, *refs), out_shape=(jax.S...  6.49 us
    pallas_call x1, Pallas kernels, unpack(): pl.pallas_call(unpack_kernel, out_shape=jax.ShapeDtypeStruct((cells, widt...  4.45 us
  transfers between devices with their start and end apart: 4, of which 1 were waited for; matrix products, arithmetic and copies ran while one was open for 0% of the time, Pallas kernels for 4%

profile of v4, /device:TPU:30, one launch (start us, length us, event | category | flops | bytes accessed | tf_op | source)
XLA Modules:
  0.0 99.3 jit_solution(5683900403643239094)
XLA Ops:
  0.0 6.5 %shard_map.91 = (bf16[8448,128]{1,0:T(8,128)(2,1)S(1)}, s32[32,128]{1,0:T(8,128)S(1)}, bf16[256,128,128]{2,1,0:T(8,128)(2,1)S(1)}) custom-call(s32[1]{0:T(128)} %bitcast.refs_0_, s32[48,128]{1,0:T(8,128)} %bitcast.20, s32[48,128]{1,0:T(8,128)} %bitcast.21, bf16[4096,128]{1,0:T(8,128)(2,1)} %bitcast.19, bf16[256,128,128]{2,1,0:T(8,128)(2,1)} %refs_4_.1), custom_call_target="tpu_custom_call" | custom-call | tf_op jit(solution)/shard_map/pallas_call | solution.py:129
  6.5 0.0 copy-start
  6.5 0.0 copy-start.1
  6.5 0.0 copy-start.2
  6.5 35.3 %all_to_all.10 = bf16[16,528,128]{2,1,0:T(8,128)(2,1)S(1)} all-to-all(bf16[16,528,128]{2,1,0:T(8,128)(2,1)S(1)} %bitcast.16), channel_id=1, replica_groups=mesh['blk'=16,'grid'=8] {'blk'}, dimensions={0} | all-to-all | bytes 4325376 | tf_op jit(solution)/shard_map/all_to_all | solution.py:409
  41.9 0.0 copy-done
  41.9 0.0 copy-done.1
  41.9 0.0 copy-done.2
  41.9 7.5 %shard_map.92 = bf16[8192,128]{1,0:T(8,128)(2,1)S(1)} custom-call(s32[1,1,768]{2,1,0:T(1,128)S(1)} %copy-done.2, bf16[8448,128]{1,0:T(8,128)(2,1)S(1)} %bitcast.13, bf16[256,128]{1,0:T(8,128)(2,1)S(1)} %copy-done, bf16[256,128]{1,0:T(8,128)(2,1)S(1)} %copy-done.1, bf16[256,128,128]{2,1,0:T(8,128)(2,1)S(1)} %get-tuple-element.14.refs_4_), custom_call_target="tpu_custom_call" | custom-call | tf_op jit(solution)/shard_map/pallas_call | solution.py:255
  49.4 0.0 copy-start.4
  49.4 29.7 %all_to_all.11 = bf16[16,512,128]{2,1,0:T(8,128)(2,1)S(1)} all-to-all(bf16[16,512,128]{2,1,0:T(8,128)(2,1)S(1)} %bitcast.15), channel_id=1, replica_groups=mesh['blk'=16,'grid'=8] {'blk'}, dimensions={0} | all-to-all | bytes 4194304 | tf_op jit(solution)/shard_map/all_to_all | solution.py:414
  79.1 1.3 %shard_map.94 = (bf16[128,128]{1,0:T(8,128)(2,1)S(1)}, bf16[128,128]{1,0:T(8,128)(2,1)S(1)}, bf16[32,128]{1,0:T(8,128)(2,1)S(1)}, bf16[32,128]{1,0:T(8,128)(2,1)S(1)}) custom-call(s32[32,128]{1,0:T(8,128)S(1)} %get-tuple-element.12.code_ref, bf16[8192,128]{1,0:T(8,128)(2,1)S(1)} %bitcast.11), custom_call_target="tpu_custom_call" | custom-call | tf_op jit(solution)/shard_map/pallas_call | solution.py:294
  80.4 0.0 copy-start.3
  80.4 1.9 %collective-permute-start = (bf16[128,128]{1,0:T(8,128)(2,1)S(1)}, bf16[128,128]{1,0:T(8,128)(2,1)S(1)}, u32[]{:S(2)}, u32[]{:S(2)}) collective-permute-start(bf16[128,128]{1,0:T(8,128)(2,1)S(1)} %get-tuple-element.15), channel_id=1, source_target_pairs={{0,1},{1,2},{2,3},{3,4},{4,5},{5,6},{6,7},{8,9},{9,10},{10,11},{11... | collective-permute-start | bytes 98312 | tf_op jit(solution)/shard_map/ppermute | solution.py:397
  82.4 3.6 %collective-permute-start.1 = (bf16[128,128]{1,0:T(8,128)(2,1)S(1)}, bf16[128,128]{1,0:T(8,128)(2,1)S(1)}, u32[]{:S(2)}, u32[]{:S(2)}) collective-permute-start(bf16[128,128]{1,0:T(8,128)(2,1)S(1)} %get-tuple-element.16), channel_id=1, source_target_pairs={{1,0},{2,1},{3,2},{4,3},{5,4},{6,5},{7,6},{9,8},{10,9},{11,10},{12... | collective-permute-start | bytes 98312 | tf_op jit(solution)/shard_map/ppermute | solution.py:397
  86.0 3.8 %collective-permute-start.2 = (bf16[32,128]{1,0:T(8,128)(2,1)S(1)}, bf16[32,128]{1,0:T(8,128)(2,1)S(1)}, u32[]{:S(2)}, u32[]{:S(2)}) collective-permute-start(bf16[32,128]{1,0:T(8,128)(2,1)S(1)} %get-tuple-element.17), channel_id=1, source_target_pairs={{0,8},{8,16},{16,24},{24,32},{32,40},{40,48},{48,56},{56,64},{64,7... | collective-permute-start | bytes 24584 | tf_op jit(solution)/shard_map/ppermute | solution.py:397
  89.8 2.1 %collective-permute-start.3 = (bf16[32,128]{1,0:T(8,128)(2,1)S(1)}, bf16[32,128]{1,0:T(8,128)(2,1)S(1)}, u32[]{:S(2)}, u32[]{:S(2)}) collective-permute-start(bf16[32,128]{1,0:T(8,128)(2,1)S(1)} %get-tuple-element.18), channel_id=1, source_target_pairs={{8,0},{16,8},{24,16},{32,24},{40,32},{48,40},{56,48},{64,56},{72,6... | collective-permute-start | bytes 24584 | tf_op jit(solution)/shard_map/ppermute | solution.py:397
  91.9 0.0 copy-done.4
  91.9 0.1 copy.10
  92.0 4.4 %shard_map.93 = f32[4096,128]{1,0:T(8,128)S(1)} custom-call(s32[32,128]{1,0:T(8,128)S(1)} %get-tuple-element.12.code_ref, bf16[8192,128]{1,0:T(8,128)(2,1)S(1)} %bitcast.12), custom_call_target="tpu_custom_call" | custom-call | bytes 16777216 | tf_op jit(solution)/shard_map/pallas_call | solution.py:324
  96.4 0.0 collective-permute-done.2.left_ref
  96.4 1.0 %collective-permute-done.3.right_ref = bf16[32,128]{1,0:T(8,128)(2,1)S(1)} collective-permute-done((bf16[32,128]{1,0:T(8,128)(2,1)S(1)}, bf16[32,128]{1,0:T(8,128)(2,1)S(1)}, u32[]{:S(2)}, u32[]{:S(2)}) %collective-permute-start.3) | collective-permute-done | bytes 8224 | tf_op jit(solution)/shard_map/ppermute | solution.py:397
  97.5 0.0 collective-permute-done.up_ref
  97.5 0.0 collective-permute-done.1.down_ref
  97.5 0.0 copy-done.3
  97.5 1.8 %shard_map.95 = f32[32,128,128]{2,1,0:T(8,128)} custom-call(f32[32,128,128]{2,1,0:T(8,128)S(1)} %bitcast.14, bf16[128,128]{1,0:T(8,128)(2,1)S(1)} %collective-permute-done.up_ref, bf16[128,128]{1,0:T(8,128)(2,1)S(1)} %collective-permute-done.1.down_ref, bf16[32,128]{1,0:T(8,128)(2,1)S(1)} %collective-permute-done.2.left_ref, ...), custom_call_target="tpu_custom_call" | custom-call | tf_op jit(solution)/shard_map/pallas_call | solution.py:381
Async XLA Ops:
  6.5 35.4 %copy-start = (bf16[256,128]{1,0:T(8,128)(2,1)S(1)}, bf16[256,128]{1,0:T(8,128)(2,1)}, u32[]{:S(2)}) copy-start(bf16[256,128]{1,0:T(8,128)(2,1)} %refs_2_.1) | copy-start | bytes 196612
  6.5 35.4 %copy-start.1 = (bf16[256,128]{1,0:T(8,128)(2,1)S(1)}, bf16[256,128]{1,0:T(8,128)(2,1)}, u32[]{:S(2)}) copy-start(bf16[256,128]{1,0:T(8,128)(2,1)} %refs_3_.1) | copy-start | bytes 196612
  6.5 35.4 %copy-start.2 = (s32[1,1,768]{2,1,0:T(1,128)S(1)}, s32[1,1,768]{2,1,0:T(1,128)}, u32[]{:S(2)}) copy-start(s32[1,1,768]{2,1,0:T(1,128)} %refs_0_.1) | copy-start | bytes 9220
  49.4 42.5 %copy-start.4 = (f32[32,128]{1,0:T(8,128)S(1)}, f32[32,128]{1,0:T(8,128)}, u32[]{:S(2)}) copy-start(f32[32,128]{1,0:T(8,128)} %param.10) | copy-start | bytes 49156
  80.4 17.1 %copy-start.3 = (f32[128]{0:T(128)S(1)}, f32[128]{0:T(128)}, u32[]{:S(2)}) copy-start(f32[128]{0:T(128)} %param.11) | copy-start | bytes 1540
  80.4 17.0 %collective-permute-start = (bf16[128,128]{1,0:T(8,128)(2,1)S(1)}, bf16[128,128]{1,0:T(8,128)(2,1)S(1)}, u32[]{:S(2)}, u32[]{:S(2)}) collective-permute-start(bf16[128,128]{1,0:T(8,128)(2,1)S(1)} %get-tuple-element.15), channel_id=1, source_target_pairs={{0,1},{1,2},{2,3},{3,4},{4,5},{5,6},{6,7},{8,9},{9,10},{10,11},{11... | collective-permute-start | bytes 98312 | tf_op jit(solution)/shard_map/ppermute | solution.py:397
  82.4 15.1 %collective-permute-start.1 = (bf16[128,128]{1,0:T(8,128)(2,1)S(1)}, bf16[128,128]{1,0:T(8,128)(2,1)S(1)}, u32[]{:S(2)}, u32[]{:S(2)}) collective-permute-start(bf16[128,128]{1,0:T(8,128)(2,1)S(1)} %get-tuple-element.16), channel_id=1, source_target_pairs={{1,0},{2,1},{3,2},{4,3},{5,4},{6,5},{7,6},{9,8},{10,9},{11,10},{12... | collective-permute-start | bytes 98312 | tf_op jit(solution)/shard_map/ppermute | solution.py:397
  86.0 10.4 %collective-permute-start.2 = (bf16[32,128]{1,0:T(8,128)(2,1)S(1)}, bf16[32,128]{1,0:T(8,128)(2,1)S(1)}, u32[]{:S(2)}, u32[]{:S(2)}) collective-permute-start(bf16[32,128]{1,0:T(8,128)(2,1)S(1)} %get-tuple-element.17), channel_id=1, source_target_pairs={{0,8},{8,16},{16,24},{24,32},{32,40},{40,48},{48,56},{56,64},{64,7... | collective-permute-start | bytes 24584 | tf_op jit(solution)/shard_map/ppermute | solution.py:397
  89.8 7.7 %collective-permute-start.3 = (bf16[32,128]{1,0:T(8,128)(2,1)S(1)}, bf16[32,128]{1,0:T(8,128)(2,1)S(1)}, u32[]{:S(2)}, u32[]{:S(2)}) collective-permute-start(bf16[32,128]{1,0:T(8,128)(2,1)S(1)} %get-tuple-element.18), channel_id=1, source_target_pairs={{8,0},{16,8},{24,16},{32,24},{40,32},{48,40},{56,48},{64,56},{72,6... | collective-permute-start | bytes 24584 | tf_op jit(solution)/shard_map/ppermute | solution.py:397

commit v5 on v4

--- a/solution.py
+++ b/solution.py
@@ -10,10 +10,10 @@
 CAP = 512
 META = 16
 SEG = CAP + META
-WIN = 16
+WIN = 24
 GROUPS = 48
 LINES = 4
-PARTS = 4
+PARTS = 8
 GROUP = 16
 
 
@@ -152,16 +152,29 @@
 
 def react_kernel(
     nparts, nblocks, entries_ref, recv_ref, value_ref, base_ref, sens_ref, out_ref,
-    rows, mapped, values, bases, begin_vmem, begin_smem, sem,
+    rows, mapped, table, begin_vmem, begin_smem, sem,
 ):
     width = recv_ref.shape[1]
-    values[...] = value_ref[...].astype(F32)
-    bases[...] = base_ref[...].astype(F32)
+    depth = base_ref.shape[0]
     for part in range(nparts):
         meta = recv_ref[pl.ds(part * SEG + CAP, META), :].astype(F32)
         begin_vmem[pl.ds(part, 1), :] = (meta[0:1] * 16.0 + meta[1:2]).astype(jnp.int32)
+    begin = begin_vmem[pl.ds(0, nparts), :]
+    lane = iota((nparts, width), 1)
+    counts = pltpu.roll(begin, width - 1, 1) - begin
+    end = width - 1
+    following = jnp.where((lane < nblocks) & (counts > WIN), lane, end)
+    ahead = 1
+    while ahead < width:
+        moved = pltpu.roll(following, width - ahead, 1)
+        following = jnp.minimum(following, jnp.where(lane + ahead < width, moved, end))
+        ahead *= 2
+    begin_vmem[pl.ds(0, nparts), :] = begin + SEG * iota((nparts, width), 0)
+    begin_vmem[pl.ds(nparts, nparts), :] = pltpu.roll(following, end, 1)
     copy = pltpu.make_async_copy(begin_vmem, begin_smem, sem)
     copy.start()
+    table[pl.ds(0, depth), :] = base_ref[...].astype(F32)
+    table[pl.ds(depth, depth), :] = value_ref[...].astype(F32)
 
     def widen(part, _):
         at = pl.multiple_of(part * SEG, 16)
@@ -170,75 +183,53 @@
 
     lax.fori_loop(0, nparts, widen, 0)
     copy.wait()
-    zero = jnp.zeros((WIN, width), BF16)
-    four = 4
 
     def delta(at, entry):
-        base = bases[pl.ds(entry, 1), :]
-        return (rows[pl.ds(at, WIN), :] - base).astype(BF16)
+        base = table[pl.ds(entry, 1), :]
+        return rows[pl.ds(at, WIN), :] - base
 
     def batch(part, first):
-        begins = [begin_smem[part, first + i] for i in range(GROUPS + 1)]
+        at = [begin_smem[part, first + i] for i in range(GROUPS + 1)]
         entry = [entries_ref[0, 0, part * nblocks + first + i] for i in range(GROUPS)]
-        at = [part * SEG + begins[i] for i in range(GROUPS)]
         dx = [delta(at[i], entry[i]) for i in range(GROUPS)]
         results = []
-        for i in range(0, GROUPS, four):
-            lhs = jnp.concatenate(
-                [
-                    jnp.concatenate([dx[i], zero], axis=1),
-                    jnp.concatenate([dx[i + 1], zero], axis=1),
-                    jnp.concatenate([zero, dx[i + 2]], axis=1),
-                    jnp.concatenate([zero, dx[i + 3]], axis=1),
-                ],
-                axis=0,
+        for i in range(0, GROUPS, 2):
+            product = dot(
+                jnp.concatenate([dx[i], dx[i + 1]], axis=0).astype(BF16),
+                jnp.concatenate([sens_ref[entry[i]], sens_ref[entry[i + 1]]], axis=1),
             )
-            rhs = jnp.concatenate(
-                [
-                    jnp.concatenate([sens_ref[entry[i]], sens_ref[entry[i + 1]]], axis=1),
-                    jnp.concatenate([sens_ref[entry[i + 2]], sens_ref[entry[i + 3]]], axis=1),
-                ],
-                axis=0,
-            )
-            product = dot(lhs, rhs)
-            for j in range(four):
-                half = (j % 2) * width
-                results.append(
-                    product[j * WIN : (j + 1) * WIN, half : half + width]
-                    + values[pl.ds(entry[i + j], 1), :]
-                )
+            results.append(product[:WIN, :width] + table[pl.ds(entry[i] + depth, 1), :])
+            results.append(product[WIN:, width:] + table[pl.ds(entry[i + 1] + depth, 1), :])
         for i in range(GROUPS):
             mapped[pl.ds(at[i], WIN), :] = results[i]
-        counts = [begins[i + 1] - begins[i] for i in range(GROUPS)]
-        most = counts[0]
-        for count in counts[1:]:
-            most = jnp.maximum(most, count)
-
-        def rest():
-            for i in range(GROUPS):
-
-                def more(w, _, i=i):
-                    here = at[i] + w * WIN
-                    left = counts[i] - w * WIN
-                    result = dot(delta(here, entry[i]), sens_ref[entry[i]])
-                    result = result + values[pl.ds(entry[i], 1), :]
-                    keep = iota((WIN, width), 0) < left
-                    mapped[pl.ds(here, WIN), :] = jnp.where(
-                        keep, result, mapped[pl.ds(here, WIN), :]
-                    )
-                    return 0
-
-                lax.fori_loop(1, (counts[i] + (WIN - 1)) >> 4, more, 0)
-
-        return most > WIN, rest
 
     def sources(step, _):
-        rests = [batch(step * PARTS + i, 0) for i in range(PARTS)]
-        for needed, rest in rests:
-            pl.when(needed)(rest)
+        for i in range(PARTS):
+            batch(step * PARTS + i, 0)
         return 0
 
     lax.fori_loop(0, nparts // PARTS, sources, 0)
+
+    def rest(part, _):
+        def group(k):
+            entry = entries_ref[0, 0, part * nblocks + k]
+            at, stop = begin_smem[part, k], begin_smem[part, k + 1]
+
+            def more(here):
+                result = dot(delta(here, entry).astype(BF16), sens_ref[entry])
+                result = result + table[pl.ds(entry + depth, 1), :]
+                mapped[pl.ds(here, WIN), :] = jnp.where(
+                    iota((WIN, width), 0) < stop - here, result, mapped[pl.ds(here, WIN), :]
+                )
+                return here + WIN
+
+            lax.while_loop(lambda here: here < stop, more, at + WIN)
+            return begin_smem[nparts + part, k]
+
+        lax.while_loop(lambda k: k < end, group, begin_smem[nparts + part, end])
+        return 0
+
+    lax.fori_loop(0, nparts, rest, 0)
 
     def narrow(part, _):
         out_ref[pl.ds(pl.multiple_of(part * CAP, 16), CAP), :] = mapped[
@@ -259,12 +250,11 @@
         + [pl.BlockSpec(memory_space=pltpu.VMEM)] * 4,
         out_specs=pl.BlockSpec(memory_space=pltpu.VMEM),
         scratch_shapes=[
-            pltpu.VMEM((nparts * SEG, width), F32),
-            pltpu.VMEM((nparts * SEG, width), F32),
-            pltpu.VMEM(value.shape, F32),
-            pltpu.VMEM(base.shape, F32),
-            pltpu.VMEM((nparts, width), jnp.int32),
-            pltpu.SMEM((nparts, width), jnp.int32),
+            pltpu.VMEM((nparts * SEG + WIN, width), F32),
+            pltpu.VMEM((nparts * SEG + WIN, width), F32),
+            pltpu.VMEM((2 * base.shape[0], width), F32),
+            pltpu.VMEM((2 * nparts, width), jnp.int32),
+            pltpu.SMEM((2 * nparts, width), jnp.int32),
             pltpu.SemaphoreType.DMA,
         ],
         compiler_params=pltpu.CompilerParams(vmem_limit_bytes=24 << 20),

time: 101 us -> 101 us (level)
  no operation moved by 1% of the time
where the time goes in v5:
time: 101 us; the launch traced here: 98.8 us
  blocking collectives  65.2 us (65%)
  Pallas kernels  21 us (21%)
  starting transfers between devices  11.4 us (11%)
    all_to_all x1, blocking collectives, local(): lax.all_to_all(send.reshape(nparts, SEG, width), 'blk', 0, 0, tiled=True)  35.3 us
    all_to_all x1, blocking collectives, local(): lax.all_to_all(done.reshape(nparts, CAP, width), 'blk', 0, 0, tiled=True)  29.9 us
    ppermute x4, starting transfers between devices, shifted(): lax.ppermute(block, axis, forward if ahead else [(j, i) for i, j in forwa...  11.4 us
    pallas_call x1, Pallas kernels, react(): pl.pallas_call(lambda *refs: react_kernel(nparts, nblocks, *refs), out_sh...  6.93 us
    pallas_call x1, Pallas kernels, pack(): pl.pallas_call(lambda *refs: pack_kernel(nparts, *refs), out_shape=(jax.S...  6.49 us
    pallas_call x1, Pallas kernels, unpack(): pl.pallas_call(unpack_kernel, out_shape=jax.ShapeDtypeStruct((cells, widt...  4.45 us
  transfers between devices with their start and end apart: 4, of which 1 were waited for; matrix products, arithmetic and copies ran while one was open for 0% of the time, Pallas kernels for 4%

profile of v5, /device:TPU:30, one launch (start us, length us, event | category | flops | bytes accessed | tf_op | source)
XLA Modules:
  0.0 98.8 jit_solution(10222947640601544751)
XLA Ops:
  0.0 6.5 %shard_map.91 = (bf16[8448,128]{1,0:T(8,128)(2,1)S(1)}, s32[32,128]{1,0:T(8,128)S(1)}, bf16[256,128,128]{2,1,0:T(8,128)(2,1)S(1)}) custom-call(s32[1]{0:T(128)} %bitcast.refs_0_, s32[48,128]{1,0:T(8,128)} %bitcast.20, s32[48,128]{1,0:T(8,128)} %bitcast.21, bf16[4096,128]{1,0:T(8,128)(2,1)} %bitcast.19, bf16[256,128,128]{2,1,0:T(8,128)(2,1)} %refs_4_.1), custom_call_target="tpu_custom_call" | custom-call | tf_op jit(solution)/shard_map/pallas_call | solution.py:129
  6.5 0.0 copy-start
  6.5 0.0 copy-start.1
  6.5 0.0 copy-start.2
  6.5 35.3 %all_to_all.10 = bf16[16,528,128]{2,1,0:T(8,128)(2,1)S(1)} all-to-all(bf16[16,528,128]{2,1,0:T(8,128)(2,1)S(1)} %bitcast.16), channel_id=1, replica_groups=mesh['blk'=16,'grid'=8] {'blk'}, dimensions={0} | all-to-all | bytes 4325376 | tf_op jit(solution)/shard_map/all_to_all | solution.py:399
  41.9 0.0 copy-done
  41.9 0.0 copy-done.1
  41.9 0.0 copy-done.2
  41.9 6.9 %shard_map.92 = bf16[8192,128]{1,0:T(8,128)(2,1)S(1)} custom-call(s32[1,1,768]{2,1,0:T(1,128)S(1)} %copy-done.2, bf16[8448,128]{1,0:T(8,128)(2,1)S(1)} %bitcast.13, bf16[256,128]{1,0:T(8,128)(2,1)S(1)} %copy-done, bf16[256,128]{1,0:T(8,128)(2,1)S(1)} %copy-done.1, bf16[256,128,128]{2,1,0:T(8,128)(2,1)S(1)} %get-tuple-element.14.refs_4_), custom_call_target="tpu_custom_call" | custom-call | tf_op jit(solution)/shard_map/pallas_call | solution.py:246
  48.8 0.0 copy-start.4
  48.8 29.9 %all_to_all.11 = bf16[16,512,128]{2,1,0:T(8,128)(2,1)S(1)} all-to-all(bf16[16,512,128]{2,1,0:T(8,128)(2,1)S(1)} %bitcast.15), channel_id=1, replica_groups=mesh['blk'=16,'grid'=8] {'blk'}, dimensions={0} | all-to-all | bytes 4194304 | tf_op jit(solution)/shard_map/all_to_all | solution.py:404
  78.7 1.3 %shard_map.94 = (bf16[128,128]{1,0:T(8,128)(2,1)S(1)}, bf16[128,128]{1,0:T(8,128)(2,1)S(1)}, bf16[32,128]{1,0:T(8,128)(2,1)S(1)}, bf16[32,128]{1,0:T(8,128)(2,1)S(1)}) custom-call(s32[32,128]{1,0:T(8,128)S(1)} %get-tuple-element.12.code_ref, bf16[8192,128]{1,0:T(8,128)(2,1)S(1)} %bitcast.11), custom_call_target="tpu_custom_call" | custom-call | tf_op jit(solution)/shard_map/pallas_call | solution.py:284
  80.1 0.0 copy-start.3
  80.1 1.9 %collective-permute-start = (bf16[128,128]{1,0:T(8,128)(2,1)S(1)}, bf16[128,128]{1,0:T(8,128)(2,1)S(1)}, u32[]{:S(2)}, u32[]{:S(2)}) collective-permute-start(bf16[128,128]{1,0:T(8,128)(2,1)S(1)} %get-tuple-element.15), channel_id=1, source_target_pairs={{0,1},{1,2},{2,3},{3,4},{4,5},{5,6},{6,7},{8,9},{9,10},{10,11},{11... | collective-permute-start | bytes 98312 | tf_op jit(solution)/shard_map/ppermute | solution.py:387
  82.0 3.6 %collective-permute-start.1 = (bf16[128,128]{1,0:T(8,128)(2,1)S(1)}, bf16[128,128]{1,0:T(8,128)(2,1)S(1)}, u32[]{:S(2)}, u32[]{:S(2)}) collective-permute-start(bf16[128,128]{1,0:T(8,128)(2,1)S(1)} %get-tuple-element.16), channel_id=1, source_target_pairs={{1,0},{2,1},{3,2},{4,3},{5,4},{6,5},{7,6},{9,8},{10,9},{11,10},{12... | collective-permute-start | bytes 98312 | tf_op jit(solution)/shard_map/ppermute | solution.py:387
  85.6 3.7 %collective-permute-start.2 = (bf16[32,128]{1,0:T(8,128)(2,1)S(1)}, bf16[32,128]{1,0:T(8,128)(2,1)S(1)}, u32[]{:S(2)}, u32[]{:S(2)}) collective-permute-start(bf16[32,128]{1,0:T(8,128)(2,1)S(1)} %get-tuple-element.17), channel_id=1, source_target_pairs={{0,8},{8,16},{16,24},{24,32},{32,40},{40,48},{48,56},{56,64},{64,7... | collective-permute-start | bytes 24584 | tf_op jit(solution)/shard_map/ppermute | solution.py:387
  89.3 2.2 %collective-permute-start.3 = (bf16[32,128]{1,0:T(8,128)(2,1)S(1)}, bf16[32,128]{1,0:T(8,128)(2,1)S(1)}, u32[]{:S(2)}, u32[]{:S(2)}) collective-permute-start(bf16[32,128]{1,0:T(8,128)(2,1)S(1)} %get-tuple-element.18), channel_id=1, source_target_pairs={{8,0},{16,8},{24,16},{32,24},{40,32},{48,40},{56,48},{64,56},{72,6... | collective-permute-start | bytes 24584 | tf_op jit(solution)/shard_map/ppermute | solution.py:387
  91.5 0.0 copy-done.4
  91.5 0.1 copy.10
  91.6 4.4 %shard_map.93 = f32[4096,128]{1,0:T(8,128)S(1)} custom-call(s32[32,128]{1,0:T(8,128)S(1)} %get-tuple-element.12.code_ref, bf16[8192,128]{1,0:T(8,128)(2,1)S(1)} %bitcast.12), custom_call_target="tpu_custom_call" | custom-call | bytes 16777216 | tf_op jit(solution)/shard_map/pallas_call | solution.py:314
  96.1 0.0 collective-permute-done.2.left_ref
  96.1 0.9 collective-permute-done.3.right_ref
  97.0 0.0 collective-permute-done.up_ref
  97.0 0.0 collective-permute-done.1.down_ref
  97.0 0.0 copy-done.3
  97.0 1.8 %shard_map.95 = f32[32,128,128]{2,1,0:T(8,128)} custom-call(f32[32,128,128]{2,1,0:T(8,128)S(1)} %bitcast.14, bf16[128,128]{1,0:T(8,128)(2,1)S(1)} %collective-permute-done.up_ref, bf16[128,128]{1,0:T(8,128)(2,1)S(1)} %collective-permute-done.1.down_ref, bf16[32,128]{1,0:T(8,128)(2,1)S(1)} %collective-permute-done.2.left_ref, ...), custom_call_target="tpu_custom_call" | custom-call | tf_op jit(solution)/shard_map/pallas_call | solution.py:371
Async XLA Ops:
  6.5 35.4 %copy-start = (bf16[256,128]{1,0:T(8,128)(2,1)S(1)}, bf16[256,128]{1,0:T(8,128)(2,1)}, u32[]{:S(2)}) copy-start(bf16[256,128]{1,0:T(8,128)(2,1)} %refs_2_.1) | copy-start | bytes 196612
  6.5 35.4 %copy-start.1 = (bf16[256,128]{1,0:T(8,128)(2,1)S(1)}, bf16[256,128]{1,0:T(8,128)(2,1)}, u32[]{:S(2)}) copy-start(bf16[256,128]{1,0:T(8,128)(2,1)} %refs_3_.1) | copy-start | bytes 196612
  6.5 35.4 %copy-start.2 = (s32[1,1,768]{2,1,0:T(1,128)S(1)}, s32[1,1,768]{2,1,0:T(1,128)}, u32[]{:S(2)}) copy-start(s32[1,1,768]{2,1,0:T(1,128)} %refs_0_.1) | copy-start | bytes 9220
  48.8 42.7 %copy-start.4 = (f32[32,128]{1,0:T(8,128)S(1)}, f32[32,128]{1,0:T(8,128)}, u32[]{:S(2)}) copy-start(f32[32,128]{1,0:T(8,128)} %param.10) | copy-start | bytes 49156
  80.1 16.9 %copy-start.3 = (f32[128]{0:T(128)S(1)}, f32[128]{0:T(128)}, u32[]{:S(2)}) copy-start(f32[128]{0:T(128)} %param.11) | copy-start | bytes 1540
  80.1 16.9 %collective-permute-start = (bf16[128,128]{1,0:T(8,128)(2,1)S(1)}, bf16[128,128]{1,0:T(8,128)(2,1)S(1)}, u32[]{:S(2)}, u32[]{:S(2)}) collective-permute-start(bf16[128,128]{1,0:T(8,128)(2,1)S(1)} %get-tuple-element.15), channel_id=1, source_target_pairs={{0,1},{1,2},{2,3},{3,4},{4,5},{5,6},{6,7},{8,9},{9,10},{10,11},{11... | collective-permute-start | bytes 98312 | tf_op jit(solution)/shard_map/ppermute | solution.py:387
  82.0 15.0 %collective-permute-start.1 = (bf16[128,128]{1,0:T(8,128)(2,1)S(1)}, bf16[128,128]{1,0:T(8,128)(2,1)S(1)}, u32[]{:S(2)}, u32[]{:S(2)}) collective-permute-start(bf16[128,128]{1,0:T(8,128)(2,1)S(1)} %get-tuple-element.16), channel_id=1, source_target_pairs={{1,0},{2,1},{3,2},{4,3},{5,4},{6,5},{7,6},{9,8},{10,9},{11,10},{12... | collective-permute-start | bytes 98312 | tf_op jit(solution)/shard_map/ppermute | solution.py:387
  85.6 10.4 %collective-permute-start.2 = (bf16[32,128]{1,0:T(8,128)(2,1)S(1)}, bf16[32,128]{1,0:T(8,128)(2,1)S(1)}, u32[]{:S(2)}, u32[]{:S(2)}) collective-permute-start(bf16[32,128]{1,0:T(8,128)(2,1)S(1)} %get-tuple-element.17), channel_id=1, source_target_pairs={{0,8},{8,16},{16,24},{24,32},{32,40},{40,48},{48,56},{56,64},{64,7... | collective-permute-start | bytes 24584 | tf_op jit(solution)/shard_map/ppermute | solution.py:387
  89.3 7.7 %collective-permute-start.3 = (bf16[32,128]{1,0:T(8,128)(2,1)S(1)}, bf16[32,128]{1,0:T(8,128)(2,1)S(1)}, u32[]{:S(2)}, u32[]{:S(2)}) collective-permute-start(bf16[32,128]{1,0:T(8,128)(2,1)S(1)} %get-tuple-element.18), channel_id=1, source_target_pairs={{8,0},{16,8},{24,16},{32,24},{40,32},{48,40},{56,48},{64,56},{72,6... | collective-permute-start | bytes 24584 | tf_op jit(solution)/shard_map/ppermute | solution.py:387

commit v6 on v5

--- a/solution.py
+++ b/solution.py
@@ -12,7 +12,7 @@
 SEG = CAP + META
 WIN = 24
 GROUPS = 48
-LINES = 4
+STEP = 4
 PARTS = 8
 GROUP = 16
 
@@ -34,7 +34,7 @@
 
 
 def pack_kernel(
-    nparts, me_ref, slots_hbm, hits_hbm, state_hbm, sens_hbm, send_ref, back_ref, sens_ref,
+    nparts, lines, me_ref, slots_hbm, hits_hbm, state_hbm, sens_hbm, send_ref, back_ref, sens_ref,
     slots_ref, hits_ref, state_ref, field, packed, code_vmem, code_smem, sems,
 ):
     nblocks, width = slots_ref.shape
@@ -58,7 +58,7 @@
     loads[1].wait()
     slots = slots_ref[...]
     live = slots >= 0
-    owner = jnp.where(live, (hits_ref[...] + me_ref[0]) & (nparts - 1), nparts)
+    owner = jnp.where(live, (hits_ref[...] + (me_ref[0] // lines)) & (nparts - 1), nparts)
     mine = [owner == part for part in range(nparts)]
     masks = [zero_one(each) for each in mine]
     ahead = [dot(earlier, mask).astype(BF16) for mask in masks]
@@ -123,11 +123,11 @@
     fetch.wait()
 
 
-def pack(me, slots, hits, flat, sens, nparts):
+def pack(me, slots, hits, flat, sens, nparts, lines):
     nblocks, width = slots.shape
     cells = flat.shape[0]
     return pl.pallas_call(
-        lambda *refs: pack_kernel(nparts, *refs),
+        lambda *refs: pack_kernel(nparts, lines, *refs),
         out_shape=(
             jax.ShapeDtypeStruct((nparts * SEG, width), BF16),
             jax.ShapeDtypeStruct((cells // width, width), jnp.int32),
@@ -261,10 +261,13 @@
     )(entries, recv, value, base, sens)
 
 
-def edges_kernel(code_ref, ret_ref, up_ref, down_ref, left_ref, right_ref, rows):
+def edges_kernel(
+    lines, me_ref, code_ref, ret_ref, along1_ref, along2_ref, across1_ref, across2_ref, rows
+):
     rows_here, width = code_ref.shape
     cols_here = width
     rows[...] = ret_ref[...].astype(F32)
+    along, across = me_ref[0] & 1, (me_ref[0] // lines) & 1
 
     def gather(out, spots):
         for first in range(0, len(spots), GROUP):
@@ -272,26 +275,30 @@
                 [rows[pl.ds(at, 1), :] for at in spots[first : first + GROUP]], axis=0
             ).astype(BF16)
 
-    gather(up_ref, [code_ref[rows_here - 1, j] for j in range(cols_here)])
-    gather(down_ref, [code_ref[0, j] for j in range(cols_here)])
-    gather(left_ref, [code_ref[i, cols_here - 1] for i in range(rows_here)])
-    gather(right_ref, [code_ref[i, 0] for i in range(rows_here)])
-
-
-def edges(code, ret):
+    for out, line in (
+        (along1_ref, (1 - along) * (rows_here - 1)),
+        (along2_ref, along * (rows_here - 1)),
+    ):
+        gather(out, [code_ref[line, j] for j in range(cols_here)])
+    for out, column in (
+        (across1_ref, (1 - across) * (cols_here - 1)),
+        (across2_ref, across * (cols_here - 1)),
+    ):
+        gather(out, [code_ref[i, column] for i in range(rows_here)])
+
+
+def edges(me, code, ret, lines):
     rows_here, width = code.shape
     ends = [rows_here if side else width for side in (0, 0, 1, 1)]
     return pl.pallas_call(
-        edges_kernel,
+        lambda *refs: edges_kernel(lines, *refs),
         out_shape=[jax.ShapeDtypeStruct((end, width), BF16) for end in ends],
-        in_specs=[
-            pl.BlockSpec(memory_space=pltpu.SMEM),
-            pl.BlockSpec(memory_space=pltpu.VMEM),
-        ],
+        in_specs=[pl.BlockSpec(memory_space=pltpu.SMEM)] * 2
+        + [pl.BlockSpec(memory_space=pltpu.VMEM)],
         out_specs=[pl.BlockSpec(memory_space=pltpu.VMEM)] * 4,
         scratch_shapes=[pltpu.VMEM(ret.shape, F32)],
         compiler_params=pltpu.CompilerParams(vmem_limit_bytes=20 << 20),
-    )(code, ret)
+    )(me, code, ret)
 
 
 def unpack_kernel(code_ref, ret_ref, out_ref, rows):
@@ -326,28 +333,35 @@
 
 
 def transport_kernel(
-    mid_ref, up_ref, down_ref, left_ref, right_ref, courant_ref, diffusion_ref, out_hbm,
-    out_ref, sems,
+    lines, me_ref, mid_ref, along1_ref, along2_ref, across1_ref, across2_ref,
+    courant_ref, diffusion_ref, out_hbm, out_ref, sems,
 ):
     rows_here, cols, width = mid_ref.shape
+
+    def sides(odd, one, two):
+        one, two = one[...].astype(F32), two[...].astype(F32)
+        return jnp.where(odd == 1, one, two), jnp.where(odd == 1, two, one)
+
+    up, down = sides(me_ref[0] & 1, along1_ref, along2_ref)
+    left_side, right_side = sides((me_ref[0] // lines) & 1, across1_ref, across2_ref)
     diffusion = diffusion_ref[...]
     first = iota((cols, width), 0) == 0
     last = iota((cols, width), 0) == cols - 1
 
     def row(i):
         if i < 0:
-            return up_ref[...].astype(F32)
+            return up
         if i >= rows_here:
-            return down_ref[...].astype(F32)
+            return down
         return mid_ref[i]
 
     stores = []
     above, here = row(-1), row(0)
     for i in range(rows_here):
         below = row(i + 1)
-        left = jnp.where(first, left_ref[i : i + 1, :].astype(F32), pltpu.roll(here, 1, 0))
+        left = jnp.where(first, left_side[i : i + 1, :], pltpu.roll(here, 1, 0))
         right = jnp.where(
-            last, right_ref[i : i + 1, :].astype(F32), pltpu.roll(here, cols - 1, 0)
+            last, right_side[i : i + 1, :], pltpu.roll(here, cols - 1, 0)
         )
         courant = courant_ref[:, i : i + 1]
         out_ref[i] = (
@@ -356,35 +370,35 @@
             + diffusion * (above + below + left + right - 4.0 * here)
         )
         above, here = here, below
-        if i % LINES == LINES - 1:
-            piece = pl.ds(i + 1 - LINES, LINES)
+        if i % STEP == STEP - 1:
+            piece = pl.ds(i + 1 - STEP, STEP)
             stores.append(
-                pltpu.make_async_copy(out_ref.at[piece], out_hbm.at[piece], sems.at[i // LINES])
+                pltpu.make_async_copy(out_ref.at[piece], out_hbm.at[piece], sems.at[i // STEP])
             )
             stores[-1].start()
     for store in stores:
         store.wait()
 
 
-def transport(reacted, up, down, left, right, courant, diffusion):
+def transport(me, lines, reacted, halo, courant, diffusion):
     shape = reacted.shape
     return pl.pallas_call(
-        transport_kernel,
+        lambda *refs: transport_kernel(lines, *refs),
         out_shape=jax.ShapeDtypeStruct(shape, F32),
-        in_specs=[pl.BlockSpec(memory_space=pltpu.VMEM)] * 7,
+        in_specs=[pl.BlockSpec(memory_space=pltpu.SMEM)]
+        + [pl.BlockSpec(memory_space=pltpu.VMEM)] * 7,
         out_specs=pl.BlockSpec(memory_space=pl.ANY),
         scratch_shapes=[
             pltpu.VMEM(shape, F32),
-            pltpu.SemaphoreType.DMA((shape[0] // LINES,)),
+            pltpu.SemaphoreType.DMA((shape[0] // STEP,)),
         ],
         compiler_params=pltpu.CompilerParams(vmem_limit_bytes=20 << 20),
-    )(reacted, up, down, left, right, courant, diffusion)
-
-
-def shifted(block, axis, ahead):
-    count = lax.axis_size(axis)
-    forward = [(i, i + 1) for i in range(count - 1)]
-    return lax.ppermute(block, axis, forward if ahead else [(j, i) for i, j in forward])
+    )(me, reacted, *halo, courant, diffusion)
+
+
+def swapped(block, axis, first):
+    pairs = [(i, i + 1) for i in range(first, lax.axis_size(axis) - 1, 2)]
+    return lax.ppermute(block, axis, pairs + [(j, i) for i, j in pairs])
 
 
 def local(
@@ -392,10 +406,10 @@
 ):
     rows_here, cols_here, width = state.shape
     cells = rows_here * cols_here
-    nparts = lax.axis_size("blk")
-    me = lax.axis_index("blk").astype(jnp.int32).reshape(1)
+    nparts, lines = lax.axis_size("blk"), lax.axis_size("grid")
+    me = lax.axis_index(("blk", "grid")).astype(jnp.int32).reshape(1)
     flat = state.reshape(cells, width)
-    send, code, sens = pack(me, slot_cell[0], hit_step[0], flat, table_sens, nparts)
+    send, code, sens = pack(me, slot_cell[0], hit_step[0], flat, table_sens, nparts, lines)
     recv = lax.all_to_all(send.reshape(nparts, SEG, width), "blk", 0, 0, tiled=True)
     done = react(
         entry_ids, recv.reshape(nparts * SEG, width),
@@ -403,15 +417,13 @@
     )
     back = lax.all_to_all(done.reshape(nparts, CAP, width), "blk", 0, 0, tiled=True)
     back = back.reshape(nparts * CAP, width)
-    last_line, first_line, last_column, first_column = edges(code, back)
-    up = shifted(last_line, "grid", True)
-    down = shifted(first_line, "grid", False)
-    left = shifted(last_column, "blk", True)
-    right = shifted(first_column, "blk", False)
+    along1, along2, across1, across2 = edges(me, code, back, lines)
+    halo = (
+        swapped(along1, "grid", 0), swapped(along2, "grid", 1),
+        swapped(across1, "blk", 0), swapped(across2, "blk", 1),
+    )
     reacted = unpack(code, back).reshape(rows_here, cols_here, width)
-    return transport(
-        reacted, up, down, left, right, courant.T, diffusion.reshape(1, width)
-    )
+    return transport(me, lines, reacted, halo, courant.T, diffusion.reshape(1, width))
 
 
 def solution(mesh):

time: 101 us -> 96.1 us (0.951)
  starting transfers between devices: 11.4 us -> 7.4 us
    ppermute x4, starting transfers between devices: 11.4 us -> 7.4 us  [swapped(): return lax.ppermute(block, axis, pairs + [(j, i) for i, j in pairs])]
  transfers between devices with their start and end apart: 4 -> 4, of which waited for: 1 -> 0; matrix products, arithmetic and copies ran while one was open for 0% -> 0% of each run, Pallas kernels for 4% -> 5%
where the time goes in v6:
time: 96.1 us; the launch traced here: 94.4 us
  blocking collectives  65.6 us (68%)
  Pallas kernels  21.1 us (22%)
  starting transfers between devices  7.4 us (8%)
    all_to_all x1, blocking collectives, local(): lax.all_to_all(send.reshape(nparts, SEG, width), 'blk', 0, 0, tiled=True)  35.3 us
    all_to_all x1, blocking collectives, local(): lax.all_to_all(done.reshape(nparts, CAP, width), 'blk', 0, 0, tiled=True)  30.3 us
    ppermute x4, starting transfers between devices, swapped(): return lax.ppermute(block, axis, pairs + [(j, i) for i, j in pairs])  7.4 us
    pallas_call x1, Pallas kernels, react(): pl.pallas_call(lambda *refs: react_kernel(nparts, nblocks, *refs), out_sh...  6.92 us
    pallas_call x1, Pallas kernels, pack(): pl.pallas_call(lambda *refs: pack_kernel(nparts, lines, *refs), out_shape...  6.49 us
    pallas_call x1, Pallas kernels, unpack(): pl.pallas_call(unpack_kernel, out_shape=jax.ShapeDtypeStruct((cells, widt...  4.45 us
  transfers between devices with their start and end apart: 4, of which 0 were waited for; matrix products, arithmetic and copies ran while one was open for 0% of the time, Pallas kernels for 5%

profile of v6, /device:TPU:30, one launch (start us, length us, event | category | flops | bytes accessed | tf_op | source)
XLA Modules:
  0.0 94.4 jit_solution(2292689125590886348)
XLA Ops:
  0.0 6.5 %shard_map.91 = (bf16[8448,128]{1,0:T(8,128)(2,1)S(1)}, s32[32,128]{1,0:T(8,128)S(1)}, bf16[256,128,128]{2,1,0:T(8,128)(2,1)S(1)}) custom-call(s32[1]{0:T(128)} %bitcast.refs_0_, s32[48,128]{1,0:T(8,128)} %bitcast.20, s32[48,128]{1,0:T(8,128)} %bitcast.21, bf16[4096,128]{1,0:T(8,128)(2,1)} %bitcast.19, bf16[256,128,128]{2,1,0:T(8,128)(2,1)} %refs_4_.1), custom_call_target="tpu_custom_call" | custom-call | tf_op jit(solution)/shard_map/pallas_call | solution.py:129
  6.5 0.0 copy-start
  6.5 0.0 copy-start.1
  6.5 0.0 copy-start.2
  6.5 35.3 %all_to_all.10 = bf16[16,528,128]{2,1,0:T(8,128)(2,1)S(1)} all-to-all(bf16[16,528,128]{2,1,0:T(8,128)(2,1)S(1)} %bitcast.16), channel_id=1, replica_groups=mesh['blk'=16,'grid'=8] {'blk'}, dimensions={0} | all-to-all | bytes 4325376 | tf_op jit(solution)/shard_map/all_to_all | solution.py:413
  41.9 0.0 copy-done
  41.9 0.0 copy-done.1
  41.9 0.0 copy-done.2
  41.9 6.9 %shard_map.92 = bf16[8192,128]{1,0:T(8,128)(2,1)S(1)} custom-call(s32[1,1,768]{2,1,0:T(1,128)S(1)} %copy-done.2, bf16[8448,128]{1,0:T(8,128)(2,1)S(1)} %bitcast.13, bf16[256,128]{1,0:T(8,128)(2,1)S(1)} %copy-done, bf16[256,128]{1,0:T(8,128)(2,1)S(1)} %copy-done.1, bf16[256,128,128]{2,1,0:T(8,128)(2,1)S(1)} %get-tuple-element.14.refs_4_), custom_call_target="tpu_custom_call" | custom-call | tf_op jit(solution)/shard_map/pallas_call | solution.py:246
  48.8 0.0 copy-start.4
  48.8 30.3 %all_to_all.11 = bf16[16,512,128]{2,1,0:T(8,128)(2,1)S(1)} all-to-all(bf16[16,512,128]{2,1,0:T(8,128)(2,1)S(1)} %bitcast.15), channel_id=1, replica_groups=mesh['blk'=16,'grid'=8] {'blk'}, dimensions={0} | all-to-all | bytes 4194304 | tf_op jit(solution)/shard_map/all_to_all | solution.py:418
  79.1 1.4 %shard_map.94 = (bf16[128,128]{1,0:T(8,128)(2,1)S(1)}, bf16[128,128]{1,0:T(8,128)(2,1)S(1)}, bf16[32,128]{1,0:T(8,128)(2,1)S(1)}, bf16[32,128]{1,0:T(8,128)(2,1)S(1)}) custom-call(s32[1]{0:T(128)} %bitcast.refs_0_, s32[32,128]{1,0:T(8,128)S(1)} %get-tuple-element.12.code_ref.refs_1_, bf16[8192,128]{1,0:T(8,128)(2,1)S(1)} %bitcast.11), custom_call_target="tpu_custom_call" | custom-call | tf_op jit(solution)/shard_map/pallas_call | solution.py:293
  80.5 0.0 copy-start.3
  80.5 0.1 collective-permute-start
  80.6 2.4 %collective-permute-start.1 = (bf16[128,128]{1,0:T(8,128)(2,1)S(1)}, bf16[128,128]{1,0:T(8,128)(2,1)S(1)}, u32[]{:S(2)}, u32[]{:S(2)}) collective-permute-start(bf16[128,128]{1,0:T(8,128)(2,1)S(1)} %get-tuple-element.16), channel_id=1, source_target_pairs={{1,2},{3,4},{5,6},{2,1},{4,3},{6,5},{9,10},{11,12},{13,14},{10,9},... | collective-permute-start | bytes 98312 | tf_op jit(solution)/shard_map/ppermute | solution.py:401
  83.0 1.2 %collective-permute-start.2 = (bf16[32,128]{1,0:T(8,128)(2,1)S(1)}, bf16[32,128]{1,0:T(8,128)(2,1)S(1)}, u32[]{:S(2)}, u32[]{:S(2)}) collective-permute-start(bf16[32,128]{1,0:T(8,128)(2,1)S(1)} %get-tuple-element.17), channel_id=1, source_target_pairs={{0,8},{16,24},{32,40},{48,56},{64,72},{80,88},{96,104},{112,120},{... | collective-permute-start | bytes 24584 | tf_op jit(solution)/shard_map/ppermute | solution.py:401
  84.2 3.7 %collective-permute-start.3 = (bf16[32,128]{1,0:T(8,128)(2,1)S(1)}, bf16[32,128]{1,0:T(8,128)(2,1)S(1)}, u32[]{:S(2)}, u32[]{:S(2)}) collective-permute-start(bf16[32,128]{1,0:T(8,128)(2,1)S(1)} %get-tuple-element.18), channel_id=1, source_target_pairs={{8,16},{24,32},{40,48},{56,64},{72,80},{88,96},{104,112},{16,8},{3... | collective-permute-start | bytes 24584 | tf_op jit(solution)/shard_map/ppermute | solution.py:401
  87.9 0.0 copy-done.4
  88.0 0.1 copy.10
  88.1 4.4 %shard_map.93 = f32[4096,128]{1,0:T(8,128)S(1)} custom-call(s32[32,128]{1,0:T(8,128)S(1)} %get-tuple-element.12.code_ref.refs_1_, bf16[8192,128]{1,0:T(8,128)(2,1)S(1)} %bitcast.12), custom_call_target="tpu_custom_call" | custom-call | bytes 16777216 | tf_op jit(solution)/shard_map/pallas_call | solution.py:321
  92.5 0.0 collective-permute-done.2.refs_4_
  92.5 0.0 collective-permute-done.3.refs_5_
  92.5 0.0 collective-permute-done.refs_2_
  92.5 0.0 collective-permute-done.1.refs_3_
  92.5 0.0 copy-done.3
  92.6 1.8 %shard_map.95 = f32[32,128,128]{2,1,0:T(8,128)} custom-call(s32[1]{0:T(128)} %bitcast.refs_0_, f32[32,128,128]{2,1,0:T(8,128)S(1)} %bitcast.14, bf16[128,128]{1,0:T(8,128)(2,1)S(1)} %collective-permute-done.refs_2_, bf16[128,128]{1,0:T(8,128)(2,1)S(1)} %collective-permute-done.1.refs_3_, bf16[32,128]{1,0:T(8,128)(2,1)S(1)} %collective-permute-done.2.refs_4_, ...), custom_call_target="tpu_custom_call" | custom-call | tf_op jit(solution)/shard_map/pallas_call | solution.py:385
Async XLA Ops:
  6.5 35.4 %copy-start = (bf16[256,128]{1,0:T(8,128)(2,1)S(1)}, bf16[256,128]{1,0:T(8,128)(2,1)}, u32[]{:S(2)}) copy-start(bf16[256,128]{1,0:T(8,128)(2,1)} %refs_2_.1) | copy-start | bytes 196612
  6.5 35.4 %copy-start.1 = (bf16[256,128]{1,0:T(8,128)(2,1)S(1)}, bf16[256,128]{1,0:T(8,128)(2,1)}, u32[]{:S(2)}) copy-start(bf16[256,128]{1,0:T(8,128)(2,1)} %refs_3_.1) | copy-start | bytes 196612
  6.5 35.4 %copy-start.2 = (s32[1,1,768]{2,1,0:T(1,128)S(1)}, s32[1,1,768]{2,1,0:T(1,128)}, u32[]{:S(2)}) copy-start(s32[1,1,768]{2,1,0:T(1,128)} %refs_0_.1) | copy-start | bytes 9220
  48.8 39.1 %copy-start.4 = (f32[32,128]{1,0:T(8,128)S(1)}, f32[32,128]{1,0:T(8,128)}, u32[]{:S(2)}) copy-start(f32[32,128]{1,0:T(8,128)} %param.10) | copy-start | bytes 49156
  80.5 12.0 %copy-start.3 = (f32[128]{0:T(128)S(1)}, f32[128]{0:T(128)}, u32[]{:S(2)}) copy-start(f32[128]{0:T(128)} %param.11) | copy-start | bytes 1540
  80.5 12.0 %collective-permute-start = (bf16[128,128]{1,0:T(8,128)(2,1)S(1)}, bf16[128,128]{1,0:T(8,128)(2,1)S(1)}, u32[]{:S(2)}, u32[]{:S(2)}) collective-permute-start(bf16[128,128]{1,0:T(8,128)(2,1)S(1)} %get-tuple-element.15), channel_id=1, source_target_pairs={{0,1},{2,3},{4,5},{6,7},{1,0},{3,2},{5,4},{7,6},{8,9},{10,11},{12,... | collective-permute-start | bytes 98312 | tf_op jit(solution)/shard_map/ppermute | solution.py:401
  80.6 11.9 %collective-permute-start.1 = (bf16[128,128]{1,0:T(8,128)(2,1)S(1)}, bf16[128,128]{1,0:T(8,128)(2,1)S(1)}, u32[]{:S(2)}, u32[]{:S(2)}) collective-permute-start(bf16[128,128]{1,0:T(8,128)(2,1)S(1)} %get-tuple-element.16), channel_id=1, source_target_pairs={{1,2},{3,4},{5,6},{2,1},{4,3},{6,5},{9,10},{11,12},{13,14},{10,9},... | collective-permute-start | bytes 98312 | tf_op jit(solution)/shard_map/ppermute | solution.py:401
  83.0 9.5 %collective-permute-start.2 = (bf16[32,128]{1,0:T(8,128)(2,1)S(1)}, bf16[32,128]{1,0:T(8,128)(2,1)S(1)}, u32[]{:S(2)}, u32[]{:S(2)}) collective-permute-start(bf16[32,128]{1,0:T(8,128)(2,1)S(1)} %get-tuple-element.17), channel_id=1, source_target_pairs={{0,8},{16,24},{32,40},{48,56},{64,72},{80,88},{96,104},{112,120},{... | collective-permute-start | bytes 24584 | tf_op jit(solution)/shard_map/ppermute | solution.py:401
  84.2 8.3 %collective-permute-start.3 = (bf16[32,128]{1,0:T(8,128)(2,1)S(1)}, bf16[32,128]{1,0:T(8,128)(2,1)S(1)}, u32[]{:S(2)}, u32[]{:S(2)}) collective-permute-start(bf16[32,128]{1,0:T(8,128)(2,1)S(1)} %get-tuple-element.18), channel_id=1, source_target_pairs={{8,16},{24,32},{40,48},{56,64},{72,80},{88,96},{104,112},{16,8},{3... | collective-permute-start | bytes 24584 | tf_op jit(solution)/shard_map/ppermute | solution.py:401

commit v7 on v6

--- a/solution.py
+++ b/solution.py
@@ -51,7 +51,8 @@
     fetch.start()
     before = zero_one(iota((width, width), 0) < iota((width, width), 1))
     weights = jnp.concatenate([jnp.ones((width, width), BF16), before], axis=0)
-    earlier = zero_one(iota((width, nblocks), 1) < iota((width, nblocks), 0))
+    earlier = zero_one(iota((nblocks, nblocks), 1) < iota((nblocks, nblocks), 0))
+    starts = zero_one(iota((nblocks, width), 0) < iota((nblocks, width), 1))
     ones = jnp.ones((META, width), BF16)
     top = iota((META, width), 0) == 0
     loads[0].wait()
@@ -64,19 +65,13 @@
     ahead = [dot(earlier, mask).astype(BF16) for mask in masks]
     ranks = dot(
         jnp.concatenate(
-            [jnp.concatenate([a[:nblocks], m], axis=1) for a, m in zip(ahead, masks)], axis=0
+            [jnp.concatenate([a, m], axis=1) for a, m in zip(ahead, masks)], axis=0
         ),
         weights,
     )
-    begins = dot_nt(ones, jnp.concatenate(ahead, axis=0))
     place = jnp.zeros((nblocks, width), F32)
     for part in range(nparts):
         place = place + jnp.where(mine[part], ranks[part * nblocks : (part + 1) * nblocks], 0.0)
-        begin = begins[:, part * width : (part + 1) * width]
-        high = jnp.floor(begin * (1.0 / 16.0))
-        send_ref[pl.ds(part * SEG + CAP, META), :] = jnp.where(
-            top, high, begin - 16.0 * high
-        ).astype(BF16)
     spot = owner * CAP + place.astype(jnp.int32)
     spot_high = (spot >> 7).astype(F32)
     spot_low = (spot & 127).astype(F32)
@@ -105,6 +100,14 @@
     code_vmem[...] = back + (back >> 9) * META
     copy = pltpu.make_async_copy(code_vmem, code_smem, sems.at[3])
     copy.start()
+    counts = jnp.concatenate([dot_nt(ones, mask) for mask in masks], axis=0).astype(BF16)
+    begins = dot(counts, starts)
+    for part in range(nparts):
+        begin = begins[part * META : (part + 1) * META]
+        high = jnp.floor(begin * (1.0 / 16.0))
+        send_ref[pl.ds(part * SEG + CAP, META), :] = jnp.where(
+            top, high, begin - 16.0 * high
+        ).astype(BF16)
     loads[2].wait()
     field[...] = state_ref[...].astype(F32)
     copy.wait()
@@ -152,14 +155,17 @@
 
 def react_kernel(
     nparts, nblocks, entries_ref, recv_ref, value_ref, base_ref, sens_ref, out_ref,
-    rows, mapped, table, begin_vmem, begin_smem, sem,
+    rows, mapped, table, begin_vmem, begin_smem, next_vmem, next_smem, sems,
 ):
     width = recv_ref.shape[1]
     depth = base_ref.shape[0]
     for part in range(nparts):
         meta = recv_ref[pl.ds(part * SEG + CAP, META), :].astype(F32)
         begin_vmem[pl.ds(part, 1), :] = (meta[0:1] * 16.0 + meta[1:2]).astype(jnp.int32)
-    begin = begin_vmem[pl.ds(0, nparts), :]
+    begin = begin_vmem[...]
+    begin_vmem[...] = begin + SEG * iota((nparts, width), 0)
+    copy = pltpu.make_async_copy(begin_vmem, begin_smem, sems.at[0])
+    copy.start()
     lane = iota((nparts, width), 1)
     counts = pltpu.roll(begin, width - 1, 1) - begin
     end = width - 1
@@ -169,10 +175,9 @@
         moved = pltpu.roll(following, width - ahead, 1)
         following = jnp.minimum(following, jnp.where(lane + ahead < width, moved, end))
         ahead *= 2
-    begin_vmem[pl.ds(0, nparts), :] = begin + SEG * iota((nparts, width), 0)
-    begin_vmem[pl.ds(nparts, nparts), :] = pltpu.roll(following, end, 1)
-    copy = pltpu.make_async_copy(begin_vmem, begin_smem, sem)
-    copy.start()
+    next_vmem[...] = pltpu.roll(following, end, 1)
+    chain = pltpu.make_async_copy(next_vmem, next_smem, sems.at[1])
+    chain.start()
     table[pl.ds(0, depth), :] = base_ref[...].astype(F32)
     table[pl.ds(depth, depth), :] = value_ref[...].astype(F32)
 
@@ -224,11 +229,12 @@
                 return here + WIN
 
             lax.while_loop(lambda here: here < stop, more, at + WIN)
-            return begin_smem[nparts + part, k]
-
-        lax.while_loop(lambda k: k < end, group, begin_smem[nparts + part, end])
-        return 0
-
+            return next_smem[part, k]
+
+        lax.while_loop(lambda k: k < end, group, next_smem[part, end])
+        return 0
+
+    chain.wait()
     lax.fori_loop(0, nparts, rest, 0)
 
     def narrow(part, _):
@@ -253,9 +259,11 @@
             pltpu.VMEM((nparts * SEG + WIN, width), F32),
             pltpu.VMEM((nparts * SEG + WIN, width), F32),
             pltpu.VMEM((2 * base.shape[0], width), F32),
-            pltpu.VMEM((2 * nparts, width), jnp.int32),
-            pltpu.SMEM((2 * nparts, width), jnp.int32),
-            pltpu.SemaphoreType.DMA,
+            pltpu.VMEM((nparts, width), jnp.int32),
+            pltpu.SMEM((nparts, width), jnp.int32),
+            pltpu.VMEM((nparts, width), jnp.int32),
+            pltpu.SMEM((nparts, width), jnp.int32),
+            pltpu.SemaphoreType.DMA((2,)),
         ],
         compiler_params=pltpu.CompilerParams(vmem_limit_bytes=24 << 20),
     )(entries, recv, value, base, sens)
@@ -333,17 +341,20 @@
 
 
 def transport_kernel(
-    lines, me_ref, mid_ref, along1_ref, along2_ref, across1_ref, across2_ref,
+    nparts, lines, me_ref, mid_ref, along1_ref, along2_ref, across1_ref, across2_ref,
     courant_ref, diffusion_ref, out_hbm, out_ref, sems,
 ):
     rows_here, cols, width = mid_ref.shape
 
-    def sides(odd, one, two):
+    def sides(at, count, one, two):
         one, two = one[...].astype(F32), two[...].astype(F32)
-        return jnp.where(odd == 1, one, two), jnp.where(odd == 1, two, one)
-
-    up, down = sides(me_ref[0] & 1, along1_ref, along2_ref)
-    left_side, right_side = sides((me_ref[0] // lines) & 1, across1_ref, across2_ref)
+        odd = (at & 1) == 1
+        before, behind = jnp.where(odd, one, two), jnp.where(odd, two, one)
+        return jnp.where(at > 0, before, 0.0), jnp.where(at < count - 1, behind, 0.0)
+
+    across, along = me_ref[0] // lines, me_ref[0] & (lines - 1)
+    up, down = sides(along, lines, along1_ref, along2_ref)
+    left_side, right_side = sides(across, nparts, across1_ref, across2_ref)
     diffusion = diffusion_ref[...]
     first = iota((cols, width), 0) == 0
     last = iota((cols, width), 0) == cols - 1
@@ -380,10 +391,10 @@
         store.wait()
 
 
-def transport(me, lines, reacted, halo, courant, diffusion):
+def transport(me, nparts, lines, reacted, halo, courant, diffusion):
     shape = reacted.shape
     return pl.pallas_call(
-        lambda *refs: transport_kernel(lines, *refs),
+        lambda *refs: transport_kernel(nparts, lines, *refs),
         out_shape=jax.ShapeDtypeStruct(shape, F32),
         in_specs=[pl.BlockSpec(memory_space=pltpu.SMEM)]
         + [pl.BlockSpec(memory_space=pltpu.VMEM)] * 7,
@@ -397,7 +408,8 @@
 
 
 def swapped(block, axis, first):
-    pairs = [(i, i + 1) for i in range(first, lax.axis_size(axis) - 1, 2)]
+    count = lax.axis_size(axis)
+    pairs = [(i, (i + 1) % count) for i in range(first, count, 2)]
     return lax.ppermute(block, axis, pairs + [(j, i) for i, j in pairs])
 
 
@@ -423,7 +435,7 @@
         swapped(across1, "blk", 0), swapped(across2, "blk", 1),
     )
     reacted = unpack(code, back).reshape(rows_here, cols_here, width)
-    return transport(me, lines, reacted, halo, courant.T, diffusion.reshape(1, width))
+    return transport(me, nparts, lines, reacted, halo, courant.T, diffusion.reshape(1, width))
 
 
 def solution(mesh):

time: 96.1 us -> 95.5 us (level)
  the two profiles are of different devices: /device:TPU:30 before, /device:TPU:0 now
where the time goes in v7:
time: 95.5 us; the launch traced here: 95.2 us
  blocking collectives  68.2 us (71%)
  Pallas kernels  20.7 us (22%)
  starting transfers between devices  4.82 us (5%)
  waiting for transfers between devices  1.22 us (1%)
    all_to_all x1, blocking collectives, local(): lax.all_to_all(send.reshape(nparts, SEG, width), 'blk', 0, 0, tiled=True)  37 us
    all_to_all x1, blocking collectives, local(): lax.all_to_all(done.reshape(nparts, CAP, width), 'blk', 0, 0, tiled=True)  31.2 us
    pallas_call x1, Pallas kernels, pack(): pl.pallas_call(lambda *refs: pack_kernel(nparts, lines, *refs), out_shape...  6.52 us
    pallas_call x1, Pallas kernels, react(): pl.pallas_call(lambda *refs: react_kernel(nparts, nblocks, *refs), out_sh...  6.47 us
    ppermute x4, starting transfers between devices, swapped(): return lax.ppermute(block, axis, pairs + [(j, i) for i, j in pairs])  4.82 us
    pallas_call x1, Pallas kernels, unpack(): pl.pallas_call(unpack_kernel, out_shape=jax.ShapeDtypeStruct((cells, widt...  4.45 us
  transfers between devices with their start and end apart: 4, of which 1 were waited for; matrix products, arithmetic and copies ran while one was open for 0% of the time, Pallas kernels for 5%

profile of v7, /device:TPU:0, one launch (start us, length us, event | category | flops | bytes accessed | tf_op | source)
XLA Modules:
  0.0 95.2 jit_solution(7621392540860292412)
XLA Ops:
  0.0 6.5 %shard_map.91 = (bf16[8448,128]{1,0:T(8,128)(2,1)S(1)}, s32[32,128]{1,0:T(8,128)S(1)}, bf16[256,128,128]{2,1,0:T(8,128)(2,1)S(1)}) custom-call(s32[1]{0:T(128)} %bitcast.refs_0_, s32[48,128]{1,0:T(8,128)} %bitcast.20, s32[48,128]{1,0:T(8,128)} %bitcast.21, bf16[4096,128]{1,0:T(8,128)(2,1)} %bitcast.19, bf16[256,128,128]{2,1,0:T(8,128)(2,1)} %refs_4_.1), custom_call_target="tpu_custom_call" | custom-call | tf_op jit(solution)/shard_map/pallas_call | solution.py:132
  6.5 0.0 copy-start
  6.5 0.0 copy-start.1
  6.6 0.0 copy-start.2
  6.6 37.0 %all_to_all.10 = bf16[16,528,128]{2,1,0:T(8,128)(2,1)S(1)} all-to-all(bf16[16,528,128]{2,1,0:T(8,128)(2,1)S(1)} %bitcast.16), channel_id=1, replica_groups=mesh['blk'=16,'grid'=8] {'blk'}, dimensions={0} | all-to-all | bytes 4325376 | tf_op jit(solution)/shard_map/all_to_all | solution.py:425
  43.6 0.0 copy-done
  43.6 0.0 copy-done.1
  43.6 0.0 copy-done.2
  43.6 6.5 %shard_map.92 = bf16[8192,128]{1,0:T(8,128)(2,1)S(1)} custom-call(s32[1,1,768]{2,1,0:T(1,128)S(1)} %copy-done.2, bf16[8448,128]{1,0:T(8,128)(2,1)S(1)} %bitcast.13, bf16[256,128]{1,0:T(8,128)(2,1)S(1)} %copy-done, bf16[256,128]{1,0:T(8,128)(2,1)S(1)} %copy-done.1, bf16[256,128,128]{2,1,0:T(8,128)(2,1)S(1)} %get-tuple-element.14.refs_4_), custom_call_target="tpu_custom_call" | custom-call | tf_op jit(solution)/shard_map/pallas_call | solution.py:252
  50.1 0.0 copy-start.4
  50.1 31.2 %all_to_all.11 = bf16[16,512,128]{2,1,0:T(8,128)(2,1)S(1)} all-to-all(bf16[16,512,128]{2,1,0:T(8,128)(2,1)S(1)} %bitcast.15), channel_id=1, replica_groups=mesh['blk'=16,'grid'=8] {'blk'}, dimensions={0} | all-to-all | bytes 4194304 | tf_op jit(solution)/shard_map/all_to_all | solution.py:430
  81.3 1.4 %shard_map.94 = (bf16[128,128]{1,0:T(8,128)(2,1)S(1)}, bf16[128,128]{1,0:T(8,128)(2,1)S(1)}, bf16[32,128]{1,0:T(8,128)(2,1)S(1)}, bf16[32,128]{1,0:T(8,128)(2,1)S(1)}) custom-call(s32[1]{0:T(128)} %bitcast.refs_0_, s32[32,128]{1,0:T(8,128)S(1)} %get-tuple-element.12.code_ref.refs_1_, bf16[8192,128]{1,0:T(8,128)(2,1)S(1)} %bitcast.11), custom_call_target="tpu_custom_call" | custom-call | tf_op jit(solution)/shard_map/pallas_call | solution.py:301
  82.7 0.0 copy-start.3
  82.7 0.1 collective-permute-start
  82.8 3.1 %collective-permute-start.1 = (bf16[128,128]{1,0:T(8,128)(2,1)S(1)}, bf16[128,128]{1,0:T(8,128)(2,1)S(1)}, u32[]{:S(2)}, u32[]{:S(2)}) collective-permute-start(bf16[128,128]{1,0:T(8,128)(2,1)S(1)} %get-tuple-element.16), channel_id=1, source_target_pairs={{1,2},{3,4},{5,6},{7,0},{2,1},{4,3},{6,5},{0,7},{9,10},{11,12},{13... | collective-permute-start | bytes 98312 | tf_op jit(solution)/shard_map/ppermute | solution.py:413
  86.0 0.4 collective-permute-start.2
  86.4 1.2 %collective-permute-start.3 = (bf16[32,128]{1,0:T(8,128)(2,1)S(1)}, bf16[32,128]{1,0:T(8,128)(2,1)S(1)}, u32[]{:S(2)}, u32[]{:S(2)}) collective-permute-start(bf16[32,128]{1,0:T(8,128)(2,1)S(1)} %get-tuple-element.18), channel_id=1, source_target_pairs={{8,16},{24,32},{40,48},{56,64},{72,80},{88,96},{104,112},{120,0},{... | collective-permute-start | bytes 24584 | tf_op jit(solution)/shard_map/ppermute | solution.py:413
  87.6 0.0 copy-done.4
  87.6 0.1 copy.10
  87.7 4.4 %shard_map.93 = f32[4096,128]{1,0:T(8,128)S(1)} custom-call(s32[32,128]{1,0:T(8,128)S(1)} %get-tuple-element.12.code_ref.refs_1_, bf16[8192,128]{1,0:T(8,128)(2,1)S(1)} %bitcast.12), custom_call_target="tpu_custom_call" | custom-call | bytes 16777216 | tf_op jit(solution)/shard_map/pallas_call | solution.py:329
  92.1 0.0 collective-permute-done.2.refs_4_
  92.1 1.2 %collective-permute-done.3.refs_5_ = bf16[32,128]{1,0:T(8,128)(2,1)S(1)} collective-permute-done((bf16[32,128]{1,0:T(8,128)(2,1)S(1)}, bf16[32,128]{1,0:T(8,128)(2,1)S(1)}, u32[]{:S(2)}, u32[]{:S(2)}) %collective-permute-start.3) | collective-permute-done | bytes 8224 | tf_op jit(solution)/shard_map/ppermute | solution.py:413
  93.3 0.0 collective-permute-done.refs_2_
  93.3 0.0 collective-permute-done.1.refs_3_
  93.4 0.0 copy-done.3
  93.4 1.8 %shard_map.95 = f32[32,128,128]{2,1,0:T(8,128)} custom-call(s32[1]{0:T(128)} %bitcast.refs_0_, f32[32,128,128]{2,1,0:T(8,128)S(1)} %bitcast.14, bf16[128,128]{1,0:T(8,128)(2,1)S(1)} %collective-permute-done.refs_2_, bf16[128,128]{1,0:T(8,128)(2,1)S(1)} %collective-permute-done.1.refs_3_, bf16[32,128]{1,0:T(8,128)(2,1)S(1)} %collective-permute-done.2.refs_4_, ...), custom_call_target="tpu_custom_call" | custom-call | tf_op jit(solution)/shard_map/pallas_call | solution.py:396
Async XLA Ops:
  6.5 37.1 %copy-start = (bf16[256,128]{1,0:T(8,128)(2,1)S(1)}, bf16[256,128]{1,0:T(8,128)(2,1)}, u32[]{:S(2)}) copy-start(bf16[256,128]{1,0:T(8,128)(2,1)} %refs_2_.1) | copy-start | bytes 196612
  6.5 37.0 %copy-start.1 = (bf16[256,128]{1,0:T(8,128)(2,1)S(1)}, bf16[256,128]{1,0:T(8,128)(2,1)}, u32[]{:S(2)}) copy-start(bf16[256,128]{1,0:T(8,128)(2,1)} %refs_3_.1) | copy-start | bytes 196612
  6.6 37.0 %copy-start.2 = (s32[1,1,768]{2,1,0:T(1,128)S(1)}, s32[1,1,768]{2,1,0:T(1,128)}, u32[]{:S(2)}) copy-start(s32[1,1,768]{2,1,0:T(1,128)} %refs_0_.1) | copy-start | bytes 9220
  50.1 37.5 %copy-start.4 = (f32[32,128]{1,0:T(8,128)S(1)}, f32[32,128]{1,0:T(8,128)}, u32[]{:S(2)}) copy-start(f32[32,128]{1,0:T(8,128)} %param.10) | copy-start | bytes 49156
  82.7 10.6 %copy-start.3 = (f32[128]{0:T(128)S(1)}, f32[128]{0:T(128)}, u32[]{:S(2)}) copy-start(f32[128]{0:T(128)} %param.11) | copy-start | bytes 1540
  82.7 10.6 %collective-permute-start = (bf16[128,128]{1,0:T(8,128)(2,1)S(1)}, bf16[128,128]{1,0:T(8,128)(2,1)S(1)}, u32[]{:S(2)}, u32[]{:S(2)}) collective-permute-start(bf16[128,128]{1,0:T(8,128)(2,1)S(1)} %get-tuple-element.15), channel_id=1, source_target_pairs={{0,1},{2,3},{4,5},{6,7},{1,0},{3,2},{5,4},{7,6},{8,9},{10,11},{12,... | collective-permute-start | bytes 98312 | tf_op jit(solution)/shard_map/ppermute | solution.py:413
  82.8 10.5 %collective-permute-start.1 = (bf16[128,128]{1,0:T(8,128)(2,1)S(1)}, bf16[128,128]{1,0:T(8,128)(2,1)S(1)}, u32[]{:S(2)}, u32[]{:S(2)}) collective-permute-start(bf16[128,128]{1,0:T(8,128)(2,1)S(1)} %get-tuple-element.16), channel_id=1, source_target_pairs={{1,2},{3,4},{5,6},{7,0},{2,1},{4,3},{6,5},{0,7},{9,10},{11,12},{13... | collective-permute-start | bytes 98312 | tf_op jit(solution)/shard_map/ppermute | solution.py:413
  86.0 6.2 %collective-permute-start.2 = (bf16[32,128]{1,0:T(8,128)(2,1)S(1)}, bf16[32,128]{1,0:T(8,128)(2,1)S(1)}, u32[]{:S(2)}, u32[]{:S(2)}) collective-permute-start(bf16[32,128]{1,0:T(8,128)(2,1)S(1)} %get-tuple-element.17), channel_id=1, source_target_pairs={{0,8},{16,24},{32,40},{48,56},{64,72},{80,88},{96,104},{112,120},{... | collective-permute-start | bytes 24584 | tf_op jit(solution)/shard_map/ppermute | solution.py:413
  86.4 7.0 %collective-permute-start.3 = (bf16[32,128]{1,0:T(8,128)(2,1)S(1)}, bf16[32,128]{1,0:T(8,128)(2,1)S(1)}, u32[]{:S(2)}, u32[]{:S(2)}) collective-permute-start(bf16[32,128]{1,0:T(8,128)(2,1)S(1)} %get-tuple-element.18), channel_id=1, source_target_pairs={{8,16},{24,32},{40,48},{56,64},{72,80},{88,96},{104,112},{120,0},{... | collective-permute-start | bytes 24584 | tf_op jit(solution)/shard_map/ppermute | solution.py:413

commit v8 on v7

--- a/solution.py
+++ b/solution.py
@@ -120,7 +120,7 @@
                 packed[pl.ds(at, 1), :] = value
         return 0
 
-    lax.fori_loop(0, rows_here, line, 0)
+    lax.fori_loop(0, rows_here, line, 0, unroll=2)
     for part in range(nparts):
         send_ref[pl.ds(part * SEG, CAP), :] = packed[pl.ds(part * SEG, CAP), :].astype(BF16)
     fetch.wait()
@@ -178,8 +178,8 @@
     next_vmem[...] = pltpu.roll(following, end, 1)
     chain = pltpu.make_async_copy(next_vmem, next_smem, sems.at[1])
     chain.start()
-    table[pl.ds(0, depth), :] = base_ref[...].astype(F32)
-    table[pl.ds(depth, depth), :] = value_ref[...].astype(F32)
+    table[:, 0:1, :] = base_ref[...].astype(F32).reshape(depth, 1, width)
+    table[:, 1:2, :] = value_ref[...].astype(F32).reshape(depth, 1, width)
 
     def widen(part, _):
         at = pl.multiple_of(part * SEG, 16)
@@ -190,7 +190,7 @@
     copy.wait()
 
     def delta(at, entry):
-        base = table[pl.ds(entry, 1), :]
+        base = table[entry, 0:1, :]
         return rows[pl.ds(at, WIN), :] - base
 
     def batch(part, first):
@@ -203,8 +203,8 @@
                 jnp.concatenate([dx[i], dx[i + 1]], axis=0).astype(BF16),
                 jnp.concatenate([sens_ref[entry[i]], sens_ref[entry[i + 1]]], axis=1),
             )
-            results.append(product[:WIN, :width] + table[pl.ds(entry[i] + depth, 1), :])
-            results.append(product[WIN:, width:] + table[pl.ds(entry[i + 1] + depth, 1), :])
+            results.append(product[:WIN, :width] + table[entry[i], 1:2, :])
+            results.append(product[WIN:, width:] + table[entry[i + 1], 1:2, :])
         for i in range(GROUPS):
             mapped[pl.ds(at[i], WIN), :] = results[i]
 
@@ -222,7 +222,7 @@
 
             def more(here):
                 result = dot(delta(here, entry).astype(BF16), sens_ref[entry])
-                result = result + table[pl.ds(entry + depth, 1), :]
+                result = result + table[entry, 1:2, :]
                 mapped[pl.ds(here, WIN), :] = jnp.where(
                     iota((WIN, width), 0) < stop - here, result, mapped[pl.ds(here, WIN), :]
                 )
@@ -258,7 +258,7 @@
         scratch_shapes=[
             pltpu.VMEM((nparts * SEG + WIN, width), F32),
             pltpu.VMEM((nparts * SEG + WIN, width), F32),
-            pltpu.VMEM((2 * base.shape[0], width), F32),
+            pltpu.VMEM((base.shape[0], 8, width), F32),
             pltpu.VMEM((nparts, width), jnp.int32),
             pltpu.SMEM((nparts, width), jnp.int32),
             pltpu.VMEM((nparts, width), jnp.int32),
@@ -321,7 +321,7 @@
                 out_ref[pl.ds(i * width + q + j, 1), :] = value
         return 0
 
-    lax.fori_loop(0, rows_here, line, 0)
+    lax.fori_loop(0, rows_here, line, 0, unroll=2)
 
 
 def unpack(code, ret):

time: 95.5 us -> 95.3 us (level)
  no operation moved by 1% of the time
where the time goes in v8:
time: 95.3 us; the launch traced here: 95 us
  blocking collectives  68.2 us (72%)
  Pallas kernels  20.4 us (21%)
  starting transfers between devices  4.85 us (5%)
  waiting for transfers between devices  1.33 us (1%)
    all_to_all x1, blocking collectives, local(): lax.all_to_all(send.reshape(nparts, SEG, width), 'blk', 0, 0, tiled=True)  37 us
    all_to_all x1, blocking collectives, local(): lax.all_to_all(done.reshape(nparts, CAP, width), 'blk', 0, 0, tiled=True)  31.2 us
    pallas_call x1, Pallas kernels, pack(): pl.pallas_call(lambda *refs: pack_kernel(nparts, lines, *refs), out_shape...  6.45 us
    pallas_call x1, Pallas kernels, react(): pl.pallas_call(lambda *refs: react_kernel(nparts, nblocks, *refs), out_sh...  6.28 us
    ppermute x4, starting transfers between devices, swapped(): return lax.ppermute(block, axis, pairs + [(j, i) for i, j in pairs])  4.85 us
    pallas_call x1, Pallas kernels, unpack(): pl.pallas_call(unpack_kernel, out_shape=jax.ShapeDtypeStruct((cells, widt...  4.38 us
  transfers between devices with their start and end apart: 4, of which 1 were waited for; matrix products, arithmetic and copies ran while one was open for 0% of the time, Pallas kernels for 5%

profile of v8, /device:TPU:0, one launch (start us, length us, event | category | flops | bytes accessed | tf_op | source)
XLA Modules:
  0.0 95.0 jit_solution(15061209646897168099)
XLA Ops:
  0.0 6.4 %shard_map.91 = (bf16[8448,128]{1,0:T(8,128)(2,1)S(1)}, s32[32,128]{1,0:T(8,128)S(1)}, bf16[256,128,128]{2,1,0:T(8,128)(2,1)S(1)}) custom-call(s32[1]{0:T(128)} %bitcast.refs_0_, s32[48,128]{1,0:T(8,128)} %bitcast.20, s32[48,128]{1,0:T(8,128)} %bitcast.21, bf16[4096,128]{1,0:T(8,128)(2,1)} %bitcast.19, bf16[256,128,128]{2,1,0:T(8,128)(2,1)} %refs_4_.1), custom_call_target="tpu_custom_call" | custom-call | tf_op jit(solution)/shard_map/pallas_call | solution.py:132
  6.5 0.0 copy-start
  6.5 0.0 copy-start.1
  6.5 0.0 copy-start.2
  6.5 37.0 %all_to_all.10 = bf16[16,528,128]{2,1,0:T(8,128)(2,1)S(1)} all-to-all(bf16[16,528,128]{2,1,0:T(8,128)(2,1)S(1)} %bitcast.16), channel_id=1, replica_groups=mesh['blk'=16,'grid'=8] {'blk'}, dimensions={0} | all-to-all | bytes 4325376 | tf_op jit(solution)/shard_map/all_to_all | solution.py:425
  43.5 0.0 copy-done
  43.5 0.0 copy-done.1
  43.5 0.0 copy-done.2
  43.5 6.3 %shard_map.92 = bf16[8192,128]{1,0:T(8,128)(2,1)S(1)} custom-call(s32[1,1,768]{2,1,0:T(1,128)S(1)} %copy-done.2, bf16[8448,128]{1,0:T(8,128)(2,1)S(1)} %bitcast.13, bf16[256,128]{1,0:T(8,128)(2,1)S(1)} %copy-done, bf16[256,128]{1,0:T(8,128)(2,1)S(1)} %copy-done.1, bf16[256,128,128]{2,1,0:T(8,128)(2,1)S(1)} %get-tuple-element.14.refs_4_), custom_call_target="tpu_custom_call" | custom-call | tf_op jit(solution)/shard_map/pallas_call | solution.py:252
  49.8 0.0 copy-start.4
  49.8 31.2 %all_to_all.11 = bf16[16,512,128]{2,1,0:T(8,128)(2,1)S(1)} all-to-all(bf16[16,512,128]{2,1,0:T(8,128)(2,1)S(1)} %bitcast.15), channel_id=1, replica_groups=mesh['blk'=16,'grid'=8] {'blk'}, dimensions={0} | all-to-all | bytes 4194304 | tf_op jit(solution)/shard_map/all_to_all | solution.py:430
  81.0 1.4 %shard_map.94 = (bf16[128,128]{1,0:T(8,128)(2,1)S(1)}, bf16[128,128]{1,0:T(8,128)(2,1)S(1)}, bf16[32,128]{1,0:T(8,128)(2,1)S(1)}, bf16[32,128]{1,0:T(8,128)(2,1)S(1)}) custom-call(s32[1]{0:T(128)} %bitcast.refs_0_, s32[32,128]{1,0:T(8,128)S(1)} %get-tuple-element.12.code_ref.refs_1_, bf16[8192,128]{1,0:T(8,128)(2,1)S(1)} %bitcast.11), custom_call_target="tpu_custom_call" | custom-call | tf_op jit(solution)/shard_map/pallas_call | solution.py:301
  82.5 0.0 copy-start.3
  82.5 0.1 collective-permute-start
  82.6 3.2 %collective-permute-start.1 = (bf16[128,128]{1,0:T(8,128)(2,1)S(1)}, bf16[128,128]{1,0:T(8,128)(2,1)S(1)}, u32[]{:S(2)}, u32[]{:S(2)}) collective-permute-start(bf16[128,128]{1,0:T(8,128)(2,1)S(1)} %get-tuple-element.16), channel_id=1, source_target_pairs={{1,2},{3,4},{5,6},{7,0},{2,1},{4,3},{6,5},{0,7},{9,10},{11,12},{13... | collective-permute-start | bytes 98312 | tf_op jit(solution)/shard_map/ppermute | solution.py:413
  85.7 0.5 collective-permute-start.2
  86.2 1.2 %collective-permute-start.3 = (bf16[32,128]{1,0:T(8,128)(2,1)S(1)}, bf16[32,128]{1,0:T(8,128)(2,1)S(1)}, u32[]{:S(2)}, u32[]{:S(2)}) collective-permute-start(bf16[32,128]{1,0:T(8,128)(2,1)S(1)} %get-tuple-element.18), channel_id=1, source_target_pairs={{8,16},{24,32},{40,48},{56,64},{72,80},{88,96},{104,112},{120,0},{... | collective-permute-start | bytes 24584 | tf_op jit(solution)/shard_map/ppermute | solution.py:413
  87.3 0.0 copy-done.4
  87.3 0.1 copy.10
  87.4 4.4 %shard_map.93 = f32[4096,128]{1,0:T(8,128)S(1)} custom-call(s32[32,128]{1,0:T(8,128)S(1)} %get-tuple-element.12.code_ref.refs_1_, bf16[8192,128]{1,0:T(8,128)(2,1)S(1)} %bitcast.12), custom_call_target="tpu_custom_call" | custom-call | bytes 16777216 | tf_op jit(solution)/shard_map/pallas_call | solution.py:329
  91.8 0.0 collective-permute-done.2.refs_4_
  91.8 1.3 %collective-permute-done.3.refs_5_ = bf16[32,128]{1,0:T(8,128)(2,1)S(1)} collective-permute-done((bf16[32,128]{1,0:T(8,128)(2,1)S(1)}, bf16[32,128]{1,0:T(8,128)(2,1)S(1)}, u32[]{:S(2)}, u32[]{:S(2)}) %collective-permute-start.3) | collective-permute-done | bytes 8224 | tf_op jit(solution)/shard_map/ppermute | solution.py:413
  93.2 0.0 collective-permute-done.refs_2_
  93.2 0.0 collective-permute-done.1.refs_3_
  93.2 0.0 copy-done.3
  93.2 1.8 %shard_map.95 = f32[32,128,128]{2,1,0:T(8,128)} custom-call(s32[1]{0:T(128)} %bitcast.refs_0_, f32[32,128,128]{2,1,0:T(8,128)S(1)} %bitcast.14, bf16[128,128]{1,0:T(8,128)(2,1)S(1)} %collective-permute-done.refs_2_, bf16[128,128]{1,0:T(8,128)(2,1)S(1)} %collective-permute-done.1.refs_3_, bf16[32,128]{1,0:T(8,128)(2,1)S(1)} %collective-permute-done.2.refs_4_, ...), custom_call_target="tpu_custom_call" | custom-call | tf_op jit(solution)/shard_map/pallas_call | solution.py:396
Async XLA Ops:
  6.5 37.1 %copy-start = (bf16[256,128]{1,0:T(8,128)(2,1)S(1)}, bf16[256,128]{1,0:T(8,128)(2,1)}, u32[]{:S(2)}) copy-start(bf16[256,128]{1,0:T(8,128)(2,1)} %refs_2_.1) | copy-start | bytes 196612
  6.5 37.0 %copy-start.1 = (bf16[256,128]{1,0:T(8,128)(2,1)S(1)}, bf16[256,128]{1,0:T(8,128)(2,1)}, u32[]{:S(2)}) copy-start(bf16[256,128]{1,0:T(8,128)(2,1)} %refs_3_.1) | copy-start | bytes 196612
  6.5 37.0 %copy-start.2 = (s32[1,1,768]{2,1,0:T(1,128)S(1)}, s32[1,1,768]{2,1,0:T(1,128)}, u32[]{:S(2)}) copy-start(s32[1,1,768]{2,1,0:T(1,128)} %refs_0_.1) | copy-start | bytes 9220
  49.8 37.5 %copy-start.4 = (f32[32,128]{1,0:T(8,128)S(1)}, f32[32,128]{1,0:T(8,128)}, u32[]{:S(2)}) copy-start(f32[32,128]{1,0:T(8,128)} %param.10) | copy-start | bytes 49156
  82.5 10.7 %copy-start.3 = (f32[128]{0:T(128)S(1)}, f32[128]{0:T(128)}, u32[]{:S(2)}) copy-start(f32[128]{0:T(128)} %param.11) | copy-start | bytes 1540
  82.5 10.7 %collective-permute-start = (bf16[128,128]{1,0:T(8,128)(2,1)S(1)}, bf16[128,128]{1,0:T(8,128)(2,1)S(1)}, u32[]{:S(2)}, u32[]{:S(2)}) collective-permute-start(bf16[128,128]{1,0:T(8,128)(2,1)S(1)} %get-tuple-element.15), channel_id=1, source_target_pairs={{0,1},{2,3},{4,5},{6,7},{1,0},{3,2},{5,4},{7,6},{8,9},{10,11},{12,... | collective-permute-start | bytes 98312 | tf_op jit(solution)/shard_map/ppermute | solution.py:413
  82.6 10.6 %collective-permute-start.1 = (bf16[128,128]{1,0:T(8,128)(2,1)S(1)}, bf16[128,128]{1,0:T(8,128)(2,1)S(1)}, u32[]{:S(2)}, u32[]{:S(2)}) collective-permute-start(bf16[128,128]{1,0:T(8,128)(2,1)S(1)} %get-tuple-element.16), channel_id=1, source_target_pairs={{1,2},{3,4},{5,6},{7,0},{2,1},{4,3},{6,5},{0,7},{9,10},{11,12},{13... | collective-permute-start | bytes 98312 | tf_op jit(solution)/shard_map/ppermute | solution.py:413
  85.7 6.1 %collective-permute-start.2 = (bf16[32,128]{1,0:T(8,128)(2,1)S(1)}, bf16[32,128]{1,0:T(8,128)(2,1)S(1)}, u32[]{:S(2)}, u32[]{:S(2)}) collective-permute-start(bf16[32,128]{1,0:T(8,128)(2,1)S(1)} %get-tuple-element.17), channel_id=1, source_target_pairs={{0,8},{16,24},{32,40},{48,56},{64,72},{80,88},{96,104},{112,120},{... | collective-permute-start | bytes 24584 | tf_op jit(solution)/shard_map/ppermute | solution.py:413
  86.2 7.0 %collective-permute-start.3 = (bf16[32,128]{1,0:T(8,128)(2,1)S(1)}, bf16[32,128]{1,0:T(8,128)(2,1)S(1)}, u32[]{:S(2)}, u32[]{:S(2)}) collective-permute-start(bf16[32,128]{1,0:T(8,128)(2,1)S(1)} %get-tuple-element.18), channel_id=1, source_target_pairs={{8,16},{24,32},{40,48},{56,64},{72,80},{88,96},{104,112},{120,0},{... | collective-permute-start | bytes 24584 | tf_op jit(solution)/shard_map/ppermute | solution.py:413

commit v9 on v8

--- a/solution.py
+++ b/solution.py
@@ -344,7 +344,7 @@
     nparts, lines, me_ref, mid_ref, along1_ref, along2_ref, across1_ref, across2_ref,
     courant_ref, diffusion_ref, out_hbm, out_ref, sems,
 ):
-    rows_here, cols, width = mid_ref.shape
+    rows_here, cols, width = out_ref.shape
 
     def sides(at, count, one, two):
         one, two = one[...].astype(F32), two[...].astype(F32)
@@ -364,16 +364,22 @@
             return up
         if i >= rows_here:
             return down
-        return mid_ref[i]
+        return mid_ref[pl.ds(i * cols, cols), :]
 
     stores = []
     above, here = row(-1), row(0)
     for i in range(rows_here):
         below = row(i + 1)
-        left = jnp.where(first, left_side[i : i + 1, :], pltpu.roll(here, 1, 0))
-        right = jnp.where(
-            last, right_side[i : i + 1, :], pltpu.roll(here, cols - 1, 0)
-        )
+        if i == 0:
+            left = pltpu.roll(here, 1, 0)
+        else:
+            left = mid_ref[pl.ds(i * cols - 1, cols), :]
+        if i == rows_here - 1:
+            right = pltpu.roll(here, cols - 1, 0)
+        else:
+            right = mid_ref[pl.ds(i * cols + 1, cols), :]
+        left = jnp.where(first, left_side[i : i + 1, :], left)
+        right = jnp.where(last, right_side[i : i + 1, :], right)
         courant = courant_ref[:, i : i + 1]
         out_ref[i] = (
             here
@@ -392,7 +398,7 @@
 
 
 def transport(me, nparts, lines, reacted, halo, courant, diffusion):
-    shape = reacted.shape
+    shape = (*courant.shape[::-1], reacted.shape[1])
     return pl.pallas_call(
         lambda *refs: transport_kernel(nparts, lines, *refs),
         out_shape=jax.ShapeDtypeStruct(shape, F32),
@@ -434,7 +440,7 @@
         swapped(along1, "grid", 0), swapped(along2, "grid", 1),
         swapped(across1, "blk", 0), swapped(across2, "blk", 1),
     )
-    reacted = unpack(code, back).reshape(rows_here, cols_here, width)
+    reacted = unpack(code, back)
     return transport(me, nparts, lines, reacted, halo, courant.T, diffusion.reshape(1, width))
 
 

time: 95.3 us -> 95.1 us (level)
  no operation moved by 1% of the time
where the time goes in v9:
time: 95.1 us; the launch traced here: 94.9 us
  blocking collectives  68.3 us (72%)
  Pallas kernels  20.3 us (21%)
  starting transfers between devices  4.82 us (5%)
  waiting for transfers between devices  1.28 us (1%)
    all_to_all x1, blocking collectives, local(): lax.all_to_all(send.reshape(nparts, SEG, width), 'blk', 0, 0, tiled=True)  37 us
    all_to_all x1, blocking collectives, local(): lax.all_to_all(done.reshape(nparts, CAP, width), 'blk', 0, 0, tiled=True)  31.2 us
    pallas_call x1, Pallas kernels, pack(): pl.pallas_call(lambda *refs: pack_kernel(nparts, lines, *refs), out_shape...  6.45 us
    pallas_call x1, Pallas kernels, react(): pl.pallas_call(lambda *refs: react_kernel(nparts, nblocks, *refs), out_sh...  6.27 us
    ppermute x4, starting transfers between devices, swapped(): return lax.ppermute(block, axis, pairs + [(j, i) for i, j in pairs])  4.82 us
    pallas_call x1, Pallas kernels, unpack(): pl.pallas_call(unpack_kernel, out_shape=jax.ShapeDtypeStruct((cells, widt...  4.38 us
  transfers between devices with their start and end apart: 4, of which 1 were waited for; matrix products, arithmetic and copies ran while one was open for 0% of the time, Pallas kernels for 5%

profile of v9, /device:TPU:0, one launch (start us, length us, event | category | flops | bytes accessed | tf_op | source)
XLA Modules:
  0.0 94.9 jit_solution(15888461766878366311)
XLA Ops:
  0.0 6.4 %shard_map.91 = (bf16[8448,128]{1,0:T(8,128)(2,1)S(1)}, s32[32,128]{1,0:T(8,128)S(1)}, bf16[256,128,128]{2,1,0:T(8,128)(2,1)S(1)}) custom-call(s32[1]{0:T(128)} %bitcast.refs_0_, s32[48,128]{1,0:T(8,128)} %bitcast.18, s32[48,128]{1,0:T(8,128)} %bitcast.19, bf16[4096,128]{1,0:T(8,128)(2,1)} %bitcast.17, bf16[256,128,128]{2,1,0:T(8,128)(2,1)} %refs_4_.1), custom_call_target="tpu_custom_call" | custom-call | tf_op jit(solution)/shard_map/pallas_call | solution.py:132
  6.5 0.0 copy-start
  6.5 0.0 copy-start.1
  6.5 0.0 copy-start.2
  6.5 37.0 %all_to_all.10 = bf16[16,528,128]{2,1,0:T(8,128)(2,1)S(1)} all-to-all(bf16[16,528,128]{2,1,0:T(8,128)(2,1)S(1)} %bitcast.14), channel_id=1, replica_groups=mesh['blk'=16,'grid'=8] {'blk'}, dimensions={0} | all-to-all | bytes 4325376 | tf_op jit(solution)/shard_map/all_to_all | solution.py:431
  43.5 0.0 copy-done
  43.5 0.0 copy-done.1
  43.5 0.0 copy-done.2
  43.5 6.3 %shard_map.92 = bf16[8192,128]{1,0:T(8,128)(2,1)S(1)} custom-call(s32[1,1,768]{2,1,0:T(1,128)S(1)} %copy-done.2, bf16[8448,128]{1,0:T(8,128)(2,1)S(1)} %bitcast.12, bf16[256,128]{1,0:T(8,128)(2,1)S(1)} %copy-done, bf16[256,128]{1,0:T(8,128)(2,1)S(1)} %copy-done.1, bf16[256,128,128]{2,1,0:T(8,128)(2,1)S(1)} %get-tuple-element.14.refs_4_), custom_call_target="tpu_custom_call" | custom-call | tf_op jit(solution)/shard_map/pallas_call | solution.py:252
  49.8 0.0 copy-start.4
  49.8 31.2 %all_to_all.11 = bf16[16,512,128]{2,1,0:T(8,128)(2,1)S(1)} all-to-all(bf16[16,512,128]{2,1,0:T(8,128)(2,1)S(1)} %bitcast.13), channel_id=1, replica_groups=mesh['blk'=16,'grid'=8] {'blk'}, dimensions={0} | all-to-all | bytes 4194304 | tf_op jit(solution)/shard_map/all_to_all | solution.py:436
  81.0 1.4 %shard_map.94 = (bf16[128,128]{1,0:T(8,128)(2,1)S(1)}, bf16[128,128]{1,0:T(8,128)(2,1)S(1)}, bf16[32,128]{1,0:T(8,128)(2,1)S(1)}, bf16[32,128]{1,0:T(8,128)(2,1)S(1)}) custom-call(s32[1]{0:T(128)} %bitcast.refs_0_, s32[32,128]{1,0:T(8,128)S(1)} %get-tuple-element.12.code_ref.refs_1_, bf16[8192,128]{1,0:T(8,128)(2,1)S(1)} %bitcast.10), custom_call_target="tpu_custom_call" | custom-call | tf_op jit(solution)/shard_map/pallas_call | solution.py:301
  82.5 0.0 copy-start.3
  82.5 0.1 collective-permute-start
  82.6 3.1 %collective-permute-start.1 = (bf16[128,128]{1,0:T(8,128)(2,1)S(1)}, bf16[128,128]{1,0:T(8,128)(2,1)S(1)}, u32[]{:S(2)}, u32[]{:S(2)}) collective-permute-start(bf16[128,128]{1,0:T(8,128)(2,1)S(1)} %get-tuple-element.16), channel_id=1, source_target_pairs={{1,2},{3,4},{5,6},{7,0},{2,1},{4,3},{6,5},{0,7},{9,10},{11,12},{13... | collective-permute-start | bytes 98312 | tf_op jit(solution)/shard_map/ppermute | solution.py:419
  85.7 0.4 collective-permute-start.2
  86.1 1.2 %collective-permute-start.3 = (bf16[32,128]{1,0:T(8,128)(2,1)S(1)}, bf16[32,128]{1,0:T(8,128)(2,1)S(1)}, u32[]{:S(2)}, u32[]{:S(2)}) collective-permute-start(bf16[32,128]{1,0:T(8,128)(2,1)S(1)} %get-tuple-element.18), channel_id=1, source_target_pairs={{8,16},{24,32},{40,48},{56,64},{72,80},{88,96},{104,112},{120,0},{... | collective-permute-start | bytes 24584 | tf_op jit(solution)/shard_map/ppermute | solution.py:419
  87.3 0.0 copy-done.4
  87.3 0.1 copy.10
  87.4 4.4 %shard_map.93.refs_1_ = f32[4096,128]{1,0:T(8,128)S(1)} custom-call(s32[32,128]{1,0:T(8,128)S(1)} %get-tuple-element.12.code_ref.refs_1_, bf16[8192,128]{1,0:T(8,128)(2,1)S(1)} %bitcast.11), custom_call_target="tpu_custom_call" | custom-call | bytes 16777216 | tf_op jit(solution)/shard_map/pallas_call | solution.py:329
  91.8 0.0 collective-permute-done.2.refs_4_
  91.8 1.3 %collective-permute-done.3.refs_5_ = bf16[32,128]{1,0:T(8,128)(2,1)S(1)} collective-permute-done((bf16[32,128]{1,0:T(8,128)(2,1)S(1)}, bf16[32,128]{1,0:T(8,128)(2,1)S(1)}, u32[]{:S(2)}, u32[]{:S(2)}) %collective-permute-start.3) | collective-permute-done | bytes 8224 | tf_op jit(solution)/shard_map/ppermute | solution.py:419
  93.1 0.0 collective-permute-done.refs_2_
  93.1 0.0 collective-permute-done.1.refs_3_
  93.1 0.0 copy-done.3
  93.1 1.8 %shard_map.95 = f32[32,128,128]{2,1,0:T(8,128)} custom-call(s32[1]{0:T(128)} %bitcast.refs_0_, f32[4096,128]{1,0:T(8,128)S(1)} %shard_map.93.refs_1_, bf16[128,128]{1,0:T(8,128)(2,1)S(1)} %collective-permute-done.refs_2_, bf16[128,128]{1,0:T(8,128)(2,1)S(1)} %collective-permute-done.1.refs_3_, bf16[32,128]{1,0:T(8,128)(2,1)S(1)} %collective-permute-done.2.refs_4_, ...), custom_call_target="tpu_custom_call" | custom-call | tf_op jit(solution)/shard_map/pallas_call | solution.py:402
Async XLA Ops:
  6.5 37.1 %copy-start = (bf16[256,128]{1,0:T(8,128)(2,1)S(1)}, bf16[256,128]{1,0:T(8,128)(2,1)}, u32[]{:S(2)}) copy-start(bf16[256,128]{1,0:T(8,128)(2,1)} %refs_2_.1) | copy-start | bytes 196612
  6.5 37.0 %copy-start.1 = (bf16[256,128]{1,0:T(8,128)(2,1)S(1)}, bf16[256,128]{1,0:T(8,128)(2,1)}, u32[]{:S(2)}) copy-start(bf16[256,128]{1,0:T(8,128)(2,1)} %refs_3_.1) | copy-start | bytes 196612
  6.5 37.0 %copy-start.2 = (s32[1,1,768]{2,1,0:T(1,128)S(1)}, s32[1,1,768]{2,1,0:T(1,128)}, u32[]{:S(2)}) copy-start(s32[1,1,768]{2,1,0:T(1,128)} %refs_0_.1) | copy-start | bytes 9220
  49.8 37.5 %copy-start.4 = (f32[32,128]{1,0:T(8,128)S(1)}, f32[32,128]{1,0:T(8,128)}, u32[]{:S(2)}) copy-start(f32[32,128]{1,0:T(8,128)} %param.10) | copy-start | bytes 49156
  82.5 10.6 %copy-start.3 = (f32[128]{0:T(128)S(1)}, f32[128]{0:T(128)}, u32[]{:S(2)}) copy-start(f32[128]{0:T(128)} %param.11) | copy-start | bytes 1540
  82.5 10.6 %collective-permute-start = (bf16[128,128]{1,0:T(8,128)(2,1)S(1)}, bf16[128,128]{1,0:T(8,128)(2,1)S(1)}, u32[]{:S(2)}, u32[]{:S(2)}) collective-permute-start(bf16[128,128]{1,0:T(8,128)(2,1)S(1)} %get-tuple-element.15), channel_id=1, source_target_pairs={{0,1},{2,3},{4,5},{6,7},{1,0},{3,2},{5,4},{7,6},{8,9},{10,11},{12,... | collective-permute-start | bytes 98312 | tf_op jit(solution)/shard_map/ppermute | solution.py:419
  82.6 10.5 %collective-permute-start.1 = (bf16[128,128]{1,0:T(8,128)(2,1)S(1)}, bf16[128,128]{1,0:T(8,128)(2,1)S(1)}, u32[]{:S(2)}, u32[]{:S(2)}) collective-permute-start(bf16[128,128]{1,0:T(8,128)(2,1)S(1)} %get-tuple-element.16), channel_id=1, source_target_pairs={{1,2},{3,4},{5,6},{7,0},{2,1},{4,3},{6,5},{0,7},{9,10},{11,12},{13... | collective-permute-start | bytes 98312 | tf_op jit(solution)/shard_map/ppermute | solution.py:419
  85.7 6.1 %collective-permute-start.2 = (bf16[32,128]{1,0:T(8,128)(2,1)S(1)}, bf16[32,128]{1,0:T(8,128)(2,1)S(1)}, u32[]{:S(2)}, u32[]{:S(2)}) collective-permute-start(bf16[32,128]{1,0:T(8,128)(2,1)S(1)} %get-tuple-element.17), channel_id=1, source_target_pairs={{0,8},{16,24},{32,40},{48,56},{64,72},{80,88},{96,104},{112,120},{... | collective-permute-start | bytes 24584 | tf_op jit(solution)/shard_map/ppermute | solution.py:419
  86.1 7.0 %collective-permute-start.3 = (bf16[32,128]{1,0:T(8,128)(2,1)S(1)}, bf16[32,128]{1,0:T(8,128)(2,1)S(1)}, u32[]{:S(2)}, u32[]{:S(2)}) collective-permute-start(bf16[32,128]{1,0:T(8,128)(2,1)S(1)} %get-tuple-element.18), channel_id=1, source_target_pairs={{8,16},{24,32},{40,48},{56,64},{72,80},{88,96},{104,112},{120,0},{... | collective-permute-start | bytes 24584 | tf_op jit(solution)/shard_map/ppermute | solution.py:419
